TPU v7x, 32 devices: a whole 2x2x4 slice. The times are simulated.
32 devices in a mesh: groups: 2 (over y), blk: 16 (over z, x, core).
Axes of the slice: x: 2, y: 2, z: 4, core: 2. Of those that a mesh axis runs over, the one named last changes fastest.
Arguments:
- embeddings: bfloat16 [1536, 768], P(('groups', 'blk')), parts along dimension 0, may hold values from -6 to 6
- cluster_id: int32 [1536], P(('groups', 'blk')), parts along dimension 0, may hold values from 0 to 3, as said below
Outputs:
- neighbour: bfloat16 [1536, 768], P(('groups', 'blk')), parts along dimension 0
- dup_score: bfloat16 [1536], P(('groups', 'blk')), parts along dimension 0
There are 2 independent parts, one for each index of `groups`. A program takes and returns all parts, laid end to end along the dimension named above; each array names one. Nothing has to cross between parts.
Inputs may be any that keep to these rules, and one draw needn't show every extreme that they name: `cluster_id`: on every device of a part, each of the 4 clusters has the same number of rows among that device's 48 rows; each such number is a positive multiple of 3, and the largest is exactly 24.
All inputs are finite; a program needn't handle non-finite values.
Results may differ from a plain program's by a relative error of at most 0.0059.
Values may be sent and summed in bfloat16 or wider, within the bound.
No kernel may reach another device: no remote copies, remote signals or barrier semaphores. Data moves between devices by JAX's collectives and lax.ppermute only.
A program may use at most 64 MiB of HBM per device.

v0:
```python
import jax
import jax.numpy as jnp
from jax import lax
from jax.experimental import pallas as pl
from jax.experimental.pallas import tpu as pltpu
from jax.sharding import PartitionSpec as P

U_MAX = 8
GATHER_LIMIT = 4 * 1024 * 1024


sharpness = 10.0
epsilon = 1e-06


def normalize_rows(values):
    widened = values.astype(jnp.float32)
    return (
        widened
        * lax.rsqrt(jnp.mean(widened * widened, axis=-1, keepdims=True) + epsilon)
        * widened.shape[-1] ** (-0.5)
    ).astype(jnp.bfloat16)


def as_column(row):
    count = row.shape[1]
    across = lax.broadcasted_iota(jnp.int32, (count, count), 1)
    down = lax.broadcasted_iota(jnp.int32, (count, count), 0)
    return jnp.sum(jnp.where(across == down, row, jnp.zeros_like(row)), axis=1, keepdims=True)


def as_row(column):
    count = column.shape[0]
    across = lax.broadcasted_iota(jnp.int32, (count, count), 1)
    down = lax.broadcasted_iota(jnp.int32, (count, count), 0)
    return jnp.sum(jnp.where(across == down, column, jnp.zeros_like(column)), axis=0, keepdims=True)


def arrange_kernel(ids_hbm, rows_hbm, out_ref, moves_ref, bounds_ref, ids_ref, rows_ref, sems):
    rows_copy = pltpu.make_async_copy(rows_hbm, rows_ref, sems.at[0])
    ids_copy = pltpu.make_async_copy(ids_hbm, ids_ref, sems.at[1])
    rows_copy.start()
    ids_copy.start()
    count = rows_ref.shape[0]
    ids_copy.wait()
    ids_row = ids_ref[...].reshape(1, count)
    ids_column = as_column(ids_row)
    across = lax.broadcasted_iota(jnp.int32, (count, count), 1)
    down = lax.broadcasted_iota(jnp.int32, (count, count), 0)
    before = (ids_column < ids_row) | ((ids_column == ids_row) & (down < across))
    rank_row = jnp.sum(before.astype(jnp.int32), axis=0, keepdims=True)
    moved = down == rank_row
    moves = moved.astype(jnp.bfloat16)
    moves_ref[...] = moves
    label = jnp.sum(jnp.where(moved, ids_row, 0), axis=1, keepdims=True)
    first = jnp.sum((ids_row < label).astype(jnp.int32), axis=1, keepdims=True)
    after = jnp.sum((ids_row <= label).astype(jnp.int32), axis=1, keepdims=True)
    lane = lax.broadcasted_iota(jnp.int32, bounds_ref.shape, 1)
    bounds_ref[...] = jnp.where(lane == 0, first, after)
    rows_copy.wait()
    unit = normalize_rows(rows_ref[...])
    out_ref[...] = jnp.dot(moves, unit, preferred_element_type=jnp.float32).astype(jnp.bfloat16)


def partial_sums(queries, key_blocks, bounds, own, block_rows):
    totals, weighted = 0.0, 0.0
    first, after = bounds[:, 0:1], bounds[:, 1:2]
    for index, keys in enumerate(key_blocks):
        similar = lax.dot_general(
            queries, keys, (((1,), (1,)), ((), ())), preferred_element_type=jnp.float32
        )
        place = lax.rem(lax.broadcasted_iota(jnp.int32, similar.shape, 1), block_rows)
        allowed = (place >= first) & (place < after)
        if own and index == 0:
            allowed = allowed & (place != lax.broadcasted_iota(jnp.int32, similar.shape, 0))
        weights = jnp.where(allowed, jnp.exp(sharpness * (similar - 1.0)), 0.0)
        totals = totals + jnp.sum(weights, axis=1, keepdims=True)
        weighted = weighted + jnp.dot(
            weights.astype(jnp.bfloat16), keys, preferred_element_type=jnp.float32
        )
    return totals, weighted


LANES = 128


def gather_refs(refs):
    return [ref[...] for ref in refs]


def first_kernel(bounds_ref, own_ref, beside_ref, *refs):
    *key_refs, weighted_ref, totals_ref = refs
    queries = jnp.concatenate([own_ref[...], beside_ref[...]], axis=0)
    bounds = jnp.concatenate([bounds_ref[...]] * 2, axis=0)
    totals, weighted = partial_sums(queries, gather_refs(key_refs), bounds, True, own_ref.shape[0])
    weighted_ref[...] = weighted
    totals_ref[...] = jnp.broadcast_to(totals, totals_ref.shape)


def beside_kernel(so_far_ref, totals_so_far_ref, bounds_ref, beside_ref, *refs):
    *key_refs, out_ref = refs
    count = beside_ref.shape[0]
    keys = gather_refs(key_refs)
    totals, weighted = partial_sums(beside_ref[...], keys, bounds_ref[...], False, count)
    totals = totals + totals_so_far_ref[count:, 0:1]
    weighted = (weighted + so_far_ref[count:, :]).astype(jnp.bfloat16)
    columns = weighted.shape[1] // LANES
    for index in range(columns):
        out_ref[index * count : (index + 1) * count, :] = weighted[
            :, index * LANES : (index + 1) * LANES
        ]
    extra = out_ref.shape[0] - columns * count
    totals = jnp.concatenate([as_row(totals), jnp.zeros((1, LANES - count), jnp.float32)], axis=1)
    high = totals.astype(jnp.bfloat16).astype(jnp.float32)
    row = lax.broadcasted_iota(jnp.int32, (extra, LANES), 0)
    out_ref[columns * count :, :] = jnp.where(row == 0, high, totals - high).astype(jnp.bfloat16)


def own_kernel(so_far_ref, totals_so_far_ref, bounds_ref, own_ref, *refs):
    *key_refs, weighted_ref, totals_ref = refs
    count = own_ref.shape[0]
    keys = gather_refs(key_refs)
    totals, weighted = partial_sums(own_ref[...], keys, bounds_ref[...], False, count)
    weighted_ref[...] = weighted + so_far_ref[:count, :]
    totals_ref[...] = as_row(totals + totals_so_far_ref[:count, 0:1])


def finish_kernel(moves_ref, weighted_ref, totals_ref, back_ref, neighbour_hbm, score_hbm, neighbour_ref, score_ref, sems):
    count, features = neighbour_ref.shape
    columns = features // LANES
    back = [
        back_ref[index * count : (index + 1) * count, :].astype(jnp.float32)
        for index in range(columns)
    ]
    weighted = weighted_ref[...] + jnp.concatenate(back, axis=1)
    normed = (
        weighted * lax.rsqrt(jnp.mean(weighted * weighted, axis=-1, keepdims=True) + epsilon)
    ).astype(jnp.bfloat16)
    moves = moves_ref[...]
    neighbour_ref[...] = lax.dot_general(
        moves, normed, (((0,), (0,)), ((), ())), preferred_element_type=jnp.float32
    ).astype(jnp.bfloat16)
    neighbour_copy = pltpu.make_async_copy(neighbour_ref, neighbour_hbm, sems.at[0])
    neighbour_copy.start()
    pair = back_ref[columns * count :, :].astype(jnp.float32)
    totals = totals_ref[...] + (pair[0:1, :count] + pair[1:2, :count])
    scores = jnp.sum(moves.astype(jnp.float32) * as_column(jnp.log(totals)), axis=0, keepdims=True)
    score_ref[...] = scores.astype(jnp.bfloat16).reshape(count)
    score_copy = pltpu.make_async_copy(score_ref, score_hbm, sems.at[1])
    score_copy.start()
    neighbour_copy.wait()
    score_copy.wait()


EXTRA = 16
CORE, ACROSS, NEAR, FAR = 1, 2, 4, 8
GRID = 16


def gathered_body(embeddings, cluster_id):
    rows_dev, features = embeddings.shape
    vmem = pl.BlockSpec(memory_space=pltpu.VMEM)
    stored = pl.BlockSpec(memory_space=pltpu.HBM)

    def swap(value, bits):
        return lax.ppermute(value, "blk", [(device, device ^ bits) for device in range(GRID)])

    def block(kind, *shape):
        return jax.ShapeDtypeStruct(shape, kind)

    def kernel(body, name, out_shape, *inputs, specs=vmem, out_specs=vmem, scratch=()):
        return pl.pallas_call(
            body,
            out_shape=out_shape,
            in_specs=[specs] * len(inputs),
            out_specs=(out_specs,) * len(out_shape),
            scratch_shapes=scratch,
            compiler_params=pltpu.CompilerParams(vmem_limit_bytes=32 * 1024 * 1024),
            name=name,
        )(*inputs)

    rows = block(jnp.bfloat16, rows_dev, features)
    own, moves, bounds = kernel(
        arrange_kernel,
        "arrange",
        (rows, block(jnp.bfloat16, rows_dev, rows_dev), block(jnp.int32, rows_dev, LANES)),
        pltpu.with_memory_space_constraint(cluster_id, pltpu.HBM),
        pltpu.with_memory_space_constraint(embeddings, pltpu.HBM),
        specs=stored,
        scratch=(
            pltpu.VMEM((rows_dev,), jnp.int32),
            pltpu.VMEM((rows_dev, features), jnp.bfloat16),
            pltpu.SemaphoreType.DMA((2,)),
        ),
    )

    farther, far, near, beside, mate = lax.optimization_barrier(
        tuple(swap(own, bits) for bits in (FAR | NEAR, FAR, NEAR, ACROSS, CORE))
    )
    mates = swap(jnp.concatenate([near, far, farther], axis=0), CORE)
    weighted, totals = kernel(
        first_kernel,
        "first",
        (block(jnp.float32, 2 * rows_dev, features), block(jnp.float32, 2 * rows_dev, LANES)),
        *(bounds, own, beside),
        *(own, mate, near, far, farther),
    )
    (partial,) = kernel(
        beside_kernel,
        "beside",
        (block(jnp.bfloat16, rows_dev * features // LANES + EXTRA, LANES),),
        *(weighted, totals, bounds, beside, mates),
    )
    back = swap(partial, ACROSS)
    weighted, totals = kernel(
        own_kernel,
        "own",
        (block(jnp.float32, rows_dev, features), block(jnp.float32, 1, rows_dev)),
        *(weighted, totals, bounds, own, mates),
    )
    return tuple(
        kernel(
            finish_kernel,
            "finish",
            (rows, block(jnp.bfloat16, rows_dev)),
            *(moves, weighted, totals, back),
            out_specs=stored,
            scratch=(
                pltpu.VMEM((rows_dev, features), jnp.bfloat16),
                pltpu.VMEM((rows_dev,), jnp.bfloat16),
                pltpu.SemaphoreType.DMA((2,)),
            ),
        )
    )


def from_behind(value, axis, steps):
    count = lax.axis_size(axis)
    initial, last = (max(0, -steps), min(count, count - steps))
    return lax.ppermute(value, axis, [(source, source + steps) for source in range(initial, last)])


def pair_terms(queries, visiting, allowed):
    similar = jnp.dot(queries, visiting.T, preferred_element_type=jnp.float32)
    return jnp.where(allowed, jnp.exp(sharpness * (similar - 1.0)), jnp.zeros_like(similar))


def finish(weighted, totals):
    normed = (
        weighted * lax.rsqrt(jnp.mean(weighted * weighted, axis=-1, keepdims=True) + epsilon)
    ).astype(jnp.bfloat16)
    return (normed, jnp.log(totals).astype(jnp.bfloat16))


def collected_body(embeddings, cluster_id):
    rows_dev, features = embeddings.shape
    devices = lax.axis_size("blk")
    per_peer = rows_dev // devices
    clusters = devices // 4
    unit_rows = normalize_rows(embeddings)
    labels = jnp.arange(clusters, dtype=jnp.int32)
    counts = jnp.sum((cluster_id[:, None] == labels[None, :]).astype(jnp.int32), axis=0)
    group_ends = jnp.cumsum(counts // per_peer)

    def owner_cluster(device):
        in_range = (device >= 0) & (device < devices)
        return jnp.where(in_range, jnp.sum((device >= group_ends).astype(jnp.int32)), -1)

    position = jnp.arange(rows_dev, dtype=jnp.int32)
    arrange_order = jnp.argsort(cluster_id * rows_dev + position)
    inverse = jnp.argsort(arrange_order)
    arranged = unit_rows[arrange_order].reshape(devices, per_peer, features)
    held_rows = lax.all_to_all(arranged, "blk", split_axis=0, concat_axis=0, tiled=True).reshape(
        rows_dev, features
    )
    self_index = lax.axis_index("blk")
    mine = owner_cluster(self_index)
    weights = pair_terms(held_rows, held_rows, position[:, None] != position[None, :])
    totals = jnp.sum(weights, axis=1)
    weighted = jnp.dot(weights.astype(jnp.bfloat16), held_rows, preferred_element_type=jnp.float32)
    from_lower = held_rows
    from_upper = held_rows
    for distance in range(1, U_MAX):
        from_lower = from_behind(from_lower, "blk", 1)
        from_upper = from_behind(from_upper, "blk", -1)
        for visiting, source in (
            (from_lower, self_index - distance),
            (from_upper, self_index + distance),
        ):
            weights = pair_terms(held_rows, visiting, owner_cluster(source) == mine)
            totals = totals + jnp.sum(weights, axis=1)
            weighted = weighted + jnp.dot(
                weights.astype(jnp.bfloat16), visiting, preferred_element_type=jnp.float32
            )
    normed, scores = finish(weighted, totals)
    returned_rows, returned_scores = (
        lax.all_to_all(
            normed.reshape(devices, per_peer, features),
            "blk",
            split_axis=0,
            concat_axis=0,
            tiled=True,
        ),
        lax.all_to_all(
            scores.reshape(devices, per_peer), "blk", split_axis=0, concat_axis=0, tiled=True
        ),
    )
    neighbour = returned_rows.reshape(rows_dev, features)[inverse]
    dup_score = returned_scores.reshape(rows_dev)[inverse]
    return (neighbour, dup_score)


def solution(mesh):
    placed = (P(("groups", "blk"), None), P(("groups", "blk")))
    devices = mesh.shape["blk"]

    def body(embeddings, cluster_id):
        gathered = embeddings.size * embeddings.dtype.itemsize * devices
        fits = gathered <= GATHER_LIMIT and devices == GRID
        plan = gathered_body if fits else collected_body
        return plan(embeddings, cluster_id)

    return jax.shard_map(
        body,
        mesh=mesh,
        in_specs=placed,
        out_specs=(P(("groups", "blk"), None), P(("groups", "blk"))),
        check_vma=False,
    )
```

profile of v0, /device:TPU:0, one launch (start us, length us, event | category | flops | bytes accessed | tf_op | source)
XLA Modules:
  0.0 20.6 jit_solution(14523090923135909358)
XLA Ops:
  0.6 1.3 %arrange.1 = (bf16[48,768]{1,0:T(8,128)(2,1)S(1)}, bf16[48,48]{1,0:T(8,128)(2,1)S(1)}, s32[48,128]{1,0:T(8,128)S(1)}) custom-call(s32[48]{0:T(128)} %ids_hbm.1, bf16[48,768]{1,0:T(8,128)(2,1)} %rows_hbm.1), custom_call_target="tpu_custom_call" | custom-call | tf_op jit(solution)/shard_map/arrange/pallas_call | solution.py:172
  1.9 5.1 %collective-permute-start = (bf16[48,768]{1,0:T(8,128)(2,1)S(1)}, bf16[48,768]{1,0:T(8,128)(2,1)S(1)}, u32[]{:S(2)}, u32[]{:S(2)}) collective-permute-start(bf16[48,768]{1,0:T(8,128)(2,1)S(1)} %get-tuple-element.16.own_ref.refs_0_), channel_id=1, source_target_pairs={{0,12},{1,13},{2,14},{3,15},{4,8},{5,9},{6,10},{7,11},{8,4},{9,5},... | collective-permute-start | bytes 221192 | tf_op jit(solution)/shard_map/ppermute | solution.py:166
  7.0 0.0 collective-permute-start.1
  7.0 0.6 %collective-permute-start.2 = (bf16[48,768]{1,0:T(8,128)(2,1)S(1)}, bf16[48,768]{1,0:T(8,128)(2,1)S(1)}, u32[]{:S(2)}, u32[]{:S(2)}) collective-permute-start(bf16[48,768]{1,0:T(8,128)(2,1)S(1)} %get-tuple-element.16.own_ref.refs_0_), channel_id=1, source_target_pairs={{0,4},{1,5},{2,6},{3,7},{4,0},{5,1},{6,2},{7,3},{8,12},{9,13},{10,... | collective-permute-start | bytes 221192 | tf_op jit(solution)/shard_map/ppermute | solution.py:166
  7.7 1.6 %collective-permute-start.3 = (bf16[48,768]{1,0:T(8,128)(2,1)S(1)}, bf16[48,768]{1,0:T(8,128)(2,1)S(1)}, u32[]{:S(2)}, u32[]{:S(2)}) collective-permute-start(bf16[48,768]{1,0:T(8,128)(2,1)S(1)} %get-tuple-element.16.own_ref.refs_0_), channel_id=1, source_target_pairs={{0,2},{1,3},{2,0},{3,1},{4,6},{5,7},{6,4},{7,5},{8,10},{9,11},{10,... | collective-permute-start | bytes 221192 | tf_op jit(solution)/shard_map/ppermute | solution.py:166
  9.3 0.0 collective-permute-start.4
  9.3 0.5 %collective-permute-done.refs_4_ = bf16[48,768]{1,0:T(8,128)(2,1)S(1)} collective-permute-done((bf16[48,768]{1,0:T(8,128)(2,1)S(1)}, bf16[48,768]{1,0:T(8,128)(2,1)S(1)}, u32[]{:S(2)}, u32[]{:S(2)}) %collective-permute-start) | collective-permute-done | bytes 73760 | tf_op jit(solution)/shard_map/ppermute | solution.py:166
  9.8 3.5 %collective-permute-done.1.refs_3_ = bf16[48,768]{1,0:T(8,128)(2,1)S(1)} collective-permute-done((bf16[48,768]{1,0:T(8,128)(2,1)S(1)}, bf16[48,768]{1,0:T(8,128)(2,1)S(1)}, u32[]{:S(2)}, u32[]{:S(2)}) %collective-permute-start.1) | collective-permute-done | bytes 73760 | tf_op jit(solution)/shard_map/ppermute | solution.py:166
  13.2 0.0 collective-permute-done.2.refs_2_
  13.2 0.0 collective-permute-done.3.beside_ref
  13.2 0.0 collective-permute-done.4.refs_1_
  13.3 0.1 collective-permute-start.5
  13.3 1.0 %first.1 = (f32[96,768]{1,0:T(8,128)S(1)}, f32[96,128]{1,0:T(8,128)S(1)}) custom-call(s32[48,128]{1,0:T(8,128)S(1)} %get-tuple-element.15.bounds_ref, bf16[48,768]{1,0:T(8,128)(2,1)S(1)} %get-tuple-element.16.own_ref.refs_0_, bf16[48,768]{1,0:T(8,128)(2,1)S(1)} %collective-permute-done.3.beside_ref, bf16[48,768]{1,0:T(8,128)(2,1)S(1)} %get-tuple-element.16.own_ref.refs_0_, ...), custom_call_target="tpu_custom_call" | custom-call | tf_op jit(solution)/shard_map/first/pallas_call | solution.py:172
  14.4 0.4 %collective-permute-done.5.refs_0_ = bf16[144,768]{1,0:T(8,128)(2,1)S(1)} collective-permute-done((bf16[144,768]{1,0:T(8,128)(2,1)S(1)}, bf16[144,768]{1,0:T(8,128)(2,1)S(1)}, u32[]{:S(2)}, u32[]{:S(2)}) %collective-permute-start.5) | collective-permute-done | bytes 221216 | tf_op jit(solution)/shard_map/ppermute | solution.py:166
  14.8 0.4 %beside.1 = bf16[304,128]{1,0:T(8,128)(2,1)S(1)} custom-call(f32[96,768]{1,0:T(8,128)S(1)} %get-tuple-element.22.so_far_ref, f32[96,128]{1,0:T(8,128)S(1)} %get-tuple-element.23.totals_so_far_ref, s32[48,128]{1,0:T(8,128)S(1)} %get-tuple-element.15.bounds_ref, bf16[48,768]{1,0:T(8,128)(2,1)S(1)} %collective-permute-done.3.beside_ref, ...), custom_call_target="tpu_custom_call" | custom-call | tf_op jit(solution)/shard_map/beside/pallas_call | solution.py:172
  15.2 1.6 %collective-permute-start.6 = (bf16[304,128]{1,0:T(8,128)(2,1)S(1)}, bf16[304,128]{1,0:T(8,128)(2,1)S(1)}, u32[]{:S(2)}, u32[]{:S(2)}) collective-permute-start(bf16[304,128]{1,0:T(8,128)(2,1)S(1)} %beside.1), channel_id=1, source_target_pairs={{0,2},{1,3},{2,0},{3,1},{4,6},{5,7},{6,4},{7,5},{8,10},{9,11},{10,... | collective-permute-start | bytes 233480 | tf_op jit(solution)/shard_map/ppermute | solution.py:166
  16.8 0.4 %own.1 = (f32[48,768]{1,0:T(8,128)S(1)}, f32[1,48]{1,0:T(1,128)S(1)}) custom-call(f32[96,768]{1,0:T(8,128)S(1)} %get-tuple-element.22.so_far_ref, f32[96,128]{1,0:T(8,128)S(1)} %get-tuple-element.23.totals_so_far_ref, s32[48,128]{1,0:T(8,128)S(1)} %get-tuple-element.15.bounds_ref, bf16[48,768]{1,0:T(8,128)(2,1)S(1)} %get-tuple-element.16.own_ref.refs_0_, ...), custom_call_target="tpu_custom_call" | custom-call | tf_op jit(solution)/shard_map/own/pallas_call | solution.py:172
  17.2 2.5 %collective-permute-done.6.back_ref = bf16[304,128]{1,0:T(8,128)(2,1)S(1)} collective-permute-done((bf16[304,128]{1,0:T(8,128)(2,1)S(1)}, bf16[304,128]{1,0:T(8,128)(2,1)S(1)}, u32[]{:S(2)}, u32[]{:S(2)}) %collective-permute-start.6) | collective-permute-done | bytes 77856 | tf_op jit(solution)/shard_map/ppermute | solution.py:166
  19.7 0.9 %finish.1 = (bf16[48,768]{1,0:T(8,128)(2,1)}, bf16[48]{0:T(256)(128)(2,1)}) custom-call(bf16[48,48]{1,0:T(8,128)(2,1)S(1)} %get-tuple-element.14.moves_ref, f32[48,768]{1,0:T(8,128)S(1)} %get-tuple-element.24.weighted_ref, f32[1,48]{1,0:T(1,128)S(1)} %get-tuple-element.25.totals_ref, bf16[304,128]{1,0:T(8,128)(2,1)S(1)} %collective-permute-done.6.back_ref), custom_call_target="tpu_custom_call" | custom-call | tf_op jit(solution)/shard_map/finish/pallas_call | solution.py:172
  (1 shorter events, 0.0 us)
Async XLA Ops:
  1.9 7.9 %collective-permute-start = (bf16[48,768]{1,0:T(8,128)(2,1)S(1)}, bf16[48,768]{1,0:T(8,128)(2,1)S(1)}, u32[]{:S(2)}, u32[]{:S(2)}) collective-permute-start(bf16[48,768]{1,0:T(8,128)(2,1)S(1)} %get-tuple-element.16.own_ref.refs_0_), channel_id=1, source_target_pairs={{0,12},{1,13},{2,14},{3,15},{4,8},{5,9},{6,10},{7,11},{8,4},{9,5},... | collective-permute-start | bytes 221192 | tf_op jit(solution)/shard_map/ppermute | solution.py:166
  7.0 6.2 %collective-permute-start.1 = (bf16[48,768]{1,0:T(8,128)(2,1)S(1)}, bf16[48,768]{1,0:T(8,128)(2,1)S(1)}, u32[]{:S(2)}, u32[]{:S(2)}) collective-permute-start(bf16[48,768]{1,0:T(8,128)(2,1)S(1)} %get-tuple-element.16.own_ref.refs_0_), channel_id=1, source_target_pairs={{0,8},{1,9},{2,10},{3,11},{4,12},{5,13},{6,14},{7,15},{8,0},{9,1},... | collective-permute-start | bytes 221192 | tf_op jit(solution)/shard_map/ppermute | solution.py:166
  7.0 6.2 %collective-permute-start.2 = (bf16[48,768]{1,0:T(8,128)(2,1)S(1)}, bf16[48,768]{1,0:T(8,128)(2,1)S(1)}, u32[]{:S(2)}, u32[]{:S(2)}) collective-permute-start(bf16[48,768]{1,0:T(8,128)(2,1)S(1)} %get-tuple-element.16.own_ref.refs_0_), channel_id=1, source_target_pairs={{0,4},{1,5},{2,6},{3,7},{4,0},{5,1},{6,2},{7,3},{8,12},{9,13},{10,... | collective-permute-start | bytes 221192 | tf_op jit(solution)/shard_map/ppermute | solution.py:166
  7.7 5.6 %collective-permute-start.3 = (bf16[48,768]{1,0:T(8,128)(2,1)S(1)}, bf16[48,768]{1,0:T(8,128)(2,1)S(1)}, u32[]{:S(2)}, u32[]{:S(2)}) collective-permute-start(bf16[48,768]{1,0:T(8,128)(2,1)S(1)} %get-tuple-element.16.own_ref.refs_0_), channel_id=1, source_target_pairs={{0,2},{1,3},{2,0},{3,1},{4,6},{5,7},{6,4},{7,5},{8,10},{9,11},{10,... | collective-permute-start | bytes 221192 | tf_op jit(solution)/shard_map/ppermute | solution.py:166
  9.3 3.9 %collective-permute-start.4 = (bf16[48,768]{1,0:T(8,128)(2,1)S(1)}, bf16[48,768]{1,0:T(8,128)(2,1)S(1)}, u32[]{:S(2)}, u32[]{:S(2)}) collective-permute-start(bf16[48,768]{1,0:T(8,128)(2,1)S(1)} %get-tuple-element.16.own_ref.refs_0_), channel_id=1, source_target_pairs={{0,1},{1,0},{2,3},{3,2},{4,5},{5,4},{6,7},{7,6},{8,9},{9,8},{10,11... | collective-permute-start | bytes 221192 | tf_op jit(solution)/shard_map/ppermute | solution.py:166
  13.3 1.5 %collective-permute-start.5 = (bf16[144,768]{1,0:T(8,128)(2,1)S(1)}, bf16[144,768]{1,0:T(8,128)(2,1)S(1)}, u32[]{:S(2)}, u32[]{:S(2)}) collective-permute-start(bf16[144,768]{1,0:T(8,128)(2,1)S(1)} %pad_maximum_fusion), channel_id=1, source_target_pairs={{0,1},{1,0},{2,3},{3,2},{4,5},{5,4},{6,7},{7,6},{8,9},{9,8},{10,11... | collective-permute-start | bytes 663560 | tf_op jit(solution)/shard_map/ppermute | solution.py:166
  15.2 4.5 %collective-permute-start.6 = (bf16[304,128]{1,0:T(8,128)(2,1)S(1)}, bf16[304,128]{1,0:T(8,128)(2,1)S(1)}, u32[]{:S(2)}, u32[]{:S(2)}) collective-permute-start(bf16[304,128]{1,0:T(8,128)(2,1)S(1)} %beside.1), channel_id=1, source_target_pairs={{0,2},{1,3},{2,0},{3,1},{4,6},{5,7},{6,4},{7,5},{8,10},{9,11},{10,... | collective-permute-start | bytes 233480 | tf_op jit(solution)/shard_map/ppermute | solution.py:166
where the time goes:
time: 20.7 us; the launch traced here: 20.6 us
  starting transfers between devices  9.02 us (44%)
  waiting for transfers between devices  6.87 us (33%)
  Pallas kernels  3.99 us (19%)
  between operations  0.67 us (3%)
    ppermute x7, starting transfers between devices, swap(): lax.ppermute(value, 'blk', [(device, device ^ bits) for device in range(G...  9.02 us
    ppermute x7, waiting for transfers between devices, swap(): lax.ppermute(value, 'blk', [(device, device ^ bits) for device in range(G...  6.87 us
    pallas_call x5, Pallas kernels, kernel(): pl.pallas_call(body, out_shape=out_shape, in_specs=[specs] * len(inputs),...  3.99 us
  transfers between devices with their start and end apart: 7, of which 4 were waited for; matrix products, arithmetic and copies ran while one was open for 0% of the time, Pallas kernels for 7%

commit v1 on v0

--- a/solution.py
+++ b/solution.py
@@ -194,8 +194,8 @@
         ),
     )
 
-    farther, far, near, beside, mate = lax.optimization_barrier(
-        tuple(swap(own, bits) for bits in (FAR | NEAR, FAR, NEAR, ACROSS, CORE))
+    far, farther, near, beside, mate = lax.optimization_barrier(
+        tuple(swap(own, bits) for bits in (FAR, FAR | NEAR, NEAR, ACROSS, CORE))
     )
     mates = swap(jnp.concatenate([near, far, farther], axis=0), CORE)
     weighted, totals = kernel(

time: 20.7 us -> 20.1 us (0.971)
  waiting for transfers between devices: 6.87 us -> 6.29 us
    ppermute x7, waiting for transfers between devices: 6.87 us -> 6.29 us  [swap(): lax.ppermute(value, 'blk', [(device, device ^ bits) for device in range(G...]
  transfers between devices with their start and end apart: 7 -> 7, of which waited for: 4 -> 5; matrix products, arithmetic and copies ran while one was open for 0% -> 0% of each run, Pallas kernels for 7% -> 7%
where the time goes in v1:
time: 20.1 us; the launch traced here: 20 us
  starting transfers between devices  9 us (45%)
  waiting for transfers between devices  6.29 us (31%)
  Pallas kernels  3.99 us (20%)
  between operations  0.67 us (3%)
    ppermute x7, starting transfers between devices, swap(): lax.ppermute(value, 'blk', [(device, device ^ bits) for device in range(G...  9 us
    ppermute x7, waiting for transfers between devices, swap(): lax.ppermute(value, 'blk', [(device, device ^ bits) for device in range(G...  6.29 us
    pallas_call x5, Pallas kernels, kernel(): pl.pallas_call(body, out_shape=out_shape, in_specs=[specs] * len(inputs),...  3.99 us
  transfers between devices with their start and end apart: 7, of which 5 were waited for; matrix products, arithmetic and copies ran while one was open for 0% of the time, Pallas kernels for 7%

profile of v1, /device:TPU:0, one launch (start us, length us, event | category | flops | bytes accessed | tf_op | source)
XLA Modules:
  0.0 20.0 jit_solution(11783455991310980062)
XLA Ops:
  0.6 1.3 %arrange.1 = (bf16[48,768]{1,0:T(8,128)(2,1)S(1)}, bf16[48,48]{1,0:T(8,128)(2,1)S(1)}, s32[48,128]{1,0:T(8,128)S(1)}) custom-call(s32[48]{0:T(128)} %ids_hbm.1, bf16[48,768]{1,0:T(8,128)(2,1)} %rows_hbm.1), custom_call_target="tpu_custom_call" | custom-call | tf_op jit(solution)/shard_map/arrange/pallas_call | solution.py:172
  1.9 4.1 %collective-permute-start = (bf16[48,768]{1,0:T(8,128)(2,1)S(1)}, bf16[48,768]{1,0:T(8,128)(2,1)S(1)}, u32[]{:S(2)}, u32[]{:S(2)}) collective-permute-start(bf16[48,768]{1,0:T(8,128)(2,1)S(1)} %get-tuple-element.16.own_ref.refs_0_), channel_id=1, source_target_pairs={{0,8},{1,9},{2,10},{3,11},{4,12},{5,13},{6,14},{7,15},{8,0},{9,1},... | collective-permute-start | bytes 221192 | tf_op jit(solution)/shard_map/ppermute | solution.py:166
  6.0 1.3 %collective-permute-start.1 = (bf16[48,768]{1,0:T(8,128)(2,1)S(1)}, bf16[48,768]{1,0:T(8,128)(2,1)S(1)}, u32[]{:S(2)}, u32[]{:S(2)}) collective-permute-start(bf16[48,768]{1,0:T(8,128)(2,1)S(1)} %get-tuple-element.16.own_ref.refs_0_), channel_id=1, source_target_pairs={{0,12},{1,13},{2,14},{3,15},{4,8},{5,9},{6,10},{7,11},{8,4},{9,5},... | collective-permute-start | bytes 221192 | tf_op jit(solution)/shard_map/ppermute | solution.py:166
  7.3 0.2 %collective-permute-start.2 = (bf16[48,768]{1,0:T(8,128)(2,1)S(1)}, bf16[48,768]{1,0:T(8,128)(2,1)S(1)}, u32[]{:S(2)}, u32[]{:S(2)}) collective-permute-start(bf16[48,768]{1,0:T(8,128)(2,1)S(1)} %get-tuple-element.16.own_ref.refs_0_), channel_id=1, source_target_pairs={{0,4},{1,5},{2,6},{3,7},{4,0},{5,1},{6,2},{7,3},{8,12},{9,13},{10,... | collective-permute-start | bytes 221192 | tf_op jit(solution)/shard_map/ppermute | solution.py:166
  7.6 1.5 %collective-permute-start.3 = (bf16[48,768]{1,0:T(8,128)(2,1)S(1)}, bf16[48,768]{1,0:T(8,128)(2,1)S(1)}, u32[]{:S(2)}, u32[]{:S(2)}) collective-permute-start(bf16[48,768]{1,0:T(8,128)(2,1)S(1)} %get-tuple-element.16.own_ref.refs_0_), channel_id=1, source_target_pairs={{0,2},{1,3},{2,0},{3,1},{4,6},{5,7},{6,4},{7,5},{8,10},{9,11},{10,... | collective-permute-start | bytes 221192 | tf_op jit(solution)/shard_map/ppermute | solution.py:166
  9.1 0.0 collective-permute-start.4
  9.1 1.8 %collective-permute-done.refs_3_ = bf16[48,768]{1,0:T(8,128)(2,1)S(1)} collective-permute-done((bf16[48,768]{1,0:T(8,128)(2,1)S(1)}, bf16[48,768]{1,0:T(8,128)(2,1)S(1)}, u32[]{:S(2)}, u32[]{:S(2)}) %collective-permute-start) | collective-permute-done | bytes 73760 | tf_op jit(solution)/shard_map/ppermute | solution.py:166
  10.9 1.6 %collective-permute-done.1.refs_4_ = bf16[48,768]{1,0:T(8,128)(2,1)S(1)} collective-permute-done((bf16[48,768]{1,0:T(8,128)(2,1)S(1)}, bf16[48,768]{1,0:T(8,128)(2,1)S(1)}, u32[]{:S(2)}, u32[]{:S(2)}) %collective-permute-start.1) | collective-permute-done | bytes 73760 | tf_op jit(solution)/shard_map/ppermute | solution.py:166
  12.5 0.2 collective-permute-done.2.refs_2_
  12.6 0.0 collective-permute-done.3.beside_ref
  12.6 0.0 collective-permute-done.4.refs_1_
  12.7 0.1 collective-permute-start.5
  12.7 1.0 %first.1 = (f32[96,768]{1,0:T(8,128)S(1)}, f32[96,128]{1,0:T(8,128)S(1)}) custom-call(s32[48,128]{1,0:T(8,128)S(1)} %get-tuple-element.15.bounds_ref, bf16[48,768]{1,0:T(8,128)(2,1)S(1)} %get-tuple-element.16.own_ref.refs_0_, bf16[48,768]{1,0:T(8,128)(2,1)S(1)} %collective-permute-done.3.beside_ref, bf16[48,768]{1,0:T(8,128)(2,1)S(1)} %get-tuple-element.16.own_ref.refs_0_, ...), custom_call_target="tpu_custom_call" | custom-call | tf_op jit(solution)/shard_map/first/pallas_call | solution.py:172
  13.8 0.4 %collective-permute-done.5.refs_0_ = bf16[144,768]{1,0:T(8,128)(2,1)S(1)} collective-permute-done((bf16[144,768]{1,0:T(8,128)(2,1)S(1)}, bf16[144,768]{1,0:T(8,128)(2,1)S(1)}, u32[]{:S(2)}, u32[]{:S(2)}) %collective-permute-start.5) | collective-permute-done | bytes 221216 | tf_op jit(solution)/shard_map/ppermute | solution.py:166
  14.2 0.4 %beside.1 = bf16[304,128]{1,0:T(8,128)(2,1)S(1)} custom-call(f32[96,768]{1,0:T(8,128)S(1)} %get-tuple-element.22.so_far_ref, f32[96,128]{1,0:T(8,128)S(1)} %get-tuple-element.23.totals_so_far_ref, s32[48,128]{1,0:T(8,128)S(1)} %get-tuple-element.15.bounds_ref, bf16[48,768]{1,0:T(8,128)(2,1)S(1)} %collective-permute-done.3.beside_ref, ...), custom_call_target="tpu_custom_call" | custom-call | tf_op jit(solution)/shard_map/beside/pallas_call | solution.py:172
  14.6 1.8 %collective-permute-start.6 = (bf16[304,128]{1,0:T(8,128)(2,1)S(1)}, bf16[304,128]{1,0:T(8,128)(2,1)S(1)}, u32[]{:S(2)}, u32[]{:S(2)}) collective-permute-start(bf16[304,128]{1,0:T(8,128)(2,1)S(1)} %beside.1), channel_id=1, source_target_pairs={{0,2},{1,3},{2,0},{3,1},{4,6},{5,7},{6,4},{7,5},{8,10},{9,11},{10,... | collective-permute-start | bytes 233480 | tf_op jit(solution)/shard_map/ppermute | solution.py:166
  16.4 0.4 %own.1 = (f32[48,768]{1,0:T(8,128)S(1)}, f32[1,48]{1,0:T(1,128)S(1)}) custom-call(f32[96,768]{1,0:T(8,128)S(1)} %get-tuple-element.22.so_far_ref, f32[96,128]{1,0:T(8,128)S(1)} %get-tuple-element.23.totals_so_far_ref, s32[48,128]{1,0:T(8,128)S(1)} %get-tuple-element.15.bounds_ref, bf16[48,768]{1,0:T(8,128)(2,1)S(1)} %get-tuple-element.16.own_ref.refs_0_, ...), custom_call_target="tpu_custom_call" | custom-call | tf_op jit(solution)/shard_map/own/pallas_call | solution.py:172
  16.8 2.3 %collective-permute-done.6.back_ref = bf16[304,128]{1,0:T(8,128)(2,1)S(1)} collective-permute-done((bf16[304,128]{1,0:T(8,128)(2,1)S(1)}, bf16[304,128]{1,0:T(8,128)(2,1)S(1)}, u32[]{:S(2)}, u32[]{:S(2)}) %collective-permute-start.6) | collective-permute-done | bytes 77856 | tf_op jit(solution)/shard_map/ppermute | solution.py:166
  19.1 0.9 %finish.1 = (bf16[48,768]{1,0:T(8,128)(2,1)}, bf16[48]{0:T(256)(128)(2,1)}) custom-call(bf16[48,48]{1,0:T(8,128)(2,1)S(1)} %get-tuple-element.14.moves_ref, f32[48,768]{1,0:T(8,128)S(1)} %get-tuple-element.24.weighted_ref, f32[1,48]{1,0:T(1,128)S(1)} %get-tuple-element.25.totals_ref, bf16[304,128]{1,0:T(8,128)(2,1)S(1)} %collective-permute-done.6.back_ref), custom_call_target="tpu_custom_call" | custom-call | tf_op jit(solution)/shard_map/finish/pallas_call | solution.py:172
  (1 shorter events, 0.0 us)
Async XLA Ops:
  1.9 9.0 %collective-permute-start = (bf16[48,768]{1,0:T(8,128)(2,1)S(1)}, bf16[48,768]{1,0:T(8,128)(2,1)S(1)}, u32[]{:S(2)}, u32[]{:S(2)}) collective-permute-start(bf16[48,768]{1,0:T(8,128)(2,1)S(1)} %get-tuple-element.16.own_ref.refs_0_), channel_id=1, source_target_pairs={{0,8},{1,9},{2,10},{3,11},{4,12},{5,13},{6,14},{7,15},{8,0},{9,1},... | collective-permute-start | bytes 221192 | tf_op jit(solution)/shard_map/ppermute | solution.py:166
  6.0 6.5 %collective-permute-start.1 = (bf16[48,768]{1,0:T(8,128)(2,1)S(1)}, bf16[48,768]{1,0:T(8,128)(2,1)S(1)}, u32[]{:S(2)}, u32[]{:S(2)}) collective-permute-start(bf16[48,768]{1,0:T(8,128)(2,1)S(1)} %get-tuple-element.16.own_ref.refs_0_), channel_id=1, source_target_pairs={{0,12},{1,13},{2,14},{3,15},{4,8},{5,9},{6,10},{7,11},{8,4},{9,5},... | collective-permute-start | bytes 221192 | tf_op jit(solution)/shard_map/ppermute | solution.py:166
  7.3 5.3 %collective-permute-start.2 = (bf16[48,768]{1,0:T(8,128)(2,1)S(1)}, bf16[48,768]{1,0:T(8,128)(2,1)S(1)}, u32[]{:S(2)}, u32[]{:S(2)}) collective-permute-start(bf16[48,768]{1,0:T(8,128)(2,1)S(1)} %get-tuple-element.16.own_ref.refs_0_), channel_id=1, source_target_pairs={{0,4},{1,5},{2,6},{3,7},{4,0},{5,1},{6,2},{7,3},{8,12},{9,13},{10,... | collective-permute-start | bytes 221192 | tf_op jit(solution)/shard_map/ppermute | solution.py:166
  7.6 5.1 %collective-permute-start.3 = (bf16[48,768]{1,0:T(8,128)(2,1)S(1)}, bf16[48,768]{1,0:T(8,128)(2,1)S(1)}, u32[]{:S(2)}, u32[]{:S(2)}) collective-permute-start(bf16[48,768]{1,0:T(8,128)(2,1)S(1)} %get-tuple-element.16.own_ref.refs_0_), channel_id=1, source_target_pairs={{0,2},{1,3},{2,0},{3,1},{4,6},{5,7},{6,4},{7,5},{8,10},{9,11},{10,... | collective-permute-start | bytes 221192 | tf_op jit(solution)/shard_map/ppermute | solution.py:166
  9.1 3.6 %collective-permute-start.4 = (bf16[48,768]{1,0:T(8,128)(2,1)S(1)}, bf16[48,768]{1,0:T(8,128)(2,1)S(1)}, u32[]{:S(2)}, u32[]{:S(2)}) collective-permute-start(bf16[48,768]{1,0:T(8,128)(2,1)S(1)} %get-tuple-element.16.own_ref.refs_0_), channel_id=1, source_target_pairs={{0,1},{1,0},{2,3},{3,2},{4,5},{5,4},{6,7},{7,6},{8,9},{9,8},{10,11... | collective-permute-start | bytes 221192 | tf_op jit(solution)/shard_map/ppermute | solution.py:166
  12.7 1.5 %collective-permute-start.5 = (bf16[144,768]{1,0:T(8,128)(2,1)S(1)}, bf16[144,768]{1,0:T(8,128)(2,1)S(1)}, u32[]{:S(2)}, u32[]{:S(2)}) collective-permute-start(bf16[144,768]{1,0:T(8,128)(2,1)S(1)} %pad_maximum_fusion), channel_id=1, source_target_pairs={{0,1},{1,0},{2,3},{3,2},{4,5},{5,4},{6,7},{7,6},{8,9},{9,8},{10,11... | collective-permute-start | bytes 663560 | tf_op jit(solution)/shard_map/ppermute | solution.py:166
  14.6 4.5 %collective-permute-start.6 = (bf16[304,128]{1,0:T(8,128)(2,1)S(1)}, bf16[304,128]{1,0:T(8,128)(2,1)S(1)}, u32[]{:S(2)}, u32[]{:S(2)}) collective-permute-start(bf16[304,128]{1,0:T(8,128)(2,1)S(1)} %beside.1), channel_id=1, source_target_pairs={{0,2},{1,3},{2,0},{3,1},{4,6},{5,7},{6,4},{7,5},{8,10},{9,11},{10,... | collective-permute-start | bytes 233480 | tf_op jit(solution)/shard_map/ppermute | solution.py:166

commit v2 on v1

--- a/solution.py
+++ b/solution.py
@@ -36,11 +36,14 @@
     return jnp.sum(jnp.where(across == down, column, jnp.zeros_like(column)), axis=0, keepdims=True)
 
 
-def arrange_kernel(ids_hbm, rows_hbm, out_ref, moves_ref, bounds_ref, ids_ref, rows_ref, sems):
-    rows_copy = pltpu.make_async_copy(rows_hbm, rows_ref, sems.at[0])
-    ids_copy = pltpu.make_async_copy(ids_hbm, ids_ref, sems.at[1])
+LANES = 128
+
+
+def arrange_kernel(ids_hbm, rows_hbm, out_ref, moves_ref, ids_out_ref, ids_ref, rows_ref, sems):
+    ids_copy = pltpu.make_async_copy(ids_hbm, ids_ref, sems.at[0])
+    rows_copy = pltpu.make_async_copy(rows_hbm, rows_ref, sems.at[1])
+    ids_copy.start()
     rows_copy.start()
-    ids_copy.start()
     count = rows_ref.shape[0]
     ids_copy.wait()
     ids_row = ids_ref[...].reshape(1, count)
@@ -49,83 +52,82 @@
     down = lax.broadcasted_iota(jnp.int32, (count, count), 0)
     before = (ids_column < ids_row) | ((ids_column == ids_row) & (down < across))
     rank_row = jnp.sum(before.astype(jnp.int32), axis=0, keepdims=True)
-    moved = down == rank_row
-    moves = moved.astype(jnp.bfloat16)
-    moves_ref[...] = moves
-    label = jnp.sum(jnp.where(moved, ids_row, 0), axis=1, keepdims=True)
-    first = jnp.sum((ids_row < label).astype(jnp.int32), axis=1, keepdims=True)
-    after = jnp.sum((ids_row <= label).astype(jnp.int32), axis=1, keepdims=True)
-    lane = lax.broadcasted_iota(jnp.int32, bounds_ref.shape, 1)
-    bounds_ref[...] = jnp.where(lane == 0, first, after)
+    moves = (down == rank_row).astype(jnp.bfloat16)
     rows_copy.wait()
     unit = normalize_rows(rows_ref[...])
     out_ref[...] = jnp.dot(moves, unit, preferred_element_type=jnp.float32).astype(jnp.bfloat16)
-
-
-def partial_sums(queries, key_blocks, bounds, own, block_rows):
-    totals, weighted = 0.0, 0.0
-    first, after = bounds[:, 0:1], bounds[:, 1:2]
-    for index, keys in enumerate(key_blocks):
-        similar = lax.dot_general(
-            queries, keys, (((1,), (1,)), ((), ())), preferred_element_type=jnp.float32
-        )
-        place = lax.rem(lax.broadcasted_iota(jnp.int32, similar.shape, 1), block_rows)
-        allowed = (place >= first) & (place < after)
-        if own and index == 0:
-            allowed = allowed & (place != lax.broadcasted_iota(jnp.int32, similar.shape, 0))
-        weights = jnp.where(allowed, jnp.exp(sharpness * (similar - 1.0)), 0.0)
-        totals = totals + jnp.sum(weights, axis=1, keepdims=True)
-        weighted = weighted + jnp.dot(
-            weights.astype(jnp.bfloat16), keys, preferred_element_type=jnp.float32
-        )
-    return totals, weighted
-
-
-LANES = 128
-
-
-def gather_refs(refs):
-    return [ref[...] for ref in refs]
-
-
-def first_kernel(bounds_ref, own_ref, beside_ref, *refs):
-    *key_refs, weighted_ref, totals_ref = refs
+    moves_ref[...] = moves
+    ids_out_ref[...] = ids_row
+
+
+def partial_sums(queries, keys, bounds, own):
+    count = bounds.shape[0]
+    blocks = queries.shape[0] // count
+    similar = lax.dot_general(
+        queries, keys, (((1,), (1,)), ((), ())), preferred_element_type=jnp.float32
+    )
+    bounds = jnp.concatenate([bounds] * blocks, axis=0)
+    key = lax.broadcasted_iota(jnp.int32, similar.shape, 1)
+    place = lax.rem(key, count)
+    allowed = (place >= bounds[:, 0:1]) & (place < bounds[:, 1:2])
+    if own:
+        query = lax.broadcasted_iota(jnp.int32, similar.shape, 0)
+        allowed = allowed & ((key != query) | (key >= count))
+    weights = jnp.where(allowed, jnp.exp(sharpness * (similar - 1.0)), 0.0)
+    totals = jnp.sum(weights, axis=1, keepdims=True)
+    return totals, jnp.dot(weights.astype(jnp.bfloat16), keys, preferred_element_type=jnp.float32)
+
+
+def first_kernel(moves_ref, ids_ref, own_ref, beside_ref, *refs):
+    *key_refs, weighted_ref, totals_ref, bounds_ref = refs
+    ids = ids_ref[...]
+    label = jnp.sum(jnp.where(moves_ref[...] > 0, ids, 0), axis=1, keepdims=True)
+    first = jnp.sum((ids < label).astype(jnp.int32), axis=1, keepdims=True)
+    after = jnp.sum((ids <= label).astype(jnp.int32), axis=1, keepdims=True)
+    lane = lax.broadcasted_iota(jnp.int32, bounds_ref.shape, 1)
+    bounds = jnp.where(lane == 0, first, after)
+    bounds_ref[...] = bounds
     queries = jnp.concatenate([own_ref[...], beside_ref[...]], axis=0)
-    bounds = jnp.concatenate([bounds_ref[...]] * 2, axis=0)
-    totals, weighted = partial_sums(queries, gather_refs(key_refs), bounds, True, own_ref.shape[0])
+    keys = jnp.concatenate([ref[...] for ref in key_refs], axis=0)
+    totals, weighted = partial_sums(queries, keys, bounds, True)
     weighted_ref[...] = weighted
     totals_ref[...] = jnp.broadcast_to(totals, totals_ref.shape)
 
 
-def beside_kernel(so_far_ref, totals_so_far_ref, bounds_ref, beside_ref, *refs):
-    *key_refs, out_ref = refs
+def beside_kernel(so_far_ref, totals_so_far_ref, bounds_ref, beside_ref, keys_ref, out_ref):
     count = beside_ref.shape[0]
-    keys = gather_refs(key_refs)
-    totals, weighted = partial_sums(beside_ref[...], keys, bounds_ref[...], False, count)
-    totals = totals + totals_so_far_ref[count:, 0:1]
+    totals, weighted = partial_sums(beside_ref[...], keys_ref[...], bounds_ref[...], False)
     weighted = (weighted + so_far_ref[count:, :]).astype(jnp.bfloat16)
     columns = weighted.shape[1] // LANES
     for index in range(columns):
         out_ref[index * count : (index + 1) * count, :] = weighted[
             :, index * LANES : (index + 1) * LANES
         ]
-    extra = out_ref.shape[0] - columns * count
-    totals = jnp.concatenate([as_row(totals), jnp.zeros((1, LANES - count), jnp.float32)], axis=1)
+    totals = as_row(totals + totals_so_far_ref[count:, 0:1])
+    totals = jnp.concatenate([totals, jnp.zeros((1, LANES - count), jnp.float32)], axis=1)
     high = totals.astype(jnp.bfloat16).astype(jnp.float32)
-    row = lax.broadcasted_iota(jnp.int32, (extra, LANES), 0)
+    row = lax.broadcasted_iota(jnp.int32, (EXTRA, LANES), 0)
     out_ref[columns * count :, :] = jnp.where(row == 0, high, totals - high).astype(jnp.bfloat16)
 
 
-def own_kernel(so_far_ref, totals_so_far_ref, bounds_ref, own_ref, *refs):
-    *key_refs, weighted_ref, totals_ref = refs
+def own_kernel(so_far_ref, totals_so_far_ref, bounds_ref, own_ref, keys_ref, weighted_ref, totals_ref):
     count = own_ref.shape[0]
-    keys = gather_refs(key_refs)
-    totals, weighted = partial_sums(own_ref[...], keys, bounds_ref[...], False, count)
+    totals, weighted = partial_sums(own_ref[...], keys_ref[...], bounds_ref[...], False)
     weighted_ref[...] = weighted + so_far_ref[:count, :]
     totals_ref[...] = as_row(totals + totals_so_far_ref[:count, 0:1])
 
 
-def finish_kernel(moves_ref, weighted_ref, totals_ref, back_ref, neighbour_hbm, score_hbm, neighbour_ref, score_ref, sems):
+def finish_kernel(
+    moves_ref,
+    weighted_ref,
+    totals_ref,
+    back_ref,
+    neighbour_hbm,
+    score_hbm,
+    neighbour_ref,
+    score_ref,
+    sems,
+):
     count, features = neighbour_ref.shape
     columns = features // LANES
     back = [
@@ -137,19 +139,26 @@
         weighted * lax.rsqrt(jnp.mean(weighted * weighted, axis=-1, keepdims=True) + epsilon)
     ).astype(jnp.bfloat16)
     moves = moves_ref[...]
-    neighbour_ref[...] = lax.dot_general(
-        moves, normed, (((0,), (0,)), ((), ())), preferred_element_type=jnp.float32
-    ).astype(jnp.bfloat16)
-    neighbour_copy = pltpu.make_async_copy(neighbour_ref, neighbour_hbm, sems.at[0])
-    neighbour_copy.start()
+    copies = []
+    for half in range(2):
+        part = slice(half * features // 2, (half + 1) * features // 2)
+        neighbour_ref[:, part] = lax.dot_general(
+            moves, normed[:, part], (((0,), (0,)), ((), ())), preferred_element_type=jnp.float32
+        ).astype(jnp.bfloat16)
+        copies.append(
+            pltpu.make_async_copy(
+                neighbour_ref.at[:, part], neighbour_hbm.at[:, part], sems.at[half]
+            )
+        )
+        copies[-1].start()
     pair = back_ref[columns * count :, :].astype(jnp.float32)
     totals = totals_ref[...] + (pair[0:1, :count] + pair[1:2, :count])
     scores = jnp.sum(moves.astype(jnp.float32) * as_column(jnp.log(totals)), axis=0, keepdims=True)
     score_ref[...] = scores.astype(jnp.bfloat16).reshape(count)
-    score_copy = pltpu.make_async_copy(score_ref, score_hbm, sems.at[1])
-    score_copy.start()
-    neighbour_copy.wait()
-    score_copy.wait()
+    copies.append(pltpu.make_async_copy(score_ref, score_hbm, sems.at[2]))
+    copies[-1].start()
+    for copy in copies:
+        copy.wait()
 
 
 EXTRA = 16
@@ -180,10 +189,10 @@
         )(*inputs)
 
     rows = block(jnp.bfloat16, rows_dev, features)
-    own, moves, bounds = kernel(
+    own, moves, ids = kernel(
         arrange_kernel,
         "arrange",
-        (rows, block(jnp.bfloat16, rows_dev, rows_dev), block(jnp.int32, rows_dev, LANES)),
+        (rows, block(jnp.bfloat16, rows_dev, rows_dev), block(jnp.int32, 1, rows_dev)),
         pltpu.with_memory_space_constraint(cluster_id, pltpu.HBM),
         pltpu.with_memory_space_constraint(embeddings, pltpu.HBM),
         specs=stored,
@@ -198,25 +207,29 @@
         tuple(swap(own, bits) for bits in (FAR, FAR | NEAR, NEAR, ACROSS, CORE))
     )
     mates = swap(jnp.concatenate([near, far, farther], axis=0), CORE)
-    weighted, totals = kernel(
+    *so_far, bounds = kernel(
         first_kernel,
         "first",
-        (block(jnp.float32, 2 * rows_dev, features), block(jnp.float32, 2 * rows_dev, LANES)),
-        *(bounds, own, beside),
+        (
+            block(jnp.float32, 2 * rows_dev, features),
+            block(jnp.float32, 2 * rows_dev, LANES),
+            block(jnp.int32, rows_dev, LANES),
+        ),
+        *(moves, ids, own, beside),
         *(own, mate, near, far, farther),
     )
     (partial,) = kernel(
         beside_kernel,
         "beside",
         (block(jnp.bfloat16, rows_dev * features // LANES + EXTRA, LANES),),
-        *(weighted, totals, bounds, beside, mates),
+        *(*so_far, bounds, beside, mates),
     )
     back = swap(partial, ACROSS)
     weighted, totals = kernel(
         own_kernel,
         "own",
         (block(jnp.float32, rows_dev, features), block(jnp.float32, 1, rows_dev)),
-        *(weighted, totals, bounds, own, mates),
+        *(*so_far, bounds, own, mates),
     )
     return tuple(
         kernel(
@@ -228,7 +241,7 @@
             scratch=(
                 pltpu.VMEM((rows_dev, features), jnp.bfloat16),
                 pltpu.VMEM((rows_dev,), jnp.bfloat16),
-                pltpu.SemaphoreType.DMA((2,)),
+                pltpu.SemaphoreType.DMA((3,)),
             ),
         )
     )

time: 20.1 us -> 20 us (level)
  Pallas kernels: 3.99 us -> 3.32 us
  waiting for transfers between devices: 6.29 us -> 6.86 us
    pallas_call x5, Pallas kernels: 3.99 us -> 3.32 us  [kernel(): pl.pallas_call(body, out_shape=out_shape, in_specs=[specs] * len(inputs),...]
    ppermute x7, waiting for transfers between devices: 6.29 us -> 6.86 us  [swap(): lax.ppermute(value, 'blk', [(device, device ^ bits) for device in range(G...]
  transfers between devices with their start and end apart: 7 -> 7, of which waited for: 5 -> 5; matrix products, arithmetic and copies ran while one was open for 0% -> 0% of each run, Pallas kernels for 7% -> 4%
where the time goes in v2:
time: 20 us; the launch traced here: 19.9 us
  starting transfers between devices  9.01 us (45%)
  waiting for transfers between devices  6.86 us (34%)
  Pallas kernels  3.32 us (17%)
  between operations  0.66 us (3%)
    ppermute x7, starting transfers between devices, swap(): lax.ppermute(value, 'blk', [(device, device ^ bits) for device in range(G...  9.01 us
    ppermute x7, waiting for transfers between devices, swap(): lax.ppermute(value, 'blk', [(device, device ^ bits) for device in range(G...  6.86 us
    pallas_call x5, Pallas kernels, kernel(): pl.pallas_call(body, out_shape=out_shape, in_specs=[specs] * len(inputs),...  3.32 us
  transfers between devices with their start and end apart: 7, of which 5 were waited for; matrix products, arithmetic and copies ran while one was open for 0% of the time, Pallas kernels for 4%

profile of v2, /device:TPU:0, one launch (start us, length us, event | category | flops | bytes accessed | tf_op | source)
XLA Modules:
  0.0 19.9 jit_solution(7335207561713676971)
XLA Ops:
  0.6 1.2 %arrange.1 = (bf16[48,768]{1,0:T(8,128)(2,1)S(1)}, bf16[48,48]{1,0:T(8,128)(2,1)S(1)}, s32[1,48]{1,0:T(1,128)S(1)}) custom-call(s32[48]{0:T(128)} %ids_hbm.1, bf16[48,768]{1,0:T(8,128)(2,1)} %rows_hbm.1), custom_call_target="tpu_custom_call" | custom-call | tf_op jit(solution)/shard_map/arrange/pallas_call | solution.py:181
  1.8 4.1 %collective-permute-start = (bf16[48,768]{1,0:T(8,128)(2,1)S(1)}, bf16[48,768]{1,0:T(8,128)(2,1)S(1)}, u32[]{:S(2)}, u32[]{:S(2)}) collective-permute-start(bf16[48,768]{1,0:T(8,128)(2,1)S(1)} %get-tuple-element.17.own_ref.refs_0_), channel_id=1, source_target_pairs={{0,8},{1,9},{2,10},{3,11},{4,12},{5,13},{6,14},{7,15},{8,0},{9,1},... | collective-permute-start | bytes 221192 | tf_op jit(solution)/shard_map/ppermute | solution.py:175
  5.9 1.3 %collective-permute-start.1 = (bf16[48,768]{1,0:T(8,128)(2,1)S(1)}, bf16[48,768]{1,0:T(8,128)(2,1)S(1)}, u32[]{:S(2)}, u32[]{:S(2)}) collective-permute-start(bf16[48,768]{1,0:T(8,128)(2,1)S(1)} %get-tuple-element.17.own_ref.refs_0_), channel_id=1, source_target_pairs={{0,12},{1,13},{2,14},{3,15},{4,8},{5,9},{6,10},{7,11},{8,4},{9,5},... | collective-permute-start | bytes 221192 | tf_op jit(solution)/shard_map/ppermute | solution.py:175
  7.3 0.2 %collective-permute-start.2 = (bf16[48,768]{1,0:T(8,128)(2,1)S(1)}, bf16[48,768]{1,0:T(8,128)(2,1)S(1)}, u32[]{:S(2)}, u32[]{:S(2)}) collective-permute-start(bf16[48,768]{1,0:T(8,128)(2,1)S(1)} %get-tuple-element.17.own_ref.refs_0_), channel_id=1, source_target_pairs={{0,4},{1,5},{2,6},{3,7},{4,0},{5,1},{6,2},{7,3},{8,12},{9,13},{10,... | collective-permute-start | bytes 221192 | tf_op jit(solution)/shard_map/ppermute | solution.py:175
  7.5 1.5 %collective-permute-start.3 = (bf16[48,768]{1,0:T(8,128)(2,1)S(1)}, bf16[48,768]{1,0:T(8,128)(2,1)S(1)}, u32[]{:S(2)}, u32[]{:S(2)}) collective-permute-start(bf16[48,768]{1,0:T(8,128)(2,1)S(1)} %get-tuple-element.17.own_ref.refs_0_), channel_id=1, source_target_pairs={{0,2},{1,3},{2,0},{3,1},{4,6},{5,7},{6,4},{7,5},{8,10},{9,11},{10,... | collective-permute-start | bytes 221192 | tf_op jit(solution)/shard_map/ppermute | solution.py:175
  9.0 0.0 collective-permute-start.4
  9.0 1.8 %collective-permute-done.refs_3_ = bf16[48,768]{1,0:T(8,128)(2,1)S(1)} collective-permute-done((bf16[48,768]{1,0:T(8,128)(2,1)S(1)}, bf16[48,768]{1,0:T(8,128)(2,1)S(1)}, u32[]{:S(2)}, u32[]{:S(2)}) %collective-permute-start) | collective-permute-done | bytes 73760 | tf_op jit(solution)/shard_map/ppermute | solution.py:175
  10.8 1.6 %collective-permute-done.1.refs_4_ = bf16[48,768]{1,0:T(8,128)(2,1)S(1)} collective-permute-done((bf16[48,768]{1,0:T(8,128)(2,1)S(1)}, bf16[48,768]{1,0:T(8,128)(2,1)S(1)}, u32[]{:S(2)}, u32[]{:S(2)}) %collective-permute-start.1) | collective-permute-done | bytes 73760 | tf_op jit(solution)/shard_map/ppermute | solution.py:175
  12.4 0.2 collective-permute-done.2.refs_2_
  12.5 0.0 collective-permute-done.3.beside_ref
  12.5 0.0 collective-permute-done.4.refs_1_
  12.6 0.1 collective-permute-start.5
  12.6 0.5 %first.1 = (f32[96,768]{1,0:T(8,128)S(1)}, f32[96,128]{1,0:T(8,128)S(1)}, s32[48,128]{1,0:T(8,128)S(1)}) custom-call(bf16[48,48]{1,0:T(8,128)(2,1)S(1)} %get-tuple-element.15.moves_ref, s32[1,48]{1,0:T(1,128)S(1)} %get-tuple-element.16.ids_ref, bf16[48,768]{1,0:T(8,128)(2,1)S(1)} %get-tuple-element.17.own_ref.refs_0_, ...), custom_call_target="tpu_custom_call" | custom-call | tf_op jit(solution)/shard_map/first/pallas_call | solution.py:181
  13.1 1.0 %collective-permute-done.5.keys_ref = bf16[144,768]{1,0:T(8,128)(2,1)S(1)} collective-permute-done((bf16[144,768]{1,0:T(8,128)(2,1)S(1)}, bf16[144,768]{1,0:T(8,128)(2,1)S(1)}, u32[]{:S(2)}, u32[]{:S(2)}) %collective-permute-start.5) | collective-permute-done | bytes 221216 | tf_op jit(solution)/shard_map/ppermute | solution.py:175
  14.1 0.4 %beside.1 = bf16[304,128]{1,0:T(8,128)(2,1)S(1)} custom-call(f32[96,768]{1,0:T(8,128)S(1)} %get-tuple-element.23.so_far_ref, f32[96,128]{1,0:T(8,128)S(1)} %get-tuple-element.24.totals_so_far_ref, s32[48,128]{1,0:T(8,128)S(1)} %get-tuple-element.25.bounds_ref, bf16[48,768]{1,0:T(8,128)(2,1)S(1)} %collective-permute-done.3.beside_ref, ...), custom_call_target="tpu_custom_call" | custom-call | tf_op jit(solution)/shard_map/beside/pallas_call | solution.py:181
  14.5 1.8 %collective-permute-start.6 = (bf16[304,128]{1,0:T(8,128)(2,1)S(1)}, bf16[304,128]{1,0:T(8,128)(2,1)S(1)}, u32[]{:S(2)}, u32[]{:S(2)}) collective-permute-start(bf16[304,128]{1,0:T(8,128)(2,1)S(1)} %beside.1), channel_id=1, source_target_pairs={{0,2},{1,3},{2,0},{3,1},{4,6},{5,7},{6,4},{7,5},{8,10},{9,11},{10,... | collective-permute-start | bytes 233480 | tf_op jit(solution)/shard_map/ppermute | solution.py:175
  16.3 0.4 %own.1 = (f32[48,768]{1,0:T(8,128)S(1)}, f32[1,48]{1,0:T(1,128)S(1)}) custom-call(f32[96,768]{1,0:T(8,128)S(1)} %get-tuple-element.23.so_far_ref, f32[96,128]{1,0:T(8,128)S(1)} %get-tuple-element.24.totals_so_far_ref, s32[48,128]{1,0:T(8,128)S(1)} %get-tuple-element.25.bounds_ref, bf16[48,768]{1,0:T(8,128)(2,1)S(1)} %get-tuple-element.17.own_ref.refs_0_, ...), custom_call_target="tpu_custom_call" | custom-call | tf_op jit(solution)/shard_map/own/pallas_call | solution.py:181
  16.7 2.3 %collective-permute-done.6.back_ref = bf16[304,128]{1,0:T(8,128)(2,1)S(1)} collective-permute-done((bf16[304,128]{1,0:T(8,128)(2,1)S(1)}, bf16[304,128]{1,0:T(8,128)(2,1)S(1)}, u32[]{:S(2)}, u32[]{:S(2)}) %collective-permute-start.6) | collective-permute-done | bytes 77856 | tf_op jit(solution)/shard_map/ppermute | solution.py:175
  19.0 0.9 %finish.1 = (bf16[48,768]{1,0:T(8,128)(2,1)}, bf16[48]{0:T(256)(128)(2,1)}) custom-call(bf16[48,48]{1,0:T(8,128)(2,1)S(1)} %get-tuple-element.15.moves_ref, f32[48,768]{1,0:T(8,128)S(1)} %get-tuple-element.26.weighted_ref, f32[1,48]{1,0:T(1,128)S(1)} %get-tuple-element.27.totals_ref, bf16[304,128]{1,0:T(8,128)(2,1)S(1)} %collective-permute-done.6.back_ref), custom_call_target="tpu_custom_call" | custom-call | tf_op jit(solution)/shard_map/finish/pallas_call | solution.py:181
  (1 shorter events, 0.0 us)
Async XLA Ops:
  1.8 9.0 %collective-permute-start = (bf16[48,768]{1,0:T(8,128)(2,1)S(1)}, bf16[48,768]{1,0:T(8,128)(2,1)S(1)}, u32[]{:S(2)}, u32[]{:S(2)}) collective-permute-start(bf16[48,768]{1,0:T(8,128)(2,1)S(1)} %get-tuple-element.17.own_ref.refs_0_), channel_id=1, source_target_pairs={{0,8},{1,9},{2,10},{3,11},{4,12},{5,13},{6,14},{7,15},{8,0},{9,1},... | collective-permute-start | bytes 221192 | tf_op jit(solution)/shard_map/ppermute | solution.py:175
  5.9 6.5 %collective-permute-start.1 = (bf16[48,768]{1,0:T(8,128)(2,1)S(1)}, bf16[48,768]{1,0:T(8,128)(2,1)S(1)}, u32[]{:S(2)}, u32[]{:S(2)}) collective-permute-start(bf16[48,768]{1,0:T(8,128)(2,1)S(1)} %get-tuple-element.17.own_ref.refs_0_), channel_id=1, source_target_pairs={{0,12},{1,13},{2,14},{3,15},{4,8},{5,9},{6,10},{7,11},{8,4},{9,5},... | collective-permute-start | bytes 221192 | tf_op jit(solution)/shard_map/ppermute | solution.py:175
  7.3 5.3 %collective-permute-start.2 = (bf16[48,768]{1,0:T(8,128)(2,1)S(1)}, bf16[48,768]{1,0:T(8,128)(2,1)S(1)}, u32[]{:S(2)}, u32[]{:S(2)}) collective-permute-start(bf16[48,768]{1,0:T(8,128)(2,1)S(1)} %get-tuple-element.17.own_ref.refs_0_), channel_id=1, source_target_pairs={{0,4},{1,5},{2,6},{3,7},{4,0},{5,1},{6,2},{7,3},{8,12},{9,13},{10,... | collective-permute-start | bytes 221192 | tf_op jit(solution)/shard_map/ppermute | solution.py:175
  7.5 5.1 %collective-permute-start.3 = (bf16[48,768]{1,0:T(8,128)(2,1)S(1)}, bf16[48,768]{1,0:T(8,128)(2,1)S(1)}, u32[]{:S(2)}, u32[]{:S(2)}) collective-permute-start(bf16[48,768]{1,0:T(8,128)(2,1)S(1)} %get-tuple-element.17.own_ref.refs_0_), channel_id=1, source_target_pairs={{0,2},{1,3},{2,0},{3,1},{4,6},{5,7},{6,4},{7,5},{8,10},{9,11},{10,... | collective-permute-start | bytes 221192 | tf_op jit(solution)/shard_map/ppermute | solution.py:175
  9.0 3.6 %collective-permute-start.4 = (bf16[48,768]{1,0:T(8,128)(2,1)S(1)}, bf16[48,768]{1,0:T(8,128)(2,1)S(1)}, u32[]{:S(2)}, u32[]{:S(2)}) collective-permute-start(bf16[48,768]{1,0:T(8,128)(2,1)S(1)} %get-tuple-element.17.own_ref.refs_0_), channel_id=1, source_target_pairs={{0,1},{1,0},{2,3},{3,2},{4,5},{5,4},{6,7},{7,6},{8,9},{9,8},{10,11... | collective-permute-start | bytes 221192 | tf_op jit(solution)/shard_map/ppermute | solution.py:175
  12.6 1.5 %collective-permute-start.5 = (bf16[144,768]{1,0:T(8,128)(2,1)S(1)}, bf16[144,768]{1,0:T(8,128)(2,1)S(1)}, u32[]{:S(2)}, u32[]{:S(2)}) collective-permute-start(bf16[144,768]{1,0:T(8,128)(2,1)S(1)} %pad_maximum_fusion), channel_id=1, source_target_pairs={{0,1},{1,0},{2,3},{3,2},{4,5},{5,4},{6,7},{7,6},{8,9},{9,8},{10,11... | collective-permute-start | bytes 663560 | tf_op jit(solution)/shard_map/ppermute | solution.py:175
  14.5 4.5 %collective-permute-start.6 = (bf16[304,128]{1,0:T(8,128)(2,1)S(1)}, bf16[304,128]{1,0:T(8,128)(2,1)S(1)}, u32[]{:S(2)}, u32[]{:S(2)}) collective-permute-start(bf16[304,128]{1,0:T(8,128)(2,1)S(1)} %beside.1), channel_id=1, source_target_pairs={{0,2},{1,3},{2,0},{3,1},{4,6},{5,7},{6,4},{7,5},{8,10},{9,11},{10,... | collective-permute-start | bytes 233480 | tf_op jit(solution)/shard_map/ppermute | solution.py:175

commit v3 on v2

--- a/solution.py
+++ b/solution.py
@@ -60,6 +60,31 @@
     ids_out_ref[...] = ids_row
 
 
+def pack(out_ref, weighted, totals):
+    count = weighted.shape[0]
+    weighted = weighted.astype(jnp.bfloat16)
+    columns = weighted.shape[1] // LANES
+    for index in range(columns):
+        out_ref[index * count : (index + 1) * count, :] = weighted[
+            :, index * LANES : (index + 1) * LANES
+        ]
+    totals = as_row(totals)
+    totals = jnp.concatenate([totals, jnp.zeros((1, LANES - count), jnp.float32)], axis=1)
+    high = totals.astype(jnp.bfloat16).astype(jnp.float32)
+    row = lax.broadcasted_iota(jnp.int32, (EXTRA, LANES), 0)
+    out_ref[columns * count :, :] = jnp.where(row == 0, high, totals - high).astype(jnp.bfloat16)
+
+
+def unpack(packed_ref, count):
+    columns = packed_ref.shape[0] // count
+    block = [
+        packed_ref[index * count : (index + 1) * count, :].astype(jnp.float32)
+        for index in range(columns)
+    ]
+    pair = packed_ref[columns * count :, :].astype(jnp.float32)
+    return jnp.concatenate(block, axis=1), pair[0:1, :count] + pair[1:2, :count]
+
+
 def partial_sums(queries, keys, bounds, own):
     count = bounds.shape[0]
     blocks = queries.shape[0] // count
@@ -78,8 +103,7 @@
     return totals, jnp.dot(weights.astype(jnp.bfloat16), keys, preferred_element_type=jnp.float32)
 
 
-def first_kernel(moves_ref, ids_ref, own_ref, beside_ref, *refs):
-    *key_refs, weighted_ref, totals_ref, bounds_ref = refs
+def visitor_kernel(moves_ref, ids_ref, visitor_ref, own_ref, beside_ref, mates_ref, out_ref, bounds_ref):
     ids = ids_ref[...]
     label = jnp.sum(jnp.where(moves_ref[...] > 0, ids, 0), axis=1, keepdims=True)
     first = jnp.sum((ids < label).astype(jnp.int32), axis=1, keepdims=True)
@@ -87,9 +111,18 @@
     lane = lax.broadcasted_iota(jnp.int32, bounds_ref.shape, 1)
     bounds = jnp.where(lane == 0, first, after)
     bounds_ref[...] = bounds
-    queries = jnp.concatenate([own_ref[...], beside_ref[...]], axis=0)
-    keys = jnp.concatenate([ref[...] for ref in key_refs], axis=0)
-    totals, weighted = partial_sums(queries, keys, bounds, True)
+    keys = jnp.concatenate([own_ref[...], beside_ref[...], mates_ref[...]], axis=0)
+    totals, weighted = partial_sums(visitor_ref[...], keys, bounds, False)
+    pack(out_ref, weighted, totals)
+
+
+def first_kernel(bounds_ref, own_ref, beside_ref, mates_ref, *refs):
+    *key_refs, weighted_ref, totals_ref = refs
+    own = own_ref[...]
+    queries = jnp.concatenate([own, beside_ref[...]], axis=0)
+    mate = mates_ref[: own.shape[0], :]
+    keys = jnp.concatenate([own, mate, *(ref[...] for ref in key_refs)], axis=0)
+    totals, weighted = partial_sums(queries, keys, bounds_ref[...], True)
     weighted_ref[...] = weighted
     totals_ref[...] = jnp.broadcast_to(totals, totals_ref.shape)
 
@@ -97,17 +130,7 @@
 def beside_kernel(so_far_ref, totals_so_far_ref, bounds_ref, beside_ref, keys_ref, out_ref):
     count = beside_ref.shape[0]
     totals, weighted = partial_sums(beside_ref[...], keys_ref[...], bounds_ref[...], False)
-    weighted = (weighted + so_far_ref[count:, :]).astype(jnp.bfloat16)
-    columns = weighted.shape[1] // LANES
-    for index in range(columns):
-        out_ref[index * count : (index + 1) * count, :] = weighted[
-            :, index * LANES : (index + 1) * LANES
-        ]
-    totals = as_row(totals + totals_so_far_ref[count:, 0:1])
-    totals = jnp.concatenate([totals, jnp.zeros((1, LANES - count), jnp.float32)], axis=1)
-    high = totals.astype(jnp.bfloat16).astype(jnp.float32)
-    row = lax.broadcasted_iota(jnp.int32, (EXTRA, LANES), 0)
-    out_ref[columns * count :, :] = jnp.where(row == 0, high, totals - high).astype(jnp.bfloat16)
+    pack(out_ref, weighted + so_far_ref[count:, :], totals + totals_so_far_ref[count:, 0:1])
 
 
 def own_kernel(so_far_ref, totals_so_far_ref, bounds_ref, own_ref, keys_ref, weighted_ref, totals_ref):
@@ -117,53 +140,35 @@
     totals_ref[...] = as_row(totals + totals_so_far_ref[:count, 0:1])
 
 
-def finish_kernel(
-    moves_ref,
-    weighted_ref,
-    totals_ref,
-    back_ref,
-    neighbour_hbm,
-    score_hbm,
-    neighbour_ref,
-    score_ref,
-    sems,
-):
-    count, features = neighbour_ref.shape
-    columns = features // LANES
-    back = [
-        back_ref[index * count : (index + 1) * count, :].astype(jnp.float32)
-        for index in range(columns)
-    ]
-    weighted = weighted_ref[...] + jnp.concatenate(back, axis=1)
+def finish_kernel(moves_ref, weighted_ref, totals_ref, *refs):
+    *back_refs, neighbour_hbm, score_hbm, neighbour_ref, score_ref, sems = refs
+    count = neighbour_ref.shape[0]
+    weighted, totals = weighted_ref[...], totals_ref[...]
+    for back_ref in back_refs:
+        back, back_totals = unpack(back_ref, count)
+        weighted = weighted + back
+        totals = totals + back_totals
     normed = (
         weighted * lax.rsqrt(jnp.mean(weighted * weighted, axis=-1, keepdims=True) + epsilon)
     ).astype(jnp.bfloat16)
     moves = moves_ref[...]
-    copies = []
-    for half in range(2):
-        part = slice(half * features // 2, (half + 1) * features // 2)
-        neighbour_ref[:, part] = lax.dot_general(
-            moves, normed[:, part], (((0,), (0,)), ((), ())), preferred_element_type=jnp.float32
-        ).astype(jnp.bfloat16)
-        copies.append(
-            pltpu.make_async_copy(
-                neighbour_ref.at[:, part], neighbour_hbm.at[:, part], sems.at[half]
-            )
-        )
-        copies[-1].start()
-    pair = back_ref[columns * count :, :].astype(jnp.float32)
-    totals = totals_ref[...] + (pair[0:1, :count] + pair[1:2, :count])
+    neighbour_ref[...] = lax.dot_general(
+        moves, normed, (((0,), (0,)), ((), ())), preferred_element_type=jnp.float32
+    ).astype(jnp.bfloat16)
+    neighbour_copy = pltpu.make_async_copy(neighbour_ref, neighbour_hbm, sems.at[0])
+    neighbour_copy.start()
     scores = jnp.sum(moves.astype(jnp.float32) * as_column(jnp.log(totals)), axis=0, keepdims=True)
     score_ref[...] = scores.astype(jnp.bfloat16).reshape(count)
-    copies.append(pltpu.make_async_copy(score_ref, score_hbm, sems.at[2]))
-    copies[-1].start()
-    for copy in copies:
-        copy.wait()
+    score_copy = pltpu.make_async_copy(score_ref, score_hbm, sems.at[1])
+    score_copy.start()
+    neighbour_copy.wait()
+    score_copy.wait()
 
 
 EXTRA = 16
-CORE, ACROSS, NEAR, FAR = 1, 2, 4, 8
-GRID = 16
+CORE, ACROSS, NEAR = 1, 2, 4
+PLANE, GRID = 4, 16
+NEXT = (3, 2, 0, 1)
 
 
 def gathered_body(embeddings, cluster_id):
@@ -173,6 +178,12 @@
 
     def swap(value, bits):
         return lax.ppermute(value, "blk", [(device, device ^ bits) for device in range(GRID)])
+
+    def visit(value, home):
+        pairs = [
+            (device, NEXT[device // PLANE] * PLANE + device % PLANE) for device in range(GRID)
+        ]
+        return lax.ppermute(value, "blk", [pair[::-1] for pair in pairs] if home else pairs)
 
     def block(kind, *shape):
         return jax.ShapeDtypeStruct(shape, kind)
@@ -203,45 +214,46 @@
         ),
     )
 
-    far, farther, near, beside, mate = lax.optimization_barrier(
-        tuple(swap(own, bits) for bits in (FAR, FAR | NEAR, NEAR, ACROSS, CORE))
-    )
-    mates = swap(jnp.concatenate([near, far, farther], axis=0), CORE)
-    *so_far, bounds = kernel(
+    packed = block(jnp.bfloat16, rows_dev * features // LANES + EXTRA, LANES)
+    visitor = visit(own, home=False)
+    beside = swap(own, ACROSS)
+    near = swap(own, NEAR)
+    mates = swap(jnp.concatenate([own, beside], axis=0), CORE)
+    visitor, near = lax.optimization_barrier((visitor, near))
+    later = swap(jnp.concatenate([near, visitor], axis=0), CORE)
+    partial, bounds = kernel(
+        visitor_kernel,
+        "visitor",
+        (packed, block(jnp.int32, rows_dev, LANES)),
+        *(moves, ids, visitor, own, beside, mates),
+    )
+    back_home = visit(partial, home=True)
+    so_far = kernel(
         first_kernel,
         "first",
-        (
-            block(jnp.float32, 2 * rows_dev, features),
-            block(jnp.float32, 2 * rows_dev, LANES),
-            block(jnp.int32, rows_dev, LANES),
-        ),
-        *(moves, ids, own, beside),
-        *(own, mate, near, far, farther),
-    )
-    (partial,) = kernel(
-        beside_kernel,
-        "beside",
-        (block(jnp.bfloat16, rows_dev * features // LANES + EXTRA, LANES),),
-        *(*so_far, bounds, beside, mates),
-    )
+        (block(jnp.float32, 2 * rows_dev, features), block(jnp.float32, 2 * rows_dev, LANES)),
+        *(bounds, own, beside, mates, near, visitor),
+    )
+    (partial,) = kernel(beside_kernel, "beside", (packed,), *so_far, bounds, beside, later)
     back = swap(partial, ACROSS)
     weighted, totals = kernel(
         own_kernel,
         "own",
         (block(jnp.float32, rows_dev, features), block(jnp.float32, 1, rows_dev)),
-        *(*so_far, bounds, own, mates),
-    )
+        *(*so_far, bounds, own, later),
+    )
+    weighted, back_home = lax.optimization_barrier((weighted, back_home))
     return tuple(
         kernel(
             finish_kernel,
             "finish",
             (rows, block(jnp.bfloat16, rows_dev)),
-            *(moves, weighted, totals, back),
+            *(moves, weighted, totals, back, back_home),
             out_specs=stored,
             scratch=(
                 pltpu.VMEM((rows_dev, features), jnp.bfloat16),
                 pltpu.VMEM((rows_dev,), jnp.bfloat16),
-                pltpu.SemaphoreType.DMA((3,)),
+                pltpu.SemaphoreType.DMA((2,)),
             ),
         )
     )

time: 20 us -> 21.1 us (1.055)
  waiting for transfers between devices: 6.86 us -> 9.14 us
  starting transfers between devices: 9.01 us -> 7.41 us
  Pallas kernels: 3.32 us -> 3.69 us
    ppermute x0 -> x2, waiting for transfers between devices: none -> 6.53 us  [visit(): lax.ppermute(value, 'blk', [pair[::-1] for pair in pairs] if home else pa...]
    ppermute x7 -> x5, starting transfers between devices: 9.01 us -> 3.75 us  [swap(): lax.ppermute(value, 'blk', [(device, device ^ bits) for device in range(G...]
    ppermute x7 -> x5, waiting for transfers between devices: 6.86 us -> 2.61 us  [swap(): lax.ppermute(value, 'blk', [(device, device ^ bits) for device in range(G...]
    ppermute x0 -> x2, starting transfers between devices: none -> 3.66 us  [visit(): lax.ppermute(value, 'blk', [pair[::-1] for pair in pairs] if home else pa...]
    pallas_call x5 -> x6, Pallas kernels: 3.32 us -> 3.69 us  [kernel(): pl.pallas_call(body, out_shape=out_shape, in_specs=[specs] * len(inputs),...]
  transfers between devices with their start and end apart: 7 -> 7, of which waited for: 5 -> 4; matrix products, arithmetic and copies ran while one was open for 0% -> 0% of each run, Pallas kernels for 4% -> 8%
where the time goes in v3:
time: 21.1 us; the launch traced here: 21 us
  waiting for transfers between devices  9.14 us (43%)
  starting transfers between devices  7.41 us (35%)
  Pallas kernels  3.69 us (17%)
  between operations  0.7 us (3%)
    ppermute x2, waiting for transfers between devices, visit(): lax.ppermute(value, 'blk', [pair[::-1] for pair in pairs] if home else pa...  6.53 us
    ppermute x5, starting transfers between devices, swap(): lax.ppermute(value, 'blk', [(device, device ^ bits) for device in range(G...  3.75 us
    pallas_call x6, Pallas kernels, kernel(): pl.pallas_call(body, out_shape=out_shape, in_specs=[specs] * len(inputs),...  3.69 us
    ppermute x2, starting transfers between devices, visit(): lax.ppermute(value, 'blk', [pair[::-1] for pair in pairs] if home else pa...  3.66 us
    ppermute x5, waiting for transfers between devices, swap(): lax.ppermute(value, 'blk', [(device, device ^ bits) for device in range(G...  2.61 us
  transfers between devices with their start and end apart: 7, of which 4 were waited for; matrix products, arithmetic and copies ran while one was open for 0% of the time, Pallas kernels for 8%

profile of v3, /device:TPU:0, one launch (start us, length us, event | category | flops | bytes accessed | tf_op | source)
XLA Modules:
  0.0 21.0 jit_solution(8043761940763509464)
XLA Ops:
  0.6 1.2 %arrange.1 = (bf16[48,768]{1,0:T(8,128)(2,1)S(1)}, bf16[48,48]{1,0:T(8,128)(2,1)S(1)}, s32[1,48]{1,0:T(1,128)S(1)}) custom-call(s32[48]{0:T(128)} %ids_hbm.1, bf16[48,768]{1,0:T(8,128)(2,1)} %rows_hbm.1), custom_call_target="tpu_custom_call" | custom-call | tf_op jit(solution)/shard_map/arrange/pallas_call | solution.py:192
  1.8 3.0 %collective-permute-start.2 = (bf16[48,768]{1,0:T(8,128)(2,1)S(1)}, bf16[48,768]{1,0:T(8,128)(2,1)S(1)}, u32[]{:S(2)}, u32[]{:S(2)}) collective-permute-start(bf16[48,768]{1,0:T(8,128)(2,1)S(1)} %get-tuple-element.17.own_ref), channel_id=1, source_target_pairs={{0,2},{1,3},{2,0},{3,1},{4,6},{5,7},{6,4},{7,5},{8,10},{9,11},{10,... | collective-permute-start | bytes 221192 | tf_op jit(solution)/shard_map/ppermute | solution.py:180
  4.8 3.6 %collective-permute-start = (bf16[48,768]{1,0:T(8,128)(2,1)S(1)}, bf16[48,768]{1,0:T(8,128)(2,1)S(1)}, u32[]{:S(2)}, u32[]{:S(2)}) collective-permute-start(bf16[48,768]{1,0:T(8,128)(2,1)S(1)} %get-tuple-element.17.own_ref), channel_id=1, source_target_pairs={{0,12},{1,13},{2,14},{3,15},{4,8},{5,9},{6,10},{7,11},{8,0},{9,1},... | collective-permute-start | bytes 221192 | tf_op jit(solution)/shard_map/ppermute | solution.py:186
  8.4 0.0 collective-permute-start.1
  8.4 0.0 collective-permute-done.2.beside_ref
  8.4 0.1 collective-permute-start.3
  8.5 2.0 %collective-permute-done.visitor_ref.refs_1_ = bf16[48,768]{1,0:T(8,128)(2,1)S(1)} collective-permute-done((bf16[48,768]{1,0:T(8,128)(2,1)S(1)}, bf16[48,768]{1,0:T(8,128)(2,1)S(1)}, u32[]{:S(2)}, u32[]{:S(2)}) %collective-permute-start) | collective-permute-done | bytes 73760 | tf_op jit(solution)/shard_map/ppermute | solution.py:186
  10.6 2.2 %collective-permute-done.1.refs_0_ = bf16[48,768]{1,0:T(8,128)(2,1)S(1)} collective-permute-done((bf16[48,768]{1,0:T(8,128)(2,1)S(1)}, bf16[48,768]{1,0:T(8,128)(2,1)S(1)}, u32[]{:S(2)}, u32[]{:S(2)}) %collective-permute-start.1) | collective-permute-done | bytes 73760 | tf_op jit(solution)/shard_map/ppermute | solution.py:180
  12.8 0.1 collective-permute-start.4
  12.9 0.0 collective-permute-done.3.mates_ref
  12.9 0.5 %visitor.1 = (bf16[304,128]{1,0:T(8,128)(2,1)S(1)}, s32[48,128]{1,0:T(8,128)S(1)}) custom-call(bf16[48,48]{1,0:T(8,128)(2,1)S(1)} %get-tuple-element.15.moves_ref, s32[1,48]{1,0:T(1,128)S(1)} %get-tuple-element.16.ids_ref, bf16[48,768]{1,0:T(8,128)(2,1)S(1)} %collective-permute-done.visitor_ref.refs_1_, bf16[48,768]{1,0:T(8,128)(2,1)S(1)} %get-tuple-element.17.own_ref, ...), custom_call_target="tpu_custom_call" | custom-call | tf_op jit(solution)/shard_map/visitor/pallas_call | solution.py:192
  13.3 0.1 collective-permute-start.5
  13.4 0.4 %first.1 = (f32[96,768]{1,0:T(8,128)S(1)}, f32[96,128]{1,0:T(8,128)S(1)}) custom-call(s32[48,128]{1,0:T(8,128)S(1)} %get-tuple-element.19.bounds_ref, bf16[48,768]{1,0:T(8,128)(2,1)S(1)} %get-tuple-element.17.own_ref, bf16[48,768]{1,0:T(8,128)(2,1)S(1)} %collective-permute-done.2.beside_ref, bf16[96,768]{1,0:T(8,128)(2,1)S(1)} %collective-permute-done.3.mates_ref, ...), custom_call_target="tpu_custom_call" | custom-call | tf_op jit(solution)/shard_map/first/pallas_call | solution.py:192
  13.8 0.4 %collective-permute-done.4.keys_ref = bf16[96,768]{1,0:T(8,128)(2,1)S(1)} collective-permute-done((bf16[96,768]{1,0:T(8,128)(2,1)S(1)}, bf16[96,768]{1,0:T(8,128)(2,1)S(1)}, u32[]{:S(2)}, u32[]{:S(2)}) %collective-permute-start.4) | collective-permute-done | bytes 147488 | tf_op jit(solution)/shard_map/ppermute | solution.py:180
  14.2 0.4 %beside.1 = bf16[304,128]{1,0:T(8,128)(2,1)S(1)} custom-call(f32[96,768]{1,0:T(8,128)S(1)} %get-tuple-element.21.so_far_ref, f32[96,128]{1,0:T(8,128)S(1)} %get-tuple-element.22.totals_so_far_ref, s32[48,128]{1,0:T(8,128)S(1)} %get-tuple-element.19.bounds_ref, bf16[48,768]{1,0:T(8,128)(2,1)S(1)} %collective-permute-done.2.beside_ref, ...), custom_call_target="tpu_custom_call" | custom-call | tf_op jit(solution)/shard_map/beside/pallas_call | solution.py:192
  14.6 0.6 %collective-permute-start.6 = (bf16[304,128]{1,0:T(8,128)(2,1)S(1)}, bf16[304,128]{1,0:T(8,128)(2,1)S(1)}, u32[]{:S(2)}, u32[]{:S(2)}) collective-permute-start(bf16[304,128]{1,0:T(8,128)(2,1)S(1)} %beside.1), channel_id=1, source_target_pairs={{0,2},{1,3},{2,0},{3,1},{4,6},{5,7},{6,4},{7,5},{8,10},{9,11},{10,... | collective-permute-start | bytes 233480 | tf_op jit(solution)/shard_map/ppermute | solution.py:180
  15.2 0.4 %own.1 = (f32[48,768]{1,0:T(8,128)S(1)}, f32[1,48]{1,0:T(1,128)S(1)}) custom-call(f32[96,768]{1,0:T(8,128)S(1)} %get-tuple-element.21.so_far_ref, f32[96,128]{1,0:T(8,128)S(1)} %get-tuple-element.22.totals_so_far_ref, s32[48,128]{1,0:T(8,128)S(1)} %get-tuple-element.19.bounds_ref, bf16[48,768]{1,0:T(8,128)(2,1)S(1)} %get-tuple-element.17.own_ref, ...), custom_call_target="tpu_custom_call" | custom-call | tf_op jit(solution)/shard_map/own/pallas_call | solution.py:192
  15.5 4.5 %collective-permute-done.5.refs_1_ = bf16[304,128]{1,0:T(8,128)(2,1)S(1)} collective-permute-done((bf16[304,128]{1,0:T(8,128)(2,1)S(1)}, bf16[304,128]{1,0:T(8,128)(2,1)S(1)}, u32[]{:S(2)}, u32[]{:S(2)}) %collective-permute-start.5) | collective-permute-done | bytes 77856 | tf_op jit(solution)/shard_map/ppermute | solution.py:186
  20.0 0.0 collective-permute-done.6.refs_0_
  20.0 0.9 %finish.1 = (bf16[48,768]{1,0:T(8,128)(2,1)}, bf16[48]{0:T(256)(128)(2,1)}) custom-call(bf16[48,48]{1,0:T(8,128)(2,1)S(1)} %get-tuple-element.15.moves_ref, f32[48,768]{1,0:T(8,128)S(1)} %get-tuple-element.25.weighted_ref, f32[1,48]{1,0:T(1,128)S(1)} %get-tuple-element.26.totals_ref, bf16[304,128]{1,0:T(8,128)(2,1)S(1)} %collective-permute-done.6.refs_0_, ...), custom_call_target="tpu_custom_call" | custom-call | tf_op jit(solution)/shard_map/finish/pallas_call | solution.py:192
  (2 shorter events, 0.0 us)
Async XLA Ops:
  1.8 6.6 %collective-permute-start.2 = (bf16[48,768]{1,0:T(8,128)(2,1)S(1)}, bf16[48,768]{1,0:T(8,128)(2,1)S(1)}, u32[]{:S(2)}, u32[]{:S(2)}) collective-permute-start(bf16[48,768]{1,0:T(8,128)(2,1)S(1)} %get-tuple-element.17.own_ref), channel_id=1, source_target_pairs={{0,2},{1,3},{2,0},{3,1},{4,6},{5,7},{6,4},{7,5},{8,10},{9,11},{10,... | collective-permute-start | bytes 221192 | tf_op jit(solution)/shard_map/ppermute | solution.py:180
  4.8 5.7 %collective-permute-start = (bf16[48,768]{1,0:T(8,128)(2,1)S(1)}, bf16[48,768]{1,0:T(8,128)(2,1)S(1)}, u32[]{:S(2)}, u32[]{:S(2)}) collective-permute-start(bf16[48,768]{1,0:T(8,128)(2,1)S(1)} %get-tuple-element.17.own_ref), channel_id=1, source_target_pairs={{0,12},{1,13},{2,14},{3,15},{4,8},{5,9},{6,10},{7,11},{8,0},{9,1},... | collective-permute-start | bytes 221192 | tf_op jit(solution)/shard_map/ppermute | solution.py:186
  8.4 4.4 %collective-permute-start.1 = (bf16[48,768]{1,0:T(8,128)(2,1)S(1)}, bf16[48,768]{1,0:T(8,128)(2,1)S(1)}, u32[]{:S(2)}, u32[]{:S(2)}) collective-permute-start(bf16[48,768]{1,0:T(8,128)(2,1)S(1)} %get-tuple-element.17.own_ref), channel_id=1, source_target_pairs={{0,4},{1,5},{2,6},{3,7},{4,0},{5,1},{6,2},{7,3},{8,12},{9,13},{10,... | collective-permute-start | bytes 221192 | tf_op jit(solution)/shard_map/ppermute | solution.py:180
  8.4 4.4 %collective-permute-start.3 = (bf16[96,768]{1,0:T(8,128)(2,1)S(1)}, bf16[96,768]{1,0:T(8,128)(2,1)S(1)}, u32[]{:S(2)}, u32[]{:S(2)}) collective-permute-start(bf16[96,768]{1,0:T(8,128)(2,1)S(1)} %pad_maximum_fusion), channel_id=1, source_target_pairs={{0,1},{1,0},{2,3},{3,2},{4,5},{5,4},{6,7},{7,6},{8,9},{9,8},{10,11... | collective-permute-start | bytes 442376 | tf_op jit(solution)/shard_map/ppermute | solution.py:180
  12.8 1.4 %collective-permute-start.4 = (bf16[96,768]{1,0:T(8,128)(2,1)S(1)}, bf16[96,768]{1,0:T(8,128)(2,1)S(1)}, u32[]{:S(2)}, u32[]{:S(2)}) collective-permute-start(bf16[96,768]{1,0:T(8,128)(2,1)S(1)} %pad_maximum_fusion.1), channel_id=1, source_target_pairs={{0,1},{1,0},{2,3},{3,2},{4,5},{5,4},{6,7},{7,6},{8,9},{9,8},{10,11... | collective-permute-start | bytes 442376 | tf_op jit(solution)/shard_map/ppermute | solution.py:180
  13.3 6.7 %collective-permute-start.5 = (bf16[304,128]{1,0:T(8,128)(2,1)S(1)}, bf16[304,128]{1,0:T(8,128)(2,1)S(1)}, u32[]{:S(2)}, u32[]{:S(2)}) collective-permute-start(bf16[304,128]{1,0:T(8,128)(2,1)S(1)} %get-tuple-element.24), channel_id=1, source_target_pairs={{12,0},{13,1},{14,2},{15,3},{8,4},{9,5},{10,6},{11,7},{0,8},{1,9},... | collective-permute-start | bytes 233480 | tf_op jit(solution)/shard_map/ppermute | solution.py:186
  14.6 5.5 %collective-permute-start.6 = (bf16[304,128]{1,0:T(8,128)(2,1)S(1)}, bf16[304,128]{1,0:T(8,128)(2,1)S(1)}, u32[]{:S(2)}, u32[]{:S(2)}) collective-permute-start(bf16[304,128]{1,0:T(8,128)(2,1)S(1)} %beside.1), channel_id=1, source_target_pairs={{0,2},{1,3},{2,0},{3,1},{4,6},{5,7},{6,4},{7,5},{8,10},{9,11},{10,... | collective-permute-start | bytes 233480 | tf_op jit(solution)/shard_map/ppermute | solution.py:180

commit v4 on v3

--- a/solution.py
+++ b/solution.py
@@ -168,7 +168,7 @@
 EXTRA = 16
 CORE, ACROSS, NEAR = 1, 2, 4
 PLANE, GRID = 4, 16
-NEXT = (3, 2, 0, 1)
+NEXT = (2, 3, 1, 0)
 
 
 def gathered_body(embeddings, cluster_id):
@@ -215,11 +215,9 @@
     )
 
     packed = block(jnp.bfloat16, rows_dev * features // LANES + EXTRA, LANES)
-    visitor = visit(own, home=False)
-    beside = swap(own, ACROSS)
     near = swap(own, NEAR)
+    visitor, beside = lax.optimization_barrier((visit(own, home=False), swap(own, ACROSS)))
     mates = swap(jnp.concatenate([own, beside], axis=0), CORE)
-    visitor, near = lax.optimization_barrier((visitor, near))
     later = swap(jnp.concatenate([near, visitor], axis=0), CORE)
     partial, bounds = kernel(
         visitor_kernel,

time: 21.1 us -> 21.7 us (1.028)
  starting transfers between devices: 7.41 us -> 11.8 us
  waiting for transfers between devices: 9.14 us -> 5.33 us
    ppermute x2, waiting for transfers between devices: 6.53 us -> 2.12 us  [visit(): lax.ppermute(value, 'blk', [pair[::-1] for pair in pairs] if home else pa...]
    ppermute x2, starting transfers between devices: 3.66 us -> 7.13 us  [visit(): lax.ppermute(value, 'blk', [pair[::-1] for pair in pairs] if home else pa...]
    ppermute x5, starting transfers between devices: 3.75 us -> 4.66 us  [swap(): lax.ppermute(value, 'blk', [(device, device ^ bits) for device in range(G...]
    ppermute x5, waiting for transfers between devices: 2.61 us -> 3.21 us  [swap(): lax.ppermute(value, 'blk', [(device, device ^ bits) for device in range(G...]
  transfers between devices with their start and end apart: 7 -> 7, of which waited for: 4 -> 5; matrix products, arithmetic and copies ran while one was open for 0% -> 0% of each run, Pallas kernels for 8% -> 7%
where the time goes in v4:
time: 21.7 us; the launch traced here: 21.5 us
  starting transfers between devices  11.8 us (54%)
  waiting for transfers between devices  5.33 us (25%)
  Pallas kernels  3.69 us (17%)
  between operations  0.7 us (3%)
    ppermute x2, starting transfers between devices, visit(): lax.ppermute(value, 'blk', [pair[::-1] for pair in pairs] if home else pa...  7.13 us
    ppermute x5, starting transfers between devices, swap(): lax.ppermute(value, 'blk', [(device, device ^ bits) for device in range(G...  4.66 us
    pallas_call x6, Pallas kernels, kernel(): pl.pallas_call(body, out_shape=out_shape, in_specs=[specs] * len(inputs),...  3.69 us
    ppermute x5, waiting for transfers between devices, swap(): lax.ppermute(value, 'blk', [(device, device ^ bits) for device in range(G...  3.21 us
    ppermute x2, waiting for transfers between devices, visit(): lax.ppermute(value, 'blk', [pair[::-1] for pair in pairs] if home else pa...  2.12 us
  transfers between devices with their start and end apart: 7, of which 5 were waited for; matrix products, arithmetic and copies ran while one was open for 0% of the time, Pallas kernels for 7%

profile of v4, /device:TPU:0, one launch (start us, length us, event | category | flops | bytes accessed | tf_op | source)
XLA Modules:
  0.0 21.5 jit_solution(11871444872146328107)
XLA Ops:
  0.6 1.2 %arrange.1 = (bf16[48,768]{1,0:T(8,128)(2,1)S(1)}, bf16[48,48]{1,0:T(8,128)(2,1)S(1)}, s32[1,48]{1,0:T(1,128)S(1)}) custom-call(s32[48]{0:T(128)} %ids_hbm.1, bf16[48,768]{1,0:T(8,128)(2,1)} %rows_hbm.1), custom_call_target="tpu_custom_call" | custom-call | tf_op jit(solution)/shard_map/arrange/pallas_call | solution.py:192
  1.8 4.1 %collective-permute-start = (bf16[48,768]{1,0:T(8,128)(2,1)S(1)}, bf16[48,768]{1,0:T(8,128)(2,1)S(1)}, u32[]{:S(2)}, u32[]{:S(2)}) collective-permute-start(bf16[48,768]{1,0:T(8,128)(2,1)S(1)} %get-tuple-element.17.own_ref), channel_id=1, source_target_pairs={{0,8},{1,9},{2,10},{3,11},{4,12},{5,13},{6,14},{7,15},{8,4},{9,5},... | collective-permute-start | bytes 221192 | tf_op jit(solution)/shard_map/ppermute | solution.py:186
  5.9 1.5 %collective-permute-start.1 = (bf16[48,768]{1,0:T(8,128)(2,1)S(1)}, bf16[48,768]{1,0:T(8,128)(2,1)S(1)}, u32[]{:S(2)}, u32[]{:S(2)}) collective-permute-start(bf16[48,768]{1,0:T(8,128)(2,1)S(1)} %get-tuple-element.17.own_ref), channel_id=1, source_target_pairs={{0,2},{1,3},{2,0},{3,1},{4,6},{5,7},{6,4},{7,5},{8,10},{9,11},{10,... | collective-permute-start | bytes 221192 | tf_op jit(solution)/shard_map/ppermute | solution.py:180
  7.4 1.6 %collective-permute-start.3 = (bf16[48,768]{1,0:T(8,128)(2,1)S(1)}, bf16[48,768]{1,0:T(8,128)(2,1)S(1)}, u32[]{:S(2)}, u32[]{:S(2)}) collective-permute-start(bf16[48,768]{1,0:T(8,128)(2,1)S(1)} %get-tuple-element.17.own_ref), channel_id=1, source_target_pairs={{0,4},{1,5},{2,6},{3,7},{4,0},{5,1},{6,2},{7,3},{8,12},{9,13},{10,... | collective-permute-start | bytes 221192 | tf_op jit(solution)/shard_map/ppermute | solution.py:180
  9.0 0.4 %collective-permute-done.visitor_ref.refs_1_ = bf16[48,768]{1,0:T(8,128)(2,1)S(1)} collective-permute-done((bf16[48,768]{1,0:T(8,128)(2,1)S(1)}, bf16[48,768]{1,0:T(8,128)(2,1)S(1)}, u32[]{:S(2)}, u32[]{:S(2)}) %collective-permute-start) | collective-permute-done | bytes 73760 | tf_op jit(solution)/shard_map/ppermute | solution.py:186
  9.4 0.9 %collective-permute-done.1.beside_ref = bf16[48,768]{1,0:T(8,128)(2,1)S(1)} collective-permute-done((bf16[48,768]{1,0:T(8,128)(2,1)S(1)}, bf16[48,768]{1,0:T(8,128)(2,1)S(1)}, u32[]{:S(2)}, u32[]{:S(2)}) %collective-permute-start.1) | collective-permute-done | bytes 73760 | tf_op jit(solution)/shard_map/ppermute | solution.py:180
  10.3 0.1 collective-permute-start.2
  10.3 1.4 %collective-permute-done.3.refs_0_ = bf16[48,768]{1,0:T(8,128)(2,1)S(1)} collective-permute-done((bf16[48,768]{1,0:T(8,128)(2,1)S(1)}, bf16[48,768]{1,0:T(8,128)(2,1)S(1)}, u32[]{:S(2)}, u32[]{:S(2)}) %collective-permute-start.3) | collective-permute-done | bytes 73760 | tf_op jit(solution)/shard_map/ppermute | solution.py:180
  11.8 0.1 collective-permute-start.4
  11.8 0.0 collective-permute-done.2.mates_ref
  11.8 0.5 %visitor.1 = (bf16[304,128]{1,0:T(8,128)(2,1)S(1)}, s32[48,128]{1,0:T(8,128)S(1)}) custom-call(bf16[48,48]{1,0:T(8,128)(2,1)S(1)} %get-tuple-element.15.moves_ref, s32[1,48]{1,0:T(1,128)S(1)} %get-tuple-element.16.ids_ref, bf16[48,768]{1,0:T(8,128)(2,1)S(1)} %collective-permute-done.visitor_ref.refs_1_, bf16[48,768]{1,0:T(8,128)(2,1)S(1)} %get-tuple-element.17.own_ref, ...), custom_call_target="tpu_custom_call" | custom-call | tf_op jit(solution)/shard_map/visitor/pallas_call | solution.py:192
  12.3 3.0 %collective-permute-start.5 = (bf16[304,128]{1,0:T(8,128)(2,1)S(1)}, bf16[304,128]{1,0:T(8,128)(2,1)S(1)}, u32[]{:S(2)}, u32[]{:S(2)}) collective-permute-start(bf16[304,128]{1,0:T(8,128)(2,1)S(1)} %get-tuple-element.24), channel_id=1, source_target_pairs={{8,0},{9,1},{10,2},{11,3},{12,4},{13,5},{14,6},{15,7},{4,8},{5,9},... | collective-permute-start | bytes 233480 | tf_op jit(solution)/shard_map/ppermute | solution.py:186
  15.3 0.4 %first.1 = (f32[96,768]{1,0:T(8,128)S(1)}, f32[96,128]{1,0:T(8,128)S(1)}) custom-call(s32[48,128]{1,0:T(8,128)S(1)} %get-tuple-element.20.bounds_ref, bf16[48,768]{1,0:T(8,128)(2,1)S(1)} %get-tuple-element.17.own_ref, bf16[48,768]{1,0:T(8,128)(2,1)S(1)} %collective-permute-done.1.beside_ref, bf16[96,768]{1,0:T(8,128)(2,1)S(1)} %collective-permute-done.2.mates_ref, ...), custom_call_target="tpu_custom_call" | custom-call | tf_op jit(solution)/shard_map/first/pallas_call | solution.py:192
  15.8 0.0 collective-permute-done.4.keys_ref
  15.8 0.4 %beside.1 = bf16[304,128]{1,0:T(8,128)(2,1)S(1)} custom-call(f32[96,768]{1,0:T(8,128)S(1)} %get-tuple-element.21.so_far_ref, f32[96,128]{1,0:T(8,128)S(1)} %get-tuple-element.22.totals_so_far_ref, s32[48,128]{1,0:T(8,128)S(1)} %get-tuple-element.20.bounds_ref, bf16[48,768]{1,0:T(8,128)(2,1)S(1)} %collective-permute-done.1.beside_ref, ...), custom_call_target="tpu_custom_call" | custom-call | tf_op jit(solution)/shard_map/beside/pallas_call | solution.py:192
  16.2 1.5 %collective-permute-start.6 = (bf16[304,128]{1,0:T(8,128)(2,1)S(1)}, bf16[304,128]{1,0:T(8,128)(2,1)S(1)}, u32[]{:S(2)}, u32[]{:S(2)}) collective-permute-start(bf16[304,128]{1,0:T(8,128)(2,1)S(1)} %beside.1), channel_id=1, source_target_pairs={{0,2},{1,3},{2,0},{3,1},{4,6},{5,7},{6,4},{7,5},{8,10},{9,11},{10,... | collective-permute-start | bytes 233480 | tf_op jit(solution)/shard_map/ppermute | solution.py:180
  17.6 0.4 %own.1 = (f32[48,768]{1,0:T(8,128)S(1)}, f32[1,48]{1,0:T(1,128)S(1)}) custom-call(f32[96,768]{1,0:T(8,128)S(1)} %get-tuple-element.21.so_far_ref, f32[96,128]{1,0:T(8,128)S(1)} %get-tuple-element.22.totals_so_far_ref, s32[48,128]{1,0:T(8,128)S(1)} %get-tuple-element.20.bounds_ref, bf16[48,768]{1,0:T(8,128)(2,1)S(1)} %get-tuple-element.17.own_ref, ...), custom_call_target="tpu_custom_call" | custom-call | tf_op jit(solution)/shard_map/own/pallas_call | solution.py:192
  18.0 1.7 %collective-permute-done.5.refs_1_ = bf16[304,128]{1,0:T(8,128)(2,1)S(1)} collective-permute-done((bf16[304,128]{1,0:T(8,128)(2,1)S(1)}, bf16[304,128]{1,0:T(8,128)(2,1)S(1)}, u32[]{:S(2)}, u32[]{:S(2)}) %collective-permute-start.5) | collective-permute-done | bytes 77856 | tf_op jit(solution)/shard_map/ppermute | solution.py:186
  19.7 0.9 %collective-permute-done.6.refs_0_ = bf16[304,128]{1,0:T(8,128)(2,1)S(1)} collective-permute-done((bf16[304,128]{1,0:T(8,128)(2,1)S(1)}, bf16[304,128]{1,0:T(8,128)(2,1)S(1)}, u32[]{:S(2)}, u32[]{:S(2)}) %collective-permute-start.6) | collective-permute-done | bytes 77856 | tf_op jit(solution)/shard_map/ppermute | solution.py:180
  20.6 0.9 %finish.1 = (bf16[48,768]{1,0:T(8,128)(2,1)}, bf16[48]{0:T(256)(128)(2,1)}) custom-call(bf16[48,48]{1,0:T(8,128)(2,1)S(1)} %get-tuple-element.15.moves_ref, f32[48,768]{1,0:T(8,128)S(1)} %get-tuple-element.25.weighted_ref, f32[1,48]{1,0:T(1,128)S(1)} %get-tuple-element.26.totals_ref, bf16[304,128]{1,0:T(8,128)(2,1)S(1)} %collective-permute-done.6.refs_0_, ...), custom_call_target="tpu_custom_call" | custom-call | tf_op jit(solution)/shard_map/finish/pallas_call | solution.py:192
  (2 shorter events, 0.0 us)
Async XLA Ops:
  1.8 7.6 %collective-permute-start = (bf16[48,768]{1,0:T(8,128)(2,1)S(1)}, bf16[48,768]{1,0:T(8,128)(2,1)S(1)}, u32[]{:S(2)}, u32[]{:S(2)}) collective-permute-start(bf16[48,768]{1,0:T(8,128)(2,1)S(1)} %get-tuple-element.17.own_ref), channel_id=1, source_target_pairs={{0,8},{1,9},{2,10},{3,11},{4,12},{5,13},{6,14},{7,15},{8,4},{9,5},... | collective-permute-start | bytes 221192 | tf_op jit(solution)/shard_map/ppermute | solution.py:186
  5.9 4.4 %collective-permute-start.1 = (bf16[48,768]{1,0:T(8,128)(2,1)S(1)}, bf16[48,768]{1,0:T(8,128)(2,1)S(1)}, u32[]{:S(2)}, u32[]{:S(2)}) collective-permute-start(bf16[48,768]{1,0:T(8,128)(2,1)S(1)} %get-tuple-element.17.own_ref), channel_id=1, source_target_pairs={{0,2},{1,3},{2,0},{3,1},{4,6},{5,7},{6,4},{7,5},{8,10},{9,11},{10,... | collective-permute-start | bytes 221192 | tf_op jit(solution)/shard_map/ppermute | solution.py:180
  7.4 4.4 %collective-permute-start.3 = (bf16[48,768]{1,0:T(8,128)(2,1)S(1)}, bf16[48,768]{1,0:T(8,128)(2,1)S(1)}, u32[]{:S(2)}, u32[]{:S(2)}) collective-permute-start(bf16[48,768]{1,0:T(8,128)(2,1)S(1)} %get-tuple-element.17.own_ref), channel_id=1, source_target_pairs={{0,4},{1,5},{2,6},{3,7},{4,0},{5,1},{6,2},{7,3},{8,12},{9,13},{10,... | collective-permute-start | bytes 221192 | tf_op jit(solution)/shard_map/ppermute | solution.py:180
  10.3 1.6 %collective-permute-start.2 = (bf16[96,768]{1,0:T(8,128)(2,1)S(1)}, bf16[96,768]{1,0:T(8,128)(2,1)S(1)}, u32[]{:S(2)}, u32[]{:S(2)}) collective-permute-start(bf16[96,768]{1,0:T(8,128)(2,1)S(1)} %pad_maximum_fusion), channel_id=1, source_target_pairs={{0,1},{1,0},{2,3},{3,2},{4,5},{5,4},{6,7},{7,6},{8,9},{9,8},{10,11... | collective-permute-start | bytes 442376 | tf_op jit(solution)/shard_map/ppermute | solution.py:180
  11.8 4.0 %collective-permute-start.4 = (bf16[96,768]{1,0:T(8,128)(2,1)S(1)}, bf16[96,768]{1,0:T(8,128)(2,1)S(1)}, u32[]{:S(2)}, u32[]{:S(2)}) collective-permute-start(bf16[96,768]{1,0:T(8,128)(2,1)S(1)} %pad_maximum_fusion.1), channel_id=1, source_target_pairs={{0,1},{1,0},{2,3},{3,2},{4,5},{5,4},{6,7},{7,6},{8,9},{9,8},{10,11... | collective-permute-start | bytes 442376 | tf_op jit(solution)/shard_map/ppermute | solution.py:180
  12.3 7.4 %collective-permute-start.5 = (bf16[304,128]{1,0:T(8,128)(2,1)S(1)}, bf16[304,128]{1,0:T(8,128)(2,1)S(1)}, u32[]{:S(2)}, u32[]{:S(2)}) collective-permute-start(bf16[304,128]{1,0:T(8,128)(2,1)S(1)} %get-tuple-element.24), channel_id=1, source_target_pairs={{8,0},{9,1},{10,2},{11,3},{12,4},{13,5},{14,6},{15,7},{4,8},{5,9},... | collective-permute-start | bytes 233480 | tf_op jit(solution)/shard_map/ppermute | solution.py:186
  16.2 4.5 %collective-permute-start.6 = (bf16[304,128]{1,0:T(8,128)(2,1)S(1)}, bf16[304,128]{1,0:T(8,128)(2,1)S(1)}, u32[]{:S(2)}, u32[]{:S(2)}) collective-permute-start(bf16[304,128]{1,0:T(8,128)(2,1)S(1)} %beside.1), channel_id=1, source_target_pairs={{0,2},{1,3},{2,0},{3,1},{4,6},{5,7},{6,4},{7,5},{8,10},{9,11},{10,... | collective-permute-start | bytes 233480 | tf_op jit(solution)/shard_map/ppermute | solution.py:180

commit v5 on v4

--- a/solution.py
+++ b/solution.py
@@ -166,9 +166,9 @@
 
 
 EXTRA = 16
-CORE, ACROSS, NEAR = 1, 2, 4
+CORE, ACROSS, MIRROR = 1, 2, 12
 PLANE, GRID = 4, 16
-NEXT = (2, 3, 1, 0)
+NEXT = (2, 0, 3, 1)
 
 
 def gathered_body(embeddings, cluster_id):
@@ -215,10 +215,10 @@
     )
 
     packed = block(jnp.bfloat16, rows_dev * features // LANES + EXTRA, LANES)
-    near = swap(own, NEAR)
-    visitor, beside = lax.optimization_barrier((visit(own, home=False), swap(own, ACROSS)))
+    mirror, beside = lax.optimization_barrier((swap(own, MIRROR), swap(own, ACROSS)))
+    visitor = visit(own, home=False)
     mates = swap(jnp.concatenate([own, beside], axis=0), CORE)
-    later = swap(jnp.concatenate([near, visitor], axis=0), CORE)
+    later = swap(jnp.concatenate([mirror, visitor], axis=0), CORE)
     partial, bounds = kernel(
         visitor_kernel,
         "visitor",
@@ -230,7 +230,7 @@
         first_kernel,
         "first",
         (block(jnp.float32, 2 * rows_dev, features), block(jnp.float32, 2 * rows_dev, LANES)),
-        *(bounds, own, beside, mates, near, visitor),
+        *(bounds, own, beside, mates, mirror, visitor),
     )
     (partial,) = kernel(beside_kernel, "beside", (packed,), *so_far, bounds, beside, later)
     back = swap(partial, ACROSS)

time: 21.7 us -> 20.2 us (0.931)
  starting transfers between devices: 11.8 us -> 8.27 us
  waiting for transfers between devices: 5.33 us -> 7.41 us
    ppermute x2, starting transfers between devices: 7.13 us -> 0.5 us  [visit(): lax.ppermute(value, 'blk', [pair[::-1] for pair in pairs] if home else pa...]
    ppermute x5, starting transfers between devices: 4.66 us -> 7.77 us  [swap(): lax.ppermute(value, 'blk', [(device, device ^ bits) for device in range(G...]
    ppermute x2, waiting for transfers between devices: 2.12 us -> 4.4 us  [visit(): lax.ppermute(value, 'blk', [pair[::-1] for pair in pairs] if home else pa...]
  transfers between devices with their start and end apart: 7 -> 7, of which waited for: 5 -> 5; matrix products, arithmetic and copies ran while one was open for 0% -> 0% of each run, Pallas kernels for 7% -> 8%
where the time goes in v5:
time: 20.2 us; the launch traced here: 20.1 us
  starting transfers between devices  8.27 us (41%)
  waiting for transfers between devices  7.41 us (37%)
  Pallas kernels  3.69 us (18%)
  between operations  0.7 us (3%)
    ppermute x5, starting transfers between devices, swap(): lax.ppermute(value, 'blk', [(device, device ^ bits) for device in range(G...  7.77 us
    ppermute x2, waiting for transfers between devices, visit(): lax.ppermute(value, 'blk', [pair[::-1] for pair in pairs] if home else pa...  4.4 us
    pallas_call x6, Pallas kernels, kernel(): pl.pallas_call(body, out_shape=out_shape, in_specs=[specs] * len(inputs),...  3.69 us
    ppermute x5, waiting for transfers between devices, swap(): lax.ppermute(value, 'blk', [(device, device ^ bits) for device in range(G...  3.01 us
    ppermute x2, starting transfers between devices, visit(): lax.ppermute(value, 'blk', [pair[::-1] for pair in pairs] if home else pa...  0.5 us
  transfers between devices with their start and end apart: 7, of which 5 were waited for; matrix products, arithmetic and copies ran while one was open for 0% of the time, Pallas kernels for 8%

profile of v5, /device:TPU:0, one launch (start us, length us, event | category | flops | bytes accessed | tf_op | source)
XLA Modules:
  0.0 20.1 jit_solution(9419469322443642135)
XLA Ops:
  0.6 1.2 %arrange.1 = (bf16[48,768]{1,0:T(8,128)(2,1)S(1)}, bf16[48,48]{1,0:T(8,128)(2,1)S(1)}, s32[1,48]{1,0:T(1,128)S(1)}) custom-call(s32[48]{0:T(128)} %ids_hbm.1, bf16[48,768]{1,0:T(8,128)(2,1)} %rows_hbm.1), custom_call_target="tpu_custom_call" | custom-call | tf_op jit(solution)/shard_map/arrange/pallas_call | solution.py:192
  1.8 5.1 %collective-permute-start.1 = (bf16[48,768]{1,0:T(8,128)(2,1)S(1)}, bf16[48,768]{1,0:T(8,128)(2,1)S(1)}, u32[]{:S(2)}, u32[]{:S(2)}) collective-permute-start(bf16[48,768]{1,0:T(8,128)(2,1)S(1)} %get-tuple-element.17.own_ref), channel_id=1, source_target_pairs={{0,12},{1,13},{2,14},{3,15},{4,8},{5,9},{6,10},{7,11},{8,4},{9,5},... | collective-permute-start | bytes 221192 | tf_op jit(solution)/shard_map/ppermute | solution.py:180
  6.9 1.5 %collective-permute-start.2 = (bf16[48,768]{1,0:T(8,128)(2,1)S(1)}, bf16[48,768]{1,0:T(8,128)(2,1)S(1)}, u32[]{:S(2)}, u32[]{:S(2)}) collective-permute-start(bf16[48,768]{1,0:T(8,128)(2,1)S(1)} %get-tuple-element.17.own_ref), channel_id=1, source_target_pairs={{0,2},{1,3},{2,0},{3,1},{4,6},{5,7},{6,4},{7,5},{8,10},{9,11},{10,... | collective-permute-start | bytes 221192 | tf_op jit(solution)/shard_map/ppermute | solution.py:180
  8.4 0.0 collective-permute-start
  8.4 1.1 %collective-permute-done.1.refs_0_ = bf16[48,768]{1,0:T(8,128)(2,1)S(1)} collective-permute-done((bf16[48,768]{1,0:T(8,128)(2,1)S(1)}, bf16[48,768]{1,0:T(8,128)(2,1)S(1)}, u32[]{:S(2)}, u32[]{:S(2)}) %collective-permute-start.1) | collective-permute-done | bytes 73760 | tf_op jit(solution)/shard_map/ppermute | solution.py:180
  9.5 1.8 %collective-permute-done.2.beside_ref = bf16[48,768]{1,0:T(8,128)(2,1)S(1)} collective-permute-done((bf16[48,768]{1,0:T(8,128)(2,1)S(1)}, bf16[48,768]{1,0:T(8,128)(2,1)S(1)}, u32[]{:S(2)}, u32[]{:S(2)}) %collective-permute-start.2) | collective-permute-done | bytes 73760 | tf_op jit(solution)/shard_map/ppermute | solution.py:180
  11.3 0.1 collective-permute-start.3
  11.4 1.4 %collective-permute-done.visitor_ref.refs_1_ = bf16[48,768]{1,0:T(8,128)(2,1)S(1)} collective-permute-done((bf16[48,768]{1,0:T(8,128)(2,1)S(1)}, bf16[48,768]{1,0:T(8,128)(2,1)S(1)}, u32[]{:S(2)}, u32[]{:S(2)}) %collective-permute-start) | collective-permute-done | bytes 73760 | tf_op jit(solution)/shard_map/ppermute | solution.py:186
  12.8 0.1 collective-permute-start.4
  12.9 0.0 collective-permute-done.3.mates_ref
  12.9 0.5 %visitor.1 = (bf16[304,128]{1,0:T(8,128)(2,1)S(1)}, s32[48,128]{1,0:T(8,128)S(1)}) custom-call(bf16[48,48]{1,0:T(8,128)(2,1)S(1)} %get-tuple-element.15.moves_ref, s32[1,48]{1,0:T(1,128)S(1)} %get-tuple-element.16.ids_ref, bf16[48,768]{1,0:T(8,128)(2,1)S(1)} %collective-permute-done.visitor_ref.refs_1_, bf16[48,768]{1,0:T(8,128)(2,1)S(1)} %get-tuple-element.17.own_ref, ...), custom_call_target="tpu_custom_call" | custom-call | tf_op jit(solution)/shard_map/visitor/pallas_call | solution.py:192
  13.3 0.5 %collective-permute-start.5 = (bf16[304,128]{1,0:T(8,128)(2,1)S(1)}, bf16[304,128]{1,0:T(8,128)(2,1)S(1)}, u32[]{:S(2)}, u32[]{:S(2)}) collective-permute-start(bf16[304,128]{1,0:T(8,128)(2,1)S(1)} %get-tuple-element.24), channel_id=1, source_target_pairs={{8,0},{9,1},{10,2},{11,3},{0,4},{1,5},{2,6},{3,7},{12,8},{13,9},{1... | collective-permute-start | bytes 233480 | tf_op jit(solution)/shard_map/ppermute | solution.py:186
  13.8 0.4 %first.1 = (f32[96,768]{1,0:T(8,128)S(1)}, f32[96,128]{1,0:T(8,128)S(1)}) custom-call(s32[48,128]{1,0:T(8,128)S(1)} %get-tuple-element.19.bounds_ref, bf16[48,768]{1,0:T(8,128)(2,1)S(1)} %get-tuple-element.17.own_ref, bf16[48,768]{1,0:T(8,128)(2,1)S(1)} %collective-permute-done.2.beside_ref, bf16[96,768]{1,0:T(8,128)(2,1)S(1)} %collective-permute-done.3.mates_ref, ...), custom_call_target="tpu_custom_call" | custom-call | tf_op jit(solution)/shard_map/first/pallas_call | solution.py:192
  14.3 0.0 collective-permute-done.4.keys_ref
  14.3 0.4 %beside.1 = bf16[304,128]{1,0:T(8,128)(2,1)S(1)} custom-call(f32[96,768]{1,0:T(8,128)S(1)} %get-tuple-element.21.so_far_ref, f32[96,128]{1,0:T(8,128)S(1)} %get-tuple-element.22.totals_so_far_ref, s32[48,128]{1,0:T(8,128)S(1)} %get-tuple-element.19.bounds_ref, bf16[48,768]{1,0:T(8,128)(2,1)S(1)} %collective-permute-done.2.beside_ref, ...), custom_call_target="tpu_custom_call" | custom-call | tf_op jit(solution)/shard_map/beside/pallas_call | solution.py:192
  14.6 1.0 %collective-permute-start.6 = (bf16[304,128]{1,0:T(8,128)(2,1)S(1)}, bf16[304,128]{1,0:T(8,128)(2,1)S(1)}, u32[]{:S(2)}, u32[]{:S(2)}) collective-permute-start(bf16[304,128]{1,0:T(8,128)(2,1)S(1)} %beside.1), channel_id=1, source_target_pairs={{0,2},{1,3},{2,0},{3,1},{4,6},{5,7},{6,4},{7,5},{8,10},{9,11},{10,... | collective-permute-start | bytes 233480 | tf_op jit(solution)/shard_map/ppermute | solution.py:180
  15.7 0.4 %own.1 = (f32[48,768]{1,0:T(8,128)S(1)}, f32[1,48]{1,0:T(1,128)S(1)}) custom-call(f32[96,768]{1,0:T(8,128)S(1)} %get-tuple-element.21.so_far_ref, f32[96,128]{1,0:T(8,128)S(1)} %get-tuple-element.22.totals_so_far_ref, s32[48,128]{1,0:T(8,128)S(1)} %get-tuple-element.19.bounds_ref, bf16[48,768]{1,0:T(8,128)(2,1)S(1)} %get-tuple-element.17.own_ref, ...), custom_call_target="tpu_custom_call" | custom-call | tf_op jit(solution)/shard_map/own/pallas_call | solution.py:192
  16.0 3.0 %collective-permute-done.5.refs_1_ = bf16[304,128]{1,0:T(8,128)(2,1)S(1)} collective-permute-done((bf16[304,128]{1,0:T(8,128)(2,1)S(1)}, bf16[304,128]{1,0:T(8,128)(2,1)S(1)}, u32[]{:S(2)}, u32[]{:S(2)}) %collective-permute-start.5) | collective-permute-done | bytes 77856 | tf_op jit(solution)/shard_map/ppermute | solution.py:186
  19.0 0.1 collective-permute-done.6.refs_0_
  19.2 0.9 %finish.1 = (bf16[48,768]{1,0:T(8,128)(2,1)}, bf16[48]{0:T(256)(128)(2,1)}) custom-call(bf16[48,48]{1,0:T(8,128)(2,1)S(1)} %get-tuple-element.15.moves_ref, f32[48,768]{1,0:T(8,128)S(1)} %get-tuple-element.25.weighted_ref, f32[1,48]{1,0:T(1,128)S(1)} %get-tuple-element.26.totals_ref, bf16[304,128]{1,0:T(8,128)(2,1)S(1)} %collective-permute-done.6.refs_0_, ...), custom_call_target="tpu_custom_call" | custom-call | tf_op jit(solution)/shard_map/finish/pallas_call | solution.py:192
  (2 shorter events, 0.0 us)
Async XLA Ops:
  1.8 7.7 %collective-permute-start.1 = (bf16[48,768]{1,0:T(8,128)(2,1)S(1)}, bf16[48,768]{1,0:T(8,128)(2,1)S(1)}, u32[]{:S(2)}, u32[]{:S(2)}) collective-permute-start(bf16[48,768]{1,0:T(8,128)(2,1)S(1)} %get-tuple-element.17.own_ref), channel_id=1, source_target_pairs={{0,12},{1,13},{2,14},{3,15},{4,8},{5,9},{6,10},{7,11},{8,4},{9,5},... | collective-permute-start | bytes 221192 | tf_op jit(solution)/shard_map/ppermute | solution.py:180
  6.9 4.4 %collective-permute-start.2 = (bf16[48,768]{1,0:T(8,128)(2,1)S(1)}, bf16[48,768]{1,0:T(8,128)(2,1)S(1)}, u32[]{:S(2)}, u32[]{:S(2)}) collective-permute-start(bf16[48,768]{1,0:T(8,128)(2,1)S(1)} %get-tuple-element.17.own_ref), channel_id=1, source_target_pairs={{0,2},{1,3},{2,0},{3,1},{4,6},{5,7},{6,4},{7,5},{8,10},{9,11},{10,... | collective-permute-start | bytes 221192 | tf_op jit(solution)/shard_map/ppermute | solution.py:180
  8.4 4.4 %collective-permute-start = (bf16[48,768]{1,0:T(8,128)(2,1)S(1)}, bf16[48,768]{1,0:T(8,128)(2,1)S(1)}, u32[]{:S(2)}, u32[]{:S(2)}) collective-permute-start(bf16[48,768]{1,0:T(8,128)(2,1)S(1)} %get-tuple-element.17.own_ref), channel_id=1, source_target_pairs={{0,8},{1,9},{2,10},{3,11},{4,0},{5,1},{6,2},{7,3},{8,12},{9,13},{1... | collective-permute-start | bytes 221192 | tf_op jit(solution)/shard_map/ppermute | solution.py:186
  11.3 1.6 %collective-permute-start.3 = (bf16[96,768]{1,0:T(8,128)(2,1)S(1)}, bf16[96,768]{1,0:T(8,128)(2,1)S(1)}, u32[]{:S(2)}, u32[]{:S(2)}) collective-permute-start(bf16[96,768]{1,0:T(8,128)(2,1)S(1)} %pad_maximum_fusion), channel_id=1, source_target_pairs={{0,1},{1,0},{2,3},{3,2},{4,5},{5,4},{6,7},{7,6},{8,9},{9,8},{10,11... | collective-permute-start | bytes 442376 | tf_op jit(solution)/shard_map/ppermute | solution.py:180
  12.8 1.5 %collective-permute-start.4 = (bf16[96,768]{1,0:T(8,128)(2,1)S(1)}, bf16[96,768]{1,0:T(8,128)(2,1)S(1)}, u32[]{:S(2)}, u32[]{:S(2)}) collective-permute-start(bf16[96,768]{1,0:T(8,128)(2,1)S(1)} %pad_maximum_fusion.1), channel_id=1, source_target_pairs={{0,1},{1,0},{2,3},{3,2},{4,5},{5,4},{6,7},{7,6},{8,9},{9,8},{10,11... | collective-permute-start | bytes 442376 | tf_op jit(solution)/shard_map/ppermute | solution.py:180
  13.3 5.7 %collective-permute-start.5 = (bf16[304,128]{1,0:T(8,128)(2,1)S(1)}, bf16[304,128]{1,0:T(8,128)(2,1)S(1)}, u32[]{:S(2)}, u32[]{:S(2)}) collective-permute-start(bf16[304,128]{1,0:T(8,128)(2,1)S(1)} %get-tuple-element.24), channel_id=1, source_target_pairs={{8,0},{9,1},{10,2},{11,3},{0,4},{1,5},{2,6},{3,7},{12,8},{13,9},{1... | collective-permute-start | bytes 233480 | tf_op jit(solution)/shard_map/ppermute | solution.py:186
  14.6 4.5 %collective-permute-start.6 = (bf16[304,128]{1,0:T(8,128)(2,1)S(1)}, bf16[304,128]{1,0:T(8,128)(2,1)S(1)}, u32[]{:S(2)}, u32[]{:S(2)}) collective-permute-start(bf16[304,128]{1,0:T(8,128)(2,1)S(1)} %beside.1), channel_id=1, source_target_pairs={{0,2},{1,3},{2,0},{3,1},{4,6},{5,7},{6,4},{7,5},{8,10},{9,11},{10,... | collective-permute-start | bytes 233480 | tf_op jit(solution)/shard_map/ppermute | solution.py:180

commit v6 on v5

--- a/solution.py
+++ b/solution.py
@@ -215,9 +215,9 @@
     )
 
     packed = block(jnp.bfloat16, rows_dev * features // LANES + EXTRA, LANES)
-    mirror, beside = lax.optimization_barrier((swap(own, MIRROR), swap(own, ACROSS)))
-    visitor = visit(own, home=False)
+    beside = swap(own, ACROSS)
     mates = swap(jnp.concatenate([own, beside], axis=0), CORE)
+    mirror, visitor = lax.optimization_barrier((swap(own, MIRROR), visit(own, home=False)))
     later = swap(jnp.concatenate([mirror, visitor], axis=0), CORE)
     partial, bounds = kernel(
         visitor_kernel,

time: 20.2 us -> 20.4 us (level)
  waiting for transfers between devices: 7.41 us -> 7.83 us
  starting transfers between devices: 8.27 us -> 7.97 us
    ppermute x5, waiting for transfers between devices: 3.01 us -> 3.61 us  [swap(): lax.ppermute(value, 'blk', [(device, device ^ bits) for device in range(G...]
    ppermute x5, starting transfers between devices: 7.77 us -> 7.35 us  [swap(): lax.ppermute(value, 'blk', [(device, device ^ bits) for device in range(G...]
  transfers between devices with their start and end apart: 7 -> 7, of which waited for: 5 -> 4; matrix products, arithmetic and copies ran while one was open for 0% -> 0% of each run, Pallas kernels for 8% -> 8%
where the time goes in v6:
time: 20.4 us; the launch traced here: 20.2 us
  starting transfers between devices  7.97 us (39%)
  waiting for transfers between devices  7.83 us (38%)
  Pallas kernels  3.69 us (18%)
  between operations  0.7 us (3%)
    ppermute x5, starting transfers between devices, swap(): lax.ppermute(value, 'blk', [(device, device ^ bits) for device in range(G...  7.35 us
    ppermute x2, waiting for transfers between devices, visit(): lax.ppermute(value, 'blk', [pair[::-1] for pair in pairs] if home else pa...  4.22 us
    pallas_call x6, Pallas kernels, kernel(): pl.pallas_call(body, out_shape=out_shape, in_specs=[specs] * len(inputs),...  3.69 us
    ppermute x5, waiting for transfers between devices, swap(): lax.ppermute(value, 'blk', [(device, device ^ bits) for device in range(G...  3.61 us
    ppermute x2, starting transfers between devices, visit(): lax.ppermute(value, 'blk', [pair[::-1] for pair in pairs] if home else pa...  0.62 us
  transfers between devices with their start and end apart: 7, of which 4 were waited for; matrix products, arithmetic and copies ran while one was open for 0% of the time, Pallas kernels for 8%

profile of v6, /device:TPU:0, one launch (start us, length us, event | category | flops | bytes accessed | tf_op | source)
XLA Modules:
  0.0 20.2 jit_solution(1543720804978633520)
XLA Ops:
  0.6 1.2 %arrange.1 = (bf16[48,768]{1,0:T(8,128)(2,1)S(1)}, bf16[48,48]{1,0:T(8,128)(2,1)S(1)}, s32[1,48]{1,0:T(1,128)S(1)}) custom-call(s32[48]{0:T(128)} %ids_hbm.1, bf16[48,768]{1,0:T(8,128)(2,1)} %rows_hbm.1), custom_call_target="tpu_custom_call" | custom-call | tf_op jit(solution)/shard_map/arrange/pallas_call | solution.py:192
  1.8 3.0 %collective-permute-start.2 = (bf16[48,768]{1,0:T(8,128)(2,1)S(1)}, bf16[48,768]{1,0:T(8,128)(2,1)S(1)}, u32[]{:S(2)}, u32[]{:S(2)}) collective-permute-start(bf16[48,768]{1,0:T(8,128)(2,1)S(1)} %get-tuple-element.17.own_ref), channel_id=1, source_target_pairs={{0,2},{1,3},{2,0},{3,1},{4,6},{5,7},{6,4},{7,5},{8,10},{9,11},{10,... | collective-permute-start | bytes 221192 | tf_op jit(solution)/shard_map/ppermute | solution.py:180
  4.8 3.6 %collective-permute-start = (bf16[48,768]{1,0:T(8,128)(2,1)S(1)}, bf16[48,768]{1,0:T(8,128)(2,1)S(1)}, u32[]{:S(2)}, u32[]{:S(2)}) collective-permute-start(bf16[48,768]{1,0:T(8,128)(2,1)S(1)} %get-tuple-element.17.own_ref), channel_id=1, source_target_pairs={{0,12},{1,13},{2,14},{3,15},{4,8},{5,9},{6,10},{7,11},{8,4},{9,5},... | collective-permute-start | bytes 221192 | tf_op jit(solution)/shard_map/ppermute | solution.py:180
  8.4 0.0 collective-permute-start.1
  8.4 0.0 collective-permute-done.2.beside_ref
  8.4 0.1 collective-permute-start.3
  8.5 3.3 %collective-permute-done.refs_0_ = bf16[48,768]{1,0:T(8,128)(2,1)S(1)} collective-permute-done((bf16[48,768]{1,0:T(8,128)(2,1)S(1)}, bf16[48,768]{1,0:T(8,128)(2,1)S(1)}, u32[]{:S(2)}, u32[]{:S(2)}) %collective-permute-start) | collective-permute-done | bytes 73760 | tf_op jit(solution)/shard_map/ppermute | solution.py:180
  11.9 0.9 %collective-permute-done.1.visitor_ref.refs_1_ = bf16[48,768]{1,0:T(8,128)(2,1)S(1)} collective-permute-done((bf16[48,768]{1,0:T(8,128)(2,1)S(1)}, bf16[48,768]{1,0:T(8,128)(2,1)S(1)}, u32[]{:S(2)}, u32[]{:S(2)}) %collective-permute-start.1) | collective-permute-done | bytes 73760 | tf_op jit(solution)/shard_map/ppermute | solution.py:186
  12.8 0.1 collective-permute-start.4
  12.9 0.0 collective-permute-done.3.mates_ref
  12.9 0.5 %visitor.1 = (bf16[304,128]{1,0:T(8,128)(2,1)S(1)}, s32[48,128]{1,0:T(8,128)S(1)}) custom-call(bf16[48,48]{1,0:T(8,128)(2,1)S(1)} %get-tuple-element.15.moves_ref, s32[1,48]{1,0:T(1,128)S(1)} %get-tuple-element.16.ids_ref, bf16[48,768]{1,0:T(8,128)(2,1)S(1)} %collective-permute-done.1.visitor_ref.refs_1_, bf16[48,768]{1,0:T(8,128)(2,1)S(1)} %get-tuple-element.17.own_ref, ...), custom_call_target="tpu_custom_call" | custom-call | tf_op jit(solution)/shard_map/visitor/pallas_call | solution.py:192
  13.3 0.6 %collective-permute-start.5 = (bf16[304,128]{1,0:T(8,128)(2,1)S(1)}, bf16[304,128]{1,0:T(8,128)(2,1)S(1)}, u32[]{:S(2)}, u32[]{:S(2)}) collective-permute-start(bf16[304,128]{1,0:T(8,128)(2,1)S(1)} %get-tuple-element.24), channel_id=1, source_target_pairs={{8,0},{9,1},{10,2},{11,3},{0,4},{1,5},{2,6},{3,7},{12,8},{13,9},{1... | collective-permute-start | bytes 233480 | tf_op jit(solution)/shard_map/ppermute | solution.py:186
  13.9 0.4 %first.1 = (f32[96,768]{1,0:T(8,128)S(1)}, f32[96,128]{1,0:T(8,128)S(1)}) custom-call(s32[48,128]{1,0:T(8,128)S(1)} %get-tuple-element.19.bounds_ref, bf16[48,768]{1,0:T(8,128)(2,1)S(1)} %get-tuple-element.17.own_ref, bf16[48,768]{1,0:T(8,128)(2,1)S(1)} %collective-permute-done.2.beside_ref, bf16[96,768]{1,0:T(8,128)(2,1)S(1)} %collective-permute-done.3.mates_ref, ...), custom_call_target="tpu_custom_call" | custom-call | tf_op jit(solution)/shard_map/first/pallas_call | solution.py:192
  14.4 0.0 collective-permute-done.4.keys_ref
  14.4 0.4 %beside.1 = bf16[304,128]{1,0:T(8,128)(2,1)S(1)} custom-call(f32[96,768]{1,0:T(8,128)S(1)} %get-tuple-element.21.so_far_ref, f32[96,128]{1,0:T(8,128)S(1)} %get-tuple-element.22.totals_so_far_ref, s32[48,128]{1,0:T(8,128)S(1)} %get-tuple-element.19.bounds_ref, bf16[48,768]{1,0:T(8,128)(2,1)S(1)} %collective-permute-done.2.beside_ref, ...), custom_call_target="tpu_custom_call" | custom-call | tf_op jit(solution)/shard_map/beside/pallas_call | solution.py:192
  14.8 0.6 %collective-permute-start.6 = (bf16[304,128]{1,0:T(8,128)(2,1)S(1)}, bf16[304,128]{1,0:T(8,128)(2,1)S(1)}, u32[]{:S(2)}, u32[]{:S(2)}) collective-permute-start(bf16[304,128]{1,0:T(8,128)(2,1)S(1)} %beside.1), channel_id=1, source_target_pairs={{0,2},{1,3},{2,0},{3,1},{4,6},{5,7},{6,4},{7,5},{8,10},{9,11},{10,... | collective-permute-start | bytes 233480 | tf_op jit(solution)/shard_map/ppermute | solution.py:180
  15.4 0.4 %own.1 = (f32[48,768]{1,0:T(8,128)S(1)}, f32[1,48]{1,0:T(1,128)S(1)}) custom-call(f32[96,768]{1,0:T(8,128)S(1)} %get-tuple-element.21.so_far_ref, f32[96,128]{1,0:T(8,128)S(1)} %get-tuple-element.22.totals_so_far_ref, s32[48,128]{1,0:T(8,128)S(1)} %get-tuple-element.19.bounds_ref, bf16[48,768]{1,0:T(8,128)(2,1)S(1)} %get-tuple-element.17.own_ref, ...), custom_call_target="tpu_custom_call" | custom-call | tf_op jit(solution)/shard_map/own/pallas_call | solution.py:192
  15.7 3.3 %collective-permute-done.5.refs_1_ = bf16[304,128]{1,0:T(8,128)(2,1)S(1)} collective-permute-done((bf16[304,128]{1,0:T(8,128)(2,1)S(1)}, bf16[304,128]{1,0:T(8,128)(2,1)S(1)}, u32[]{:S(2)}, u32[]{:S(2)}) %collective-permute-start.5) | collective-permute-done | bytes 77856 | tf_op jit(solution)/shard_map/ppermute | solution.py:186
  19.0 0.3 %collective-permute-done.6.refs_0_ = bf16[304,128]{1,0:T(8,128)(2,1)S(1)} collective-permute-done((bf16[304,128]{1,0:T(8,128)(2,1)S(1)}, bf16[304,128]{1,0:T(8,128)(2,1)S(1)}, u32[]{:S(2)}, u32[]{:S(2)}) %collective-permute-start.6) | collective-permute-done | bytes 77856 | tf_op jit(solution)/shard_map/ppermute | solution.py:180
  19.3 0.9 %finish.1 = (bf16[48,768]{1,0:T(8,128)(2,1)}, bf16[48]{0:T(256)(128)(2,1)}) custom-call(bf16[48,48]{1,0:T(8,128)(2,1)S(1)} %get-tuple-element.15.moves_ref, f32[48,768]{1,0:T(8,128)S(1)} %get-tuple-element.25.weighted_ref, f32[1,48]{1,0:T(1,128)S(1)} %get-tuple-element.26.totals_ref, bf16[304,128]{1,0:T(8,128)(2,1)S(1)} %collective-permute-done.6.refs_0_, ...), custom_call_target="tpu_custom_call" | custom-call | tf_op jit(solution)/shard_map/finish/pallas_call | solution.py:192
  (2 shorter events, 0.0 us)
Async XLA Ops:
  1.8 6.6 %collective-permute-start.2 = (bf16[48,768]{1,0:T(8,128)(2,1)S(1)}, bf16[48,768]{1,0:T(8,128)(2,1)S(1)}, u32[]{:S(2)}, u32[]{:S(2)}) collective-permute-start(bf16[48,768]{1,0:T(8,128)(2,1)S(1)} %get-tuple-element.17.own_ref), channel_id=1, source_target_pairs={{0,2},{1,3},{2,0},{3,1},{4,6},{5,7},{6,4},{7,5},{8,10},{9,11},{10,... | collective-permute-start | bytes 221192 | tf_op jit(solution)/shard_map/ppermute | solution.py:180
  4.8 7.0 %collective-permute-start = (bf16[48,768]{1,0:T(8,128)(2,1)S(1)}, bf16[48,768]{1,0:T(8,128)(2,1)S(1)}, u32[]{:S(2)}, u32[]{:S(2)}) collective-permute-start(bf16[48,768]{1,0:T(8,128)(2,1)S(1)} %get-tuple-element.17.own_ref), channel_id=1, source_target_pairs={{0,12},{1,13},{2,14},{3,15},{4,8},{5,9},{6,10},{7,11},{8,4},{9,5},... | collective-permute-start | bytes 221192 | tf_op jit(solution)/shard_map/ppermute | solution.py:180
  8.4 4.4 %collective-permute-start.1 = (bf16[48,768]{1,0:T(8,128)(2,1)S(1)}, bf16[48,768]{1,0:T(8,128)(2,1)S(1)}, u32[]{:S(2)}, u32[]{:S(2)}) collective-permute-start(bf16[48,768]{1,0:T(8,128)(2,1)S(1)} %get-tuple-element.17.own_ref), channel_id=1, source_target_pairs={{0,8},{1,9},{2,10},{3,11},{4,0},{5,1},{6,2},{7,3},{8,12},{9,13},{1... | collective-permute-start | bytes 221192 | tf_op jit(solution)/shard_map/ppermute | solution.py:186
  8.4 4.4 %collective-permute-start.3 = (bf16[96,768]{1,0:T(8,128)(2,1)S(1)}, bf16[96,768]{1,0:T(8,128)(2,1)S(1)}, u32[]{:S(2)}, u32[]{:S(2)}) collective-permute-start(bf16[96,768]{1,0:T(8,128)(2,1)S(1)} %pad_maximum_fusion), channel_id=1, source_target_pairs={{0,1},{1,0},{2,3},{3,2},{4,5},{5,4},{6,7},{7,6},{8,9},{9,8},{10,11... | collective-permute-start | bytes 442376 | tf_op jit(solution)/shard_map/ppermute | solution.py:180
  12.8 1.6 %collective-permute-start.4 = (bf16[96,768]{1,0:T(8,128)(2,1)S(1)}, bf16[96,768]{1,0:T(8,128)(2,1)S(1)}, u32[]{:S(2)}, u32[]{:S(2)}) collective-permute-start(bf16[96,768]{1,0:T(8,128)(2,1)S(1)} %pad_maximum_fusion.1), channel_id=1, source_target_pairs={{0,1},{1,0},{2,3},{3,2},{4,5},{5,4},{6,7},{7,6},{8,9},{9,8},{10,11... | collective-permute-start | bytes 442376 | tf_op jit(solution)/shard_map/ppermute | solution.py:180
  13.3 5.7 %collective-permute-start.5 = (bf16[304,128]{1,0:T(8,128)(2,1)S(1)}, bf16[304,128]{1,0:T(8,128)(2,1)S(1)}, u32[]{:S(2)}, u32[]{:S(2)}) collective-permute-start(bf16[304,128]{1,0:T(8,128)(2,1)S(1)} %get-tuple-element.24), channel_id=1, source_target_pairs={{8,0},{9,1},{10,2},{11,3},{0,4},{1,5},{2,6},{3,7},{12,8},{13,9},{1... | collective-permute-start | bytes 233480 | tf_op jit(solution)/shard_map/ppermute | solution.py:186
  14.8 4.5 %collective-permute-start.6 = (bf16[304,128]{1,0:T(8,128)(2,1)S(1)}, bf16[304,128]{1,0:T(8,128)(2,1)S(1)}, u32[]{:S(2)}, u32[]{:S(2)}) collective-permute-start(bf16[304,128]{1,0:T(8,128)(2,1)S(1)} %beside.1), channel_id=1, source_target_pairs={{0,2},{1,3},{2,0},{3,1},{4,6},{5,7},{6,4},{7,5},{8,10},{9,11},{10,... | collective-permute-start | bytes 233480 | tf_op jit(solution)/shard_map/ppermute | solution.py:180

commit v7 on v2

--- a/solution.py
+++ b/solution.py
@@ -37,14 +37,22 @@
 
 
 LANES = 128
+PART = 16
+
+
+def row_parts(count):
+    return [pl.ds(start, PART) for start in range(0, count, PART)]
 
 
 def arrange_kernel(ids_hbm, rows_hbm, out_ref, moves_ref, ids_out_ref, ids_ref, rows_ref, sems):
+    count = rows_ref.shape[0]
     ids_copy = pltpu.make_async_copy(ids_hbm, ids_ref, sems.at[0])
-    rows_copy = pltpu.make_async_copy(rows_hbm, rows_ref, sems.at[1])
-    ids_copy.start()
-    rows_copy.start()
-    count = rows_ref.shape[0]
+    rows_copies = [
+        pltpu.make_async_copy(rows_hbm.at[part], rows_ref.at[part], sems.at[index + 1])
+        for index, part in enumerate(row_parts(count))
+    ]
+    for copy in (ids_copy, *rows_copies):
+        copy.start()
     ids_copy.wait()
     ids_row = ids_ref[...].reshape(1, count)
     ids_column = as_column(ids_row)
@@ -53,8 +61,11 @@
     before = (ids_column < ids_row) | ((ids_column == ids_row) & (down < across))
     rank_row = jnp.sum(before.astype(jnp.int32), axis=0, keepdims=True)
     moves = (down == rank_row).astype(jnp.bfloat16)
-    rows_copy.wait()
-    unit = normalize_rows(rows_ref[...])
+    unit = []
+    for copy, part in zip(rows_copies, row_parts(count)):
+        copy.wait()
+        unit.append(normalize_rows(rows_ref[part, :]))
+    unit = jnp.concatenate(unit, axis=0)
     out_ref[...] = jnp.dot(moves, unit, preferred_element_type=jnp.float32).astype(jnp.bfloat16)
     moves_ref[...] = moves
     ids_out_ref[...] = ids_row
@@ -139,23 +150,20 @@
         weighted * lax.rsqrt(jnp.mean(weighted * weighted, axis=-1, keepdims=True) + epsilon)
     ).astype(jnp.bfloat16)
     moves = moves_ref[...]
-    copies = []
-    for half in range(2):
-        part = slice(half * features // 2, (half + 1) * features // 2)
-        neighbour_ref[:, part] = lax.dot_general(
-            moves, normed[:, part], (((0,), (0,)), ((), ())), preferred_element_type=jnp.float32
-        ).astype(jnp.bfloat16)
-        copies.append(
-            pltpu.make_async_copy(
-                neighbour_ref.at[:, part], neighbour_hbm.at[:, part], sems.at[half]
-            )
-        )
-        copies[-1].start()
+    neighbour_ref[...] = lax.dot_general(
+        moves, normed, (((0,), (0,)), ((), ())), preferred_element_type=jnp.float32
+    ).astype(jnp.bfloat16)
+    copies = [
+        pltpu.make_async_copy(neighbour_ref.at[part], neighbour_hbm.at[part], sems.at[index])
+        for index, part in enumerate(row_parts(count))
+    ]
+    for copy in copies:
+        copy.start()
     pair = back_ref[columns * count :, :].astype(jnp.float32)
     totals = totals_ref[...] + (pair[0:1, :count] + pair[1:2, :count])
     scores = jnp.sum(moves.astype(jnp.float32) * as_column(jnp.log(totals)), axis=0, keepdims=True)
     score_ref[...] = scores.astype(jnp.bfloat16).reshape(count)
-    copies.append(pltpu.make_async_copy(score_ref, score_hbm, sems.at[2]))
+    copies.append(pltpu.make_async_copy(score_ref, score_hbm, sems.at[len(copies)]))
     copies[-1].start()
     for copy in copies:
         copy.wait()
@@ -199,7 +207,7 @@
         scratch=(
             pltpu.VMEM((rows_dev,), jnp.int32),
             pltpu.VMEM((rows_dev, features), jnp.bfloat16),
-            pltpu.SemaphoreType.DMA((2,)),
+            pltpu.SemaphoreType.DMA((1 + rows_dev // PART,)),
         ),
     )
 
@@ -241,7 +249,7 @@
             scratch=(
                 pltpu.VMEM((rows_dev, features), jnp.bfloat16),
                 pltpu.VMEM((rows_dev,), jnp.bfloat16),
-                pltpu.SemaphoreType.DMA((3,)),
+                pltpu.SemaphoreType.DMA((1 + rows_dev // PART,)),
             ),
         )
     )
@@ -329,7 +337,7 @@
 
     def body(embeddings, cluster_id):
         gathered = embeddings.size * embeddings.dtype.itemsize * devices
-        fits = gathered <= GATHER_LIMIT and devices == GRID
+        fits = gathered <= GATHER_LIMIT and devices == GRID and embeddings.shape[0] % PART == 0
         plan = gathered_body if fits else collected_body
         return plan(embeddings, cluster_id)
 

time: 20 us -> 20.1 us (level)
  no operation moved by 1% of the time
where the time goes in v7:
time: 20.1 us; the launch traced here: 20 us
  starting transfers between devices  9.01 us (45%)
  waiting for transfers between devices  6.86 us (34%)
  Pallas kernels  3.4 us (17%)
  between operations  0.66 us (3%)
    ppermute x7, starting transfers between devices, swap(): lax.ppermute(value, 'blk', [(device, device ^ bits) for device in range(G...  9.01 us
    ppermute x7, waiting for transfers between devices, swap(): lax.ppermute(value, 'blk', [(device, device ^ bits) for device in range(G...  6.86 us
    pallas_call x5, Pallas kernels, kernel(): pl.pallas_call(body, out_shape=out_shape, in_specs=[specs] * len(inputs),...  3.4 us
  transfers between devices with their start and end apart: 7, of which 5 were waited for; matrix products, arithmetic and copies ran while one was open for 0% of the time, Pallas kernels for 4%

profile of v7, /device:TPU:0, one launch (start us, length us, event | category | flops | bytes accessed | tf_op | source)
XLA Modules:
  0.0 20.0 jit_solution(15749228025435223829)
XLA Ops:
  0.6 1.2 %arrange.1 = (bf16[48,768]{1,0:T(8,128)(2,1)S(1)}, bf16[48,48]{1,0:T(8,128)(2,1)S(1)}, s32[1,48]{1,0:T(1,128)S(1)}) custom-call(s32[48]{0:T(128)} %ids_hbm.1, bf16[48,768]{1,0:T(8,128)(2,1)} %rows_hbm.1), custom_call_target="tpu_custom_call" | custom-call | tf_op jit(solution)/shard_map/arrange/pallas_call | solution.py:189
  1.9 4.1 %collective-permute-start = (bf16[48,768]{1,0:T(8,128)(2,1)S(1)}, bf16[48,768]{1,0:T(8,128)(2,1)S(1)}, u32[]{:S(2)}, u32[]{:S(2)}) collective-permute-start(bf16[48,768]{1,0:T(8,128)(2,1)S(1)} %get-tuple-element.17.own_ref.refs_0_), channel_id=1, source_target_pairs={{0,8},{1,9},{2,10},{3,11},{4,12},{5,13},{6,14},{7,15},{8,0},{9,1},... | collective-permute-start | bytes 221192 | tf_op jit(solution)/shard_map/ppermute | solution.py:183
  6.0 1.3 %collective-permute-start.1 = (bf16[48,768]{1,0:T(8,128)(2,1)S(1)}, bf16[48,768]{1,0:T(8,128)(2,1)S(1)}, u32[]{:S(2)}, u32[]{:S(2)}) collective-permute-start(bf16[48,768]{1,0:T(8,128)(2,1)S(1)} %get-tuple-element.17.own_ref.refs_0_), channel_id=1, source_target_pairs={{0,12},{1,13},{2,14},{3,15},{4,8},{5,9},{6,10},{7,11},{8,4},{9,5},... | collective-permute-start | bytes 221192 | tf_op jit(solution)/shard_map/ppermute | solution.py:183
  7.3 0.2 %collective-permute-start.2 = (bf16[48,768]{1,0:T(8,128)(2,1)S(1)}, bf16[48,768]{1,0:T(8,128)(2,1)S(1)}, u32[]{:S(2)}, u32[]{:S(2)}) collective-permute-start(bf16[48,768]{1,0:T(8,128)(2,1)S(1)} %get-tuple-element.17.own_ref.refs_0_), channel_id=1, source_target_pairs={{0,4},{1,5},{2,6},{3,7},{4,0},{5,1},{6,2},{7,3},{8,12},{9,13},{10,... | collective-permute-start | bytes 221192 | tf_op jit(solution)/shard_map/ppermute | solution.py:183
  7.6 1.5 %collective-permute-start.3 = (bf16[48,768]{1,0:T(8,128)(2,1)S(1)}, bf16[48,768]{1,0:T(8,128)(2,1)S(1)}, u32[]{:S(2)}, u32[]{:S(2)}) collective-permute-start(bf16[48,768]{1,0:T(8,128)(2,1)S(1)} %get-tuple-element.17.own_ref.refs_0_), channel_id=1, source_target_pairs={{0,2},{1,3},{2,0},{3,1},{4,6},{5,7},{6,4},{7,5},{8,10},{9,11},{10,... | collective-permute-start | bytes 221192 | tf_op jit(solution)/shard_map/ppermute | solution.py:183
  9.0 0.0 collective-permute-start.4
  9.0 1.8 %collective-permute-done.refs_3_ = bf16[48,768]{1,0:T(8,128)(2,1)S(1)} collective-permute-done((bf16[48,768]{1,0:T(8,128)(2,1)S(1)}, bf16[48,768]{1,0:T(8,128)(2,1)S(1)}, u32[]{:S(2)}, u32[]{:S(2)}) %collective-permute-start) | collective-permute-done | bytes 73760 | tf_op jit(solution)/shard_map/ppermute | solution.py:183
  10.8 1.6 %collective-permute-done.1.refs_4_ = bf16[48,768]{1,0:T(8,128)(2,1)S(1)} collective-permute-done((bf16[48,768]{1,0:T(8,128)(2,1)S(1)}, bf16[48,768]{1,0:T(8,128)(2,1)S(1)}, u32[]{:S(2)}, u32[]{:S(2)}) %collective-permute-start.1) | collective-permute-done | bytes 73760 | tf_op jit(solution)/shard_map/ppermute | solution.py:183
  12.4 0.2 collective-permute-done.2.refs_2_
  12.6 0.0 collective-permute-done.3.beside_ref
  12.6 0.0 collective-permute-done.4.refs_1_
  12.6 0.1 collective-permute-start.5
  12.7 0.5 %first.1 = (f32[96,768]{1,0:T(8,128)S(1)}, f32[96,128]{1,0:T(8,128)S(1)}, s32[48,128]{1,0:T(8,128)S(1)}) custom-call(bf16[48,48]{1,0:T(8,128)(2,1)S(1)} %get-tuple-element.15.moves_ref, s32[1,48]{1,0:T(1,128)S(1)} %get-tuple-element.16.ids_ref, bf16[48,768]{1,0:T(8,128)(2,1)S(1)} %get-tuple-element.17.own_ref.refs_0_, ...), custom_call_target="tpu_custom_call" | custom-call | tf_op jit(solution)/shard_map/first/pallas_call | solution.py:189
  13.2 1.0 %collective-permute-done.5.keys_ref = bf16[144,768]{1,0:T(8,128)(2,1)S(1)} collective-permute-done((bf16[144,768]{1,0:T(8,128)(2,1)S(1)}, bf16[144,768]{1,0:T(8,128)(2,1)S(1)}, u32[]{:S(2)}, u32[]{:S(2)}) %collective-permute-start.5) | collective-permute-done | bytes 221216 | tf_op jit(solution)/shard_map/ppermute | solution.py:183
  14.2 0.4 %beside.1 = bf16[304,128]{1,0:T(8,128)(2,1)S(1)} custom-call(f32[96,768]{1,0:T(8,128)S(1)} %get-tuple-element.23.so_far_ref, f32[96,128]{1,0:T(8,128)S(1)} %get-tuple-element.24.totals_so_far_ref, s32[48,128]{1,0:T(8,128)S(1)} %get-tuple-element.25.bounds_ref, bf16[48,768]{1,0:T(8,128)(2,1)S(1)} %collective-permute-done.3.beside_ref, ...), custom_call_target="tpu_custom_call" | custom-call | tf_op jit(solution)/shard_map/beside/pallas_call | solution.py:189
  14.6 1.8 %collective-permute-start.6 = (bf16[304,128]{1,0:T(8,128)(2,1)S(1)}, bf16[304,128]{1,0:T(8,128)(2,1)S(1)}, u32[]{:S(2)}, u32[]{:S(2)}) collective-permute-start(bf16[304,128]{1,0:T(8,128)(2,1)S(1)} %beside.1), channel_id=1, source_target_pairs={{0,2},{1,3},{2,0},{3,1},{4,6},{5,7},{6,4},{7,5},{8,10},{9,11},{10,... | collective-permute-start | bytes 233480 | tf_op jit(solution)/shard_map/ppermute | solution.py:183
  16.3 0.4 %own.1 = (f32[48,768]{1,0:T(8,128)S(1)}, f32[1,48]{1,0:T(1,128)S(1)}) custom-call(f32[96,768]{1,0:T(8,128)S(1)} %get-tuple-element.23.so_far_ref, f32[96,128]{1,0:T(8,128)S(1)} %get-tuple-element.24.totals_so_far_ref, s32[48,128]{1,0:T(8,128)S(1)} %get-tuple-element.25.bounds_ref, bf16[48,768]{1,0:T(8,128)(2,1)S(1)} %get-tuple-element.17.own_ref.refs_0_, ...), custom_call_target="tpu_custom_call" | custom-call | tf_op jit(solution)/shard_map/own/pallas_call | solution.py:189
  16.7 2.3 %collective-permute-done.6.back_ref = bf16[304,128]{1,0:T(8,128)(2,1)S(1)} collective-permute-done((bf16[304,128]{1,0:T(8,128)(2,1)S(1)}, bf16[304,128]{1,0:T(8,128)(2,1)S(1)}, u32[]{:S(2)}, u32[]{:S(2)}) %collective-permute-start.6) | collective-permute-done | bytes 77856 | tf_op jit(solution)/shard_map/ppermute | solution.py:183
  19.0 0.9 %finish.1 = (bf16[48,768]{1,0:T(8,128)(2,1)}, bf16[48]{0:T(256)(128)(2,1)}) custom-call(bf16[48,48]{1,0:T(8,128)(2,1)S(1)} %get-tuple-element.15.moves_ref, f32[48,768]{1,0:T(8,128)S(1)} %get-tuple-element.26.weighted_ref, f32[1,48]{1,0:T(1,128)S(1)} %get-tuple-element.27.totals_ref, bf16[304,128]{1,0:T(8,128)(2,1)S(1)} %collective-permute-done.6.back_ref), custom_call_target="tpu_custom_call" | custom-call | tf_op jit(solution)/shard_map/finish/pallas_call | solution.py:189
  (1 shorter events, 0.0 us)
Async XLA Ops:
  1.9 9.0 %collective-permute-start = (bf16[48,768]{1,0:T(8,128)(2,1)S(1)}, bf16[48,768]{1,0:T(8,128)(2,1)S(1)}, u32[]{:S(2)}, u32[]{:S(2)}) collective-permute-start(bf16[48,768]{1,0:T(8,128)(2,1)S(1)} %get-tuple-element.17.own_ref.refs_0_), channel_id=1, source_target_pairs={{0,8},{1,9},{2,10},{3,11},{4,12},{5,13},{6,14},{7,15},{8,0},{9,1},... | collective-permute-start | bytes 221192 | tf_op jit(solution)/shard_map/ppermute | solution.py:183
  6.0 6.5 %collective-permute-start.1 = (bf16[48,768]{1,0:T(8,128)(2,1)S(1)}, bf16[48,768]{1,0:T(8,128)(2,1)S(1)}, u32[]{:S(2)}, u32[]{:S(2)}) collective-permute-start(bf16[48,768]{1,0:T(8,128)(2,1)S(1)} %get-tuple-element.17.own_ref.refs_0_), channel_id=1, source_target_pairs={{0,12},{1,13},{2,14},{3,15},{4,8},{5,9},{6,10},{7,11},{8,4},{9,5},... | collective-permute-start | bytes 221192 | tf_op jit(solution)/shard_map/ppermute | solution.py:183
  7.3 5.3 %collective-permute-start.2 = (bf16[48,768]{1,0:T(8,128)(2,1)S(1)}, bf16[48,768]{1,0:T(8,128)(2,1)S(1)}, u32[]{:S(2)}, u32[]{:S(2)}) collective-permute-start(bf16[48,768]{1,0:T(8,128)(2,1)S(1)} %get-tuple-element.17.own_ref.refs_0_), channel_id=1, source_target_pairs={{0,4},{1,5},{2,6},{3,7},{4,0},{5,1},{6,2},{7,3},{8,12},{9,13},{10,... | collective-permute-start | bytes 221192 | tf_op jit(solution)/shard_map/ppermute | solution.py:183
  7.6 5.1 %collective-permute-start.3 = (bf16[48,768]{1,0:T(8,128)(2,1)S(1)}, bf16[48,768]{1,0:T(8,128)(2,1)S(1)}, u32[]{:S(2)}, u32[]{:S(2)}) collective-permute-start(bf16[48,768]{1,0:T(8,128)(2,1)S(1)} %get-tuple-element.17.own_ref.refs_0_), channel_id=1, source_target_pairs={{0,2},{1,3},{2,0},{3,1},{4,6},{5,7},{6,4},{7,5},{8,10},{9,11},{10,... | collective-permute-start | bytes 221192 | tf_op jit(solution)/shard_map/ppermute | solution.py:183
  9.0 3.6 %collective-permute-start.4 = (bf16[48,768]{1,0:T(8,128)(2,1)S(1)}, bf16[48,768]{1,0:T(8,128)(2,1)S(1)}, u32[]{:S(2)}, u32[]{:S(2)}) collective-permute-start(bf16[48,768]{1,0:T(8,128)(2,1)S(1)} %get-tuple-element.17.own_ref.refs_0_), channel_id=1, source_target_pairs={{0,1},{1,0},{2,3},{3,2},{4,5},{5,4},{6,7},{7,6},{8,9},{9,8},{10,11... | collective-permute-start | bytes 221192 | tf_op jit(solution)/shard_map/ppermute | solution.py:183
  12.6 1.5 %collective-permute-start.5 = (bf16[144,768]{1,0:T(8,128)(2,1)S(1)}, bf16[144,768]{1,0:T(8,128)(2,1)S(1)}, u32[]{:S(2)}, u32[]{:S(2)}) collective-permute-start(bf16[144,768]{1,0:T(8,128)(2,1)S(1)} %pad_maximum_fusion), channel_id=1, source_target_pairs={{0,1},{1,0},{2,3},{3,2},{4,5},{5,4},{6,7},{7,6},{8,9},{9,8},{10,11... | collective-permute-start | bytes 663560 | tf_op jit(solution)/shard_map/ppermute | solution.py:183
  14.6 4.5 %collective-permute-start.6 = (bf16[304,128]{1,0:T(8,128)(2,1)S(1)}, bf16[304,128]{1,0:T(8,128)(2,1)S(1)}, u32[]{:S(2)}, u32[]{:S(2)}) collective-permute-start(bf16[304,128]{1,0:T(8,128)(2,1)S(1)} %beside.1), channel_id=1, source_target_pairs={{0,2},{1,3},{2,0},{3,1},{4,6},{5,7},{6,4},{7,5},{8,10},{9,11},{10,... | collective-permute-start | bytes 233480 | tf_op jit(solution)/shard_map/ppermute | solution.py:183

commit v8 on v2

--- a/solution.py
+++ b/solution.py
@@ -164,6 +164,7 @@
 EXTRA = 16
 CORE, ACROSS, NEAR, FAR = 1, 2, 4, 8
 GRID = 16
+Z_TURNS = ((FAR, FAR | NEAR, NEAR), (FAR | NEAR, NEAR, FAR))
 
 
 def gathered_body(embeddings, cluster_id):
@@ -172,7 +173,8 @@
     stored = pl.BlockSpec(memory_space=pltpu.HBM)
 
     def swap(value, bits):
-        return lax.ppermute(value, "blk", [(device, device ^ bits) for device in range(GRID)])
+        pairs = [(device, device ^ bits[device & CORE]) for device in range(GRID)]
+        return lax.ppermute(value, "blk", pairs)
 
     def block(kind, *shape):
         return jax.ShapeDtypeStruct(shape, kind)
@@ -203,10 +205,10 @@
         ),
     )
 
-    far, farther, near, beside, mate = lax.optimization_barrier(
-        tuple(swap(own, bits) for bits in (FAR, FAR | NEAR, NEAR, ACROSS, CORE))
-    )
-    mates = swap(jnp.concatenate([near, far, farther], axis=0), CORE)
+    *visiting, beside, mate = lax.optimization_barrier(
+        (*(swap(own, turn) for turn in zip(*Z_TURNS)), swap(own, (ACROSS,) * 2), swap(own, (CORE,) * 2))
+    )
+    mates = swap(jnp.concatenate(visiting, axis=0), (CORE,) * 2)
     *so_far, bounds = kernel(
         first_kernel,
         "first",
@@ -216,7 +218,7 @@
             block(jnp.int32, rows_dev, LANES),
         ),
         *(moves, ids, own, beside),
-        *(own, mate, near, far, farther),
+        *(own, mate, *visiting),
     )
     (partial,) = kernel(
         beside_kernel,
@@ -224,7 +226,7 @@
         (block(jnp.bfloat16, rows_dev * features // LANES + EXTRA, LANES),),
         *(*so_far, bounds, beside, mates),
     )
-    back = swap(partial, ACROSS)
+    back = swap(partial, (ACROSS,) * 2)
     weighted, totals = kernel(
         own_kernel,
         "own",
@@ -329,7 +331,7 @@
 
     def body(embeddings, cluster_id):
         gathered = embeddings.size * embeddings.dtype.itemsize * devices
-        fits = gathered <= GATHER_LIMIT and devices == GRID
+        fits = gathered <= GATHER_LIMIT and devices == GRID and embeddings.shape[0] % 16 == 0
         plan = gathered_body if fits else collected_body
         return plan(embeddings, cluster_id)
 

time: 20 us -> 20.3 us (1.015)
  waiting for transfers between devices: 6.86 us -> 7.36 us
  starting transfers between devices: 9.01 us -> 8.8 us
    ppermute x7, waiting for transfers between devices: 6.86 us -> 7.36 us  [swap(): return lax.ppermute(value, 'blk', pairs)]
    ppermute x7, starting transfers between devices: 9.01 us -> 8.8 us  [swap(): return lax.ppermute(value, 'blk', pairs)]
  transfers between devices with their start and end apart: 7 -> 7, of which waited for: 5 -> 4; matrix products, arithmetic and copies ran while one was open for 0% -> 0% of each run, Pallas kernels for 4% -> 4%
where the time goes in v8:
time: 20.3 us; the launch traced here: 20.2 us
  starting transfers between devices  8.8 us (43%)
  waiting for transfers between devices  7.36 us (36%)
  Pallas kernels  3.33 us (16%)
  between operations  0.67 us (3%)
    ppermute x7, starting transfers between devices, swap(): return lax.ppermute(value, 'blk', pairs)  8.8 us
    ppermute x7, waiting for transfers between devices, swap(): return lax.ppermute(value, 'blk', pairs)  7.36 us
    pallas_call x5, Pallas kernels, kernel(): pl.pallas_call(body, out_shape=out_shape, in_specs=[specs] * len(inputs),...  3.33 us
  transfers between devices with their start and end apart: 7, of which 4 were waited for; matrix products, arithmetic and copies ran while one was open for 0% of the time, Pallas kernels for 4%

profile of v8, /device:TPU:0, one launch (start us, length us, event | category | flops | bytes accessed | tf_op | source)
XLA Modules:
  0.0 20.2 jit_solution(4982005517848442911)
XLA Ops:
  0.6 1.2 %arrange.1 = (bf16[48,768]{1,0:T(8,128)(2,1)S(1)}, bf16[48,48]{1,0:T(8,128)(2,1)S(1)}, s32[1,48]{1,0:T(1,128)S(1)}) custom-call(s32[48]{0:T(128)} %ids_hbm.1, bf16[48,768]{1,0:T(8,128)(2,1)} %rows_hbm.1), custom_call_target="tpu_custom_call" | custom-call | tf_op jit(solution)/shard_map/arrange/pallas_call | solution.py:183
  1.8 4.1 %collective-permute-start = (bf16[48,768]{1,0:T(8,128)(2,1)S(1)}, bf16[48,768]{1,0:T(8,128)(2,1)S(1)}, u32[]{:S(2)}, u32[]{:S(2)}) collective-permute-start(bf16[48,768]{1,0:T(8,128)(2,1)S(1)} %get-tuple-element.17.own_ref.refs_0_), channel_id=1, source_target_pairs={{0,8},{1,13},{2,10},{3,15},{4,12},{5,9},{6,14},{7,11},{8,0},{9,5},... | collective-permute-start | bytes 221192 | tf_op jit(solution)/shard_map/ppermute | solution.py:177
  5.9 1.3 %collective-permute-start.1 = (bf16[48,768]{1,0:T(8,128)(2,1)S(1)}, bf16[48,768]{1,0:T(8,128)(2,1)S(1)}, u32[]{:S(2)}, u32[]{:S(2)}) collective-permute-start(bf16[48,768]{1,0:T(8,128)(2,1)S(1)} %get-tuple-element.17.own_ref.refs_0_), channel_id=1, source_target_pairs={{0,12},{1,5},{2,14},{3,7},{4,8},{5,1},{6,10},{7,3},{8,4},{9,13},{1... | collective-permute-start | bytes 221192 | tf_op jit(solution)/shard_map/ppermute | solution.py:177
  7.3 0.2 %collective-permute-start.2 = (bf16[48,768]{1,0:T(8,128)(2,1)S(1)}, bf16[48,768]{1,0:T(8,128)(2,1)S(1)}, u32[]{:S(2)}, u32[]{:S(2)}) collective-permute-start(bf16[48,768]{1,0:T(8,128)(2,1)S(1)} %get-tuple-element.17.own_ref.refs_0_), channel_id=1, source_target_pairs={{0,4},{1,9},{2,6},{3,11},{4,0},{5,13},{6,2},{7,15},{8,12},{9,1},{1... | collective-permute-start | bytes 221192 | tf_op jit(solution)/shard_map/ppermute | solution.py:177
  7.5 1.5 %collective-permute-start.3 = (bf16[48,768]{1,0:T(8,128)(2,1)S(1)}, bf16[48,768]{1,0:T(8,128)(2,1)S(1)}, u32[]{:S(2)}, u32[]{:S(2)}) collective-permute-start(bf16[48,768]{1,0:T(8,128)(2,1)S(1)} %get-tuple-element.17.own_ref.refs_0_), channel_id=1, source_target_pairs={{0,2},{1,3},{2,0},{3,1},{4,6},{5,7},{6,4},{7,5},{8,10},{9,11},{10,... | collective-permute-start | bytes 221192 | tf_op jit(solution)/shard_map/ppermute | solution.py:177
  9.0 0.0 collective-permute-start.4
  9.0 0.5 %collective-permute-done.refs_2_ = bf16[48,768]{1,0:T(8,128)(2,1)S(1)} collective-permute-done((bf16[48,768]{1,0:T(8,128)(2,1)S(1)}, bf16[48,768]{1,0:T(8,128)(2,1)S(1)}, u32[]{:S(2)}, u32[]{:S(2)}) %collective-permute-start) | collective-permute-done | bytes 73760 | tf_op jit(solution)/shard_map/ppermute | solution.py:177
  9.4 3.4 %collective-permute-done.1.refs_3_ = bf16[48,768]{1,0:T(8,128)(2,1)S(1)} collective-permute-done((bf16[48,768]{1,0:T(8,128)(2,1)S(1)}, bf16[48,768]{1,0:T(8,128)(2,1)S(1)}, u32[]{:S(2)}, u32[]{:S(2)}) %collective-permute-start.1) | collective-permute-done | bytes 73760 | tf_op jit(solution)/shard_map/ppermute | solution.py:177
  12.8 0.0 collective-permute-done.2.refs_4_
  12.8 0.0 collective-permute-done.3.beside_ref
  12.8 0.0 collective-permute-done.4.refs_1_
  12.9 0.1 collective-permute-start.5
  12.9 0.5 %first.1 = (f32[96,768]{1,0:T(8,128)S(1)}, f32[96,128]{1,0:T(8,128)S(1)}, s32[48,128]{1,0:T(8,128)S(1)}) custom-call(bf16[48,48]{1,0:T(8,128)(2,1)S(1)} %get-tuple-element.15.moves_ref, s32[1,48]{1,0:T(1,128)S(1)} %get-tuple-element.16.ids_ref, bf16[48,768]{1,0:T(8,128)(2,1)S(1)} %get-tuple-element.17.own_ref.refs_0_, ...), custom_call_target="tpu_custom_call" | custom-call | tf_op jit(solution)/shard_map/first/pallas_call | solution.py:183
  13.4 1.0 %collective-permute-done.5.keys_ref = bf16[144,768]{1,0:T(8,128)(2,1)S(1)} collective-permute-done((bf16[144,768]{1,0:T(8,128)(2,1)S(1)}, bf16[144,768]{1,0:T(8,128)(2,1)S(1)}, u32[]{:S(2)}, u32[]{:S(2)}) %collective-permute-start.5) | collective-permute-done | bytes 221216 | tf_op jit(solution)/shard_map/ppermute | solution.py:177
  14.4 0.4 %beside.1 = bf16[304,128]{1,0:T(8,128)(2,1)S(1)} custom-call(f32[96,768]{1,0:T(8,128)S(1)} %get-tuple-element.23.so_far_ref, f32[96,128]{1,0:T(8,128)S(1)} %get-tuple-element.24.totals_so_far_ref, s32[48,128]{1,0:T(8,128)S(1)} %get-tuple-element.25.bounds_ref, bf16[48,768]{1,0:T(8,128)(2,1)S(1)} %collective-permute-done.3.beside_ref, ...), custom_call_target="tpu_custom_call" | custom-call | tf_op jit(solution)/shard_map/beside/pallas_call | solution.py:183
  14.8 1.6 %collective-permute-start.6 = (bf16[304,128]{1,0:T(8,128)(2,1)S(1)}, bf16[304,128]{1,0:T(8,128)(2,1)S(1)}, u32[]{:S(2)}, u32[]{:S(2)}) collective-permute-start(bf16[304,128]{1,0:T(8,128)(2,1)S(1)} %beside.1), channel_id=1, source_target_pairs={{0,2},{1,3},{2,0},{3,1},{4,6},{5,7},{6,4},{7,5},{8,10},{9,11},{10,... | collective-permute-start | bytes 233480 | tf_op jit(solution)/shard_map/ppermute | solution.py:177
  16.4 0.4 %own.1 = (f32[48,768]{1,0:T(8,128)S(1)}, f32[1,48]{1,0:T(1,128)S(1)}) custom-call(f32[96,768]{1,0:T(8,128)S(1)} %get-tuple-element.23.so_far_ref, f32[96,128]{1,0:T(8,128)S(1)} %get-tuple-element.24.totals_so_far_ref, s32[48,128]{1,0:T(8,128)S(1)} %get-tuple-element.25.bounds_ref, bf16[48,768]{1,0:T(8,128)(2,1)S(1)} %get-tuple-element.17.own_ref.refs_0_, ...), custom_call_target="tpu_custom_call" | custom-call | tf_op jit(solution)/shard_map/own/pallas_call | solution.py:183
  16.8 2.5 %collective-permute-done.6.back_ref = bf16[304,128]{1,0:T(8,128)(2,1)S(1)} collective-permute-done((bf16[304,128]{1,0:T(8,128)(2,1)S(1)}, bf16[304,128]{1,0:T(8,128)(2,1)S(1)}, u32[]{:S(2)}, u32[]{:S(2)}) %collective-permute-start.6) | collective-permute-done | bytes 77856 | tf_op jit(solution)/shard_map/ppermute | solution.py:177
  19.3 0.9 %finish.1 = (bf16[48,768]{1,0:T(8,128)(2,1)}, bf16[48]{0:T(256)(128)(2,1)}) custom-call(bf16[48,48]{1,0:T(8,128)(2,1)S(1)} %get-tuple-element.15.moves_ref, f32[48,768]{1,0:T(8,128)S(1)} %get-tuple-element.26.weighted_ref, f32[1,48]{1,0:T(1,128)S(1)} %get-tuple-element.27.totals_ref, bf16[304,128]{1,0:T(8,128)(2,1)S(1)} %collective-permute-done.6.back_ref), custom_call_target="tpu_custom_call" | custom-call | tf_op jit(solution)/shard_map/finish/pallas_call | solution.py:183
  (1 shorter events, 0.0 us)
Async XLA Ops:
  1.8 7.6 %collective-permute-start = (bf16[48,768]{1,0:T(8,128)(2,1)S(1)}, bf16[48,768]{1,0:T(8,128)(2,1)S(1)}, u32[]{:S(2)}, u32[]{:S(2)}) collective-permute-start(bf16[48,768]{1,0:T(8,128)(2,1)S(1)} %get-tuple-element.17.own_ref.refs_0_), channel_id=1, source_target_pairs={{0,8},{1,13},{2,10},{3,15},{4,12},{5,9},{6,14},{7,11},{8,0},{9,5},... | collective-permute-start | bytes 221192 | tf_op jit(solution)/shard_map/ppermute | solution.py:177
  5.9 6.9 %collective-permute-start.1 = (bf16[48,768]{1,0:T(8,128)(2,1)S(1)}, bf16[48,768]{1,0:T(8,128)(2,1)S(1)}, u32[]{:S(2)}, u32[]{:S(2)}) collective-permute-start(bf16[48,768]{1,0:T(8,128)(2,1)S(1)} %get-tuple-element.17.own_ref.refs_0_), channel_id=1, source_target_pairs={{0,12},{1,5},{2,14},{3,7},{4,8},{5,1},{6,10},{7,3},{8,4},{9,13},{1... | collective-permute-start | bytes 221192 | tf_op jit(solution)/shard_map/ppermute | solution.py:177
  7.3 5.6 %collective-permute-start.2 = (bf16[48,768]{1,0:T(8,128)(2,1)S(1)}, bf16[48,768]{1,0:T(8,128)(2,1)S(1)}, u32[]{:S(2)}, u32[]{:S(2)}) collective-permute-start(bf16[48,768]{1,0:T(8,128)(2,1)S(1)} %get-tuple-element.17.own_ref.refs_0_), channel_id=1, source_target_pairs={{0,4},{1,9},{2,6},{3,11},{4,0},{5,13},{6,2},{7,15},{8,12},{9,1},{1... | collective-permute-start | bytes 221192 | tf_op jit(solution)/shard_map/ppermute | solution.py:177
  7.5 5.4 %collective-permute-start.3 = (bf16[48,768]{1,0:T(8,128)(2,1)S(1)}, bf16[48,768]{1,0:T(8,128)(2,1)S(1)}, u32[]{:S(2)}, u32[]{:S(2)}) collective-permute-start(bf16[48,768]{1,0:T(8,128)(2,1)S(1)} %get-tuple-element.17.own_ref.refs_0_), channel_id=1, source_target_pairs={{0,2},{1,3},{2,0},{3,1},{4,6},{5,7},{6,4},{7,5},{8,10},{9,11},{10,... | collective-permute-start | bytes 221192 | tf_op jit(solution)/shard_map/ppermute | solution.py:177
  9.0 3.9 %collective-permute-start.4 = (bf16[48,768]{1,0:T(8,128)(2,1)S(1)}, bf16[48,768]{1,0:T(8,128)(2,1)S(1)}, u32[]{:S(2)}, u32[]{:S(2)}) collective-permute-start(bf16[48,768]{1,0:T(8,128)(2,1)S(1)} %get-tuple-element.17.own_ref.refs_0_), channel_id=1, source_target_pairs={{0,1},{1,0},{2,3},{3,2},{4,5},{5,4},{6,7},{7,6},{8,9},{9,8},{10,11... | collective-permute-start | bytes 221192 | tf_op jit(solution)/shard_map/ppermute | solution.py:177
  12.9 1.5 %collective-permute-start.5 = (bf16[144,768]{1,0:T(8,128)(2,1)S(1)}, bf16[144,768]{1,0:T(8,128)(2,1)S(1)}, u32[]{:S(2)}, u32[]{:S(2)}) collective-permute-start(bf16[144,768]{1,0:T(8,128)(2,1)S(1)} %pad_maximum_fusion), channel_id=1, source_target_pairs={{0,1},{1,0},{2,3},{3,2},{4,5},{5,4},{6,7},{7,6},{8,9},{9,8},{10,11... | collective-permute-start | bytes 663560 | tf_op jit(solution)/shard_map/ppermute | solution.py:177
  14.8 4.5 %collective-permute-start.6 = (bf16[304,128]{1,0:T(8,128)(2,1)S(1)}, bf16[304,128]{1,0:T(8,128)(2,1)S(1)}, u32[]{:S(2)}, u32[]{:S(2)}) collective-permute-start(bf16[304,128]{1,0:T(8,128)(2,1)S(1)} %beside.1), channel_id=1, source_target_pairs={{0,2},{1,3},{2,0},{3,1},{4,6},{5,7},{6,4},{7,5},{8,10},{9,11},{10,... | collective-permute-start | bytes 233480 | tf_op jit(solution)/shard_map/ppermute | solution.py:177

commit v9 on v2

--- a/solution.py
+++ b/solution.py
@@ -139,23 +139,16 @@
         weighted * lax.rsqrt(jnp.mean(weighted * weighted, axis=-1, keepdims=True) + epsilon)
     ).astype(jnp.bfloat16)
     moves = moves_ref[...]
-    copies = []
-    for half in range(2):
-        part = slice(half * features // 2, (half + 1) * features // 2)
-        neighbour_ref[:, part] = lax.dot_general(
-            moves, normed[:, part], (((0,), (0,)), ((), ())), preferred_element_type=jnp.float32
-        ).astype(jnp.bfloat16)
-        copies.append(
-            pltpu.make_async_copy(
-                neighbour_ref.at[:, part], neighbour_hbm.at[:, part], sems.at[half]
-            )
-        )
-        copies[-1].start()
+    neighbour_ref[...] = lax.dot_general(
+        moves, normed, (((0,), (0,)), ((), ())), preferred_element_type=jnp.float32
+    ).astype(jnp.bfloat16)
+    copies = [pltpu.make_async_copy(neighbour_ref, neighbour_hbm, sems.at[0])]
+    copies[0].start()
     pair = back_ref[columns * count :, :].astype(jnp.float32)
     totals = totals_ref[...] + (pair[0:1, :count] + pair[1:2, :count])
     scores = jnp.sum(moves.astype(jnp.float32) * as_column(jnp.log(totals)), axis=0, keepdims=True)
     score_ref[...] = scores.astype(jnp.bfloat16).reshape(count)
-    copies.append(pltpu.make_async_copy(score_ref, score_hbm, sems.at[2]))
+    copies.append(pltpu.make_async_copy(score_ref, score_hbm, sems.at[1]))
     copies[-1].start()
     for copy in copies:
         copy.wait()
@@ -241,7 +234,7 @@
             scratch=(
                 pltpu.VMEM((rows_dev, features), jnp.bfloat16),
                 pltpu.VMEM((rows_dev,), jnp.bfloat16),
-                pltpu.SemaphoreType.DMA((3,)),
+                pltpu.SemaphoreType.DMA((2,)),
             ),
         )
     )

time: 20 us -> 20 us (level)
  no operation moved by 1% of the time
where the time goes in v9:
time: 20 us; the launch traced here: 19.9 us
  starting transfers between devices  9.01 us (45%)
  waiting for transfers between devices  6.86 us (34%)
  Pallas kernels  3.33 us (17%)
  between operations  0.66 us (3%)
    ppermute x7, starting transfers between devices, swap(): lax.ppermute(value, 'blk', [(device, device ^ bits) for device in range(G...  9.01 us
    ppermute x7, waiting for transfers between devices, swap(): lax.ppermute(value, 'blk', [(device, device ^ bits) for device in range(G...  6.86 us
    pallas_call x5, Pallas kernels, kernel(): pl.pallas_call(body, out_shape=out_shape, in_specs=[specs] * len(inputs),...  3.33 us
  transfers between devices with their start and end apart: 7, of which 5 were waited for; matrix products, arithmetic and copies ran while one was open for 0% of the time, Pallas kernels for 4%

profile of v9, /device:TPU:0, one launch (start us, length us, event | category | flops | bytes accessed | tf_op | source)
XLA Modules:
  0.0 19.9 jit_solution(13516588056491519622)
XLA Ops:
  0.6 1.2 %arrange.1 = (bf16[48,768]{1,0:T(8,128)(2,1)S(1)}, bf16[48,48]{1,0:T(8,128)(2,1)S(1)}, s32[1,48]{1,0:T(1,128)S(1)}) custom-call(s32[48]{0:T(128)} %ids_hbm.1, bf16[48,768]{1,0:T(8,128)(2,1)} %rows_hbm.1), custom_call_target="tpu_custom_call" | custom-call | tf_op jit(solution)/shard_map/arrange/pallas_call | solution.py:174
  1.8 4.1 %collective-permute-start = (bf16[48,768]{1,0:T(8,128)(2,1)S(1)}, bf16[48,768]{1,0:T(8,128)(2,1)S(1)}, u32[]{:S(2)}, u32[]{:S(2)}) collective-permute-start(bf16[48,768]{1,0:T(8,128)(2,1)S(1)} %get-tuple-element.17.own_ref.refs_0_), channel_id=1, source_target_pairs={{0,8},{1,9},{2,10},{3,11},{4,12},{5,13},{6,14},{7,15},{8,0},{9,1},... | collective-permute-start | bytes 221192 | tf_op jit(solution)/shard_map/ppermute | solution.py:168
  5.9 1.3 %collective-permute-start.1 = (bf16[48,768]{1,0:T(8,128)(2,1)S(1)}, bf16[48,768]{1,0:T(8,128)(2,1)S(1)}, u32[]{:S(2)}, u32[]{:S(2)}) collective-permute-start(bf16[48,768]{1,0:T(8,128)(2,1)S(1)} %get-tuple-element.17.own_ref.refs_0_), channel_id=1, source_target_pairs={{0,12},{1,13},{2,14},{3,15},{4,8},{5,9},{6,10},{7,11},{8,4},{9,5},... | collective-permute-start | bytes 221192 | tf_op jit(solution)/shard_map/ppermute | solution.py:168
  7.3 0.2 %collective-permute-start.2 = (bf16[48,768]{1,0:T(8,128)(2,1)S(1)}, bf16[48,768]{1,0:T(8,128)(2,1)S(1)}, u32[]{:S(2)}, u32[]{:S(2)}) collective-permute-start(bf16[48,768]{1,0:T(8,128)(2,1)S(1)} %get-tuple-element.17.own_ref.refs_0_), channel_id=1, source_target_pairs={{0,4},{1,5},{2,6},{3,7},{4,0},{5,1},{6,2},{7,3},{8,12},{9,13},{10,... | collective-permute-start | bytes 221192 | tf_op jit(solution)/shard_map/ppermute | solution.py:168
  7.5 1.5 %collective-permute-start.3 = (bf16[48,768]{1,0:T(8,128)(2,1)S(1)}, bf16[48,768]{1,0:T(8,128)(2,1)S(1)}, u32[]{:S(2)}, u32[]{:S(2)}) collective-permute-start(bf16[48,768]{1,0:T(8,128)(2,1)S(1)} %get-tuple-element.17.own_ref.refs_0_), channel_id=1, source_target_pairs={{0,2},{1,3},{2,0},{3,1},{4,6},{5,7},{6,4},{7,5},{8,10},{9,11},{10,... | collective-permute-start | bytes 221192 | tf_op jit(solution)/shard_map/ppermute | solution.py:168
  9.0 0.0 collective-permute-start.4
  9.0 1.8 %collective-permute-done.refs_3_ = bf16[48,768]{1,0:T(8,128)(2,1)S(1)} collective-permute-done((bf16[48,768]{1,0:T(8,128)(2,1)S(1)}, bf16[48,768]{1,0:T(8,128)(2,1)S(1)}, u32[]{:S(2)}, u32[]{:S(2)}) %collective-permute-start) | collective-permute-done | bytes 73760 | tf_op jit(solution)/shard_map/ppermute | solution.py:168
  10.8 1.6 %collective-permute-done.1.refs_4_ = bf16[48,768]{1,0:T(8,128)(2,1)S(1)} collective-permute-done((bf16[48,768]{1,0:T(8,128)(2,1)S(1)}, bf16[48,768]{1,0:T(8,128)(2,1)S(1)}, u32[]{:S(2)}, u32[]{:S(2)}) %collective-permute-start.1) | collective-permute-done | bytes 73760 | tf_op jit(solution)/shard_map/ppermute | solution.py:168
  12.4 0.2 collective-permute-done.2.refs_2_
  12.5 0.0 collective-permute-done.3.beside_ref
  12.5 0.0 collective-permute-done.4.refs_1_
  12.6 0.1 collective-permute-start.5
  12.6 0.5 %first.1 = (f32[96,768]{1,0:T(8,128)S(1)}, f32[96,128]{1,0:T(8,128)S(1)}, s32[48,128]{1,0:T(8,128)S(1)}) custom-call(bf16[48,48]{1,0:T(8,128)(2,1)S(1)} %get-tuple-element.15.moves_ref, s32[1,48]{1,0:T(1,128)S(1)} %get-tuple-element.16.ids_ref, bf16[48,768]{1,0:T(8,128)(2,1)S(1)} %get-tuple-element.17.own_ref.refs_0_, ...), custom_call_target="tpu_custom_call" | custom-call | tf_op jit(solution)/shard_map/first/pallas_call | solution.py:174
  13.1 1.0 %collective-permute-done.5.keys_ref = bf16[144,768]{1,0:T(8,128)(2,1)S(1)} collective-permute-done((bf16[144,768]{1,0:T(8,128)(2,1)S(1)}, bf16[144,768]{1,0:T(8,128)(2,1)S(1)}, u32[]{:S(2)}, u32[]{:S(2)}) %collective-permute-start.5) | collective-permute-done | bytes 221216 | tf_op jit(solution)/shard_map/ppermute | solution.py:168
  14.1 0.4 %beside.1 = bf16[304,128]{1,0:T(8,128)(2,1)S(1)} custom-call(f32[96,768]{1,0:T(8,128)S(1)} %get-tuple-element.23.so_far_ref, f32[96,128]{1,0:T(8,128)S(1)} %get-tuple-element.24.totals_so_far_ref, s32[48,128]{1,0:T(8,128)S(1)} %get-tuple-element.25.bounds_ref, bf16[48,768]{1,0:T(8,128)(2,1)S(1)} %collective-permute-done.3.beside_ref, ...), custom_call_target="tpu_custom_call" | custom-call | tf_op jit(solution)/shard_map/beside/pallas_call | solution.py:174
  14.5 1.8 %collective-permute-start.6 = (bf16[304,128]{1,0:T(8,128)(2,1)S(1)}, bf16[304,128]{1,0:T(8,128)(2,1)S(1)}, u32[]{:S(2)}, u32[]{:S(2)}) collective-permute-start(bf16[304,128]{1,0:T(8,128)(2,1)S(1)} %beside.1), channel_id=1, source_target_pairs={{0,2},{1,3},{2,0},{3,1},{4,6},{5,7},{6,4},{7,5},{8,10},{9,11},{10,... | collective-permute-start | bytes 233480 | tf_op jit(solution)/shard_map/ppermute | solution.py:168
  16.3 0.4 %own.1 = (f32[48,768]{1,0:T(8,128)S(1)}, f32[1,48]{1,0:T(1,128)S(1)}) custom-call(f32[96,768]{1,0:T(8,128)S(1)} %get-tuple-element.23.so_far_ref, f32[96,128]{1,0:T(8,128)S(1)} %get-tuple-element.24.totals_so_far_ref, s32[48,128]{1,0:T(8,128)S(1)} %get-tuple-element.25.bounds_ref, bf16[48,768]{1,0:T(8,128)(2,1)S(1)} %get-tuple-element.17.own_ref.refs_0_, ...), custom_call_target="tpu_custom_call" | custom-call | tf_op jit(solution)/shard_map/own/pallas_call | solution.py:174
  16.7 2.3 %collective-permute-done.6.back_ref = bf16[304,128]{1,0:T(8,128)(2,1)S(1)} collective-permute-done((bf16[304,128]{1,0:T(8,128)(2,1)S(1)}, bf16[304,128]{1,0:T(8,128)(2,1)S(1)}, u32[]{:S(2)}, u32[]{:S(2)}) %collective-permute-start.6) | collective-permute-done | bytes 77856 | tf_op jit(solution)/shard_map/ppermute | solution.py:168
  19.0 0.9 %finish.1 = (bf16[48,768]{1,0:T(8,128)(2,1)}, bf16[48]{0:T(256)(128)(2,1)}) custom-call(bf16[48,48]{1,0:T(8,128)(2,1)S(1)} %get-tuple-element.15.moves_ref, f32[48,768]{1,0:T(8,128)S(1)} %get-tuple-element.26.weighted_ref, f32[1,48]{1,0:T(1,128)S(1)} %get-tuple-element.27.totals_ref, bf16[304,128]{1,0:T(8,128)(2,1)S(1)} %collective-permute-done.6.back_ref), custom_call_target="tpu_custom_call" | custom-call | tf_op jit(solution)/shard_map/finish/pallas_call | solution.py:174
  (1 shorter events, 0.0 us)
Async XLA Ops:
  1.8 9.0 %collective-permute-start = (bf16[48,768]{1,0:T(8,128)(2,1)S(1)}, bf16[48,768]{1,0:T(8,128)(2,1)S(1)}, u32[]{:S(2)}, u32[]{:S(2)}) collective-permute-start(bf16[48,768]{1,0:T(8,128)(2,1)S(1)} %get-tuple-element.17.own_ref.refs_0_), channel_id=1, source_target_pairs={{0,8},{1,9},{2,10},{3,11},{4,12},{5,13},{6,14},{7,15},{8,0},{9,1},... | collective-permute-start | bytes 221192 | tf_op jit(solution)/shard_map/ppermute | solution.py:168
  5.9 6.5 %collective-permute-start.1 = (bf16[48,768]{1,0:T(8,128)(2,1)S(1)}, bf16[48,768]{1,0:T(8,128)(2,1)S(1)}, u32[]{:S(2)}, u32[]{:S(2)}) collective-permute-start(bf16[48,768]{1,0:T(8,128)(2,1)S(1)} %get-tuple-element.17.own_ref.refs_0_), channel_id=1, source_target_pairs={{0,12},{1,13},{2,14},{3,15},{4,8},{5,9},{6,10},{7,11},{8,4},{9,5},... | collective-permute-start | bytes 221192 | tf_op jit(solution)/shard_map/ppermute | solution.py:168
  7.3 5.3 %collective-permute-start.2 = (bf16[48,768]{1,0:T(8,128)(2,1)S(1)}, bf16[48,768]{1,0:T(8,128)(2,1)S(1)}, u32[]{:S(2)}, u32[]{:S(2)}) collective-permute-start(bf16[48,768]{1,0:T(8,128)(2,1)S(1)} %get-tuple-element.17.own_ref.refs_0_), channel_id=1, source_target_pairs={{0,4},{1,5},{2,6},{3,7},{4,0},{5,1},{6,2},{7,3},{8,12},{9,13},{10,... | collective-permute-start | bytes 221192 | tf_op jit(solution)/shard_map/ppermute | solution.py:168
  7.5 5.1 %collective-permute-start.3 = (bf16[48,768]{1,0:T(8,128)(2,1)S(1)}, bf16[48,768]{1,0:T(8,128)(2,1)S(1)}, u32[]{:S(2)}, u32[]{:S(2)}) collective-permute-start(bf16[48,768]{1,0:T(8,128)(2,1)S(1)} %get-tuple-element.17.own_ref.refs_0_), channel_id=1, source_target_pairs={{0,2},{1,3},{2,0},{3,1},{4,6},{5,7},{6,4},{7,5},{8,10},{9,11},{10,... | collective-permute-start | bytes 221192 | tf_op jit(solution)/shard_map/ppermute | solution.py:168
  9.0 3.6 %collective-permute-start.4 = (bf16[48,768]{1,0:T(8,128)(2,1)S(1)}, bf16[48,768]{1,0:T(8,128)(2,1)S(1)}, u32[]{:S(2)}, u32[]{:S(2)}) collective-permute-start(bf16[48,768]{1,0:T(8,128)(2,1)S(1)} %get-tuple-element.17.own_ref.refs_0_), channel_id=1, source_target_pairs={{0,1},{1,0},{2,3},{3,2},{4,5},{5,4},{6,7},{7,6},{8,9},{9,8},{10,11... | collective-permute-start | bytes 221192 | tf_op jit(solution)/shard_map/ppermute | solution.py:168
  12.6 1.5 %collective-permute-start.5 = (bf16[144,768]{1,0:T(8,128)(2,1)S(1)}, bf16[144,768]{1,0:T(8,128)(2,1)S(1)}, u32[]{:S(2)}, u32[]{:S(2)}) collective-permute-start(bf16[144,768]{1,0:T(8,128)(2,1)S(1)} %pad_maximum_fusion), channel_id=1, source_target_pairs={{0,1},{1,0},{2,3},{3,2},{4,5},{5,4},{6,7},{7,6},{8,9},{9,8},{10,11... | collective-permute-start | bytes 663560 | tf_op jit(solution)/shard_map/ppermute | solution.py:168
  14.5 4.5 %collective-permute-start.6 = (bf16[304,128]{1,0:T(8,128)(2,1)S(1)}, bf16[304,128]{1,0:T(8,128)(2,1)S(1)}, u32[]{:S(2)}, u32[]{:S(2)}) collective-permute-start(bf16[304,128]{1,0:T(8,128)(2,1)S(1)} %beside.1), channel_id=1, source_target_pairs={{0,2},{1,3},{2,0},{3,1},{4,6},{5,7},{6,4},{7,5},{8,10},{9,11},{10,... | collective-permute-start | bytes 233480 | tf_op jit(solution)/shard_map/ppermute | solution.py:168
